TPU v7x, 128 devices: a whole 4x4x4 slice. The times are simulated.
128 devices in a mesh: member: 2 (over x_hi), space: 64 (over y, z, x_lo, core).
Axes of the slice: x: 4 (x_hi: 2, x_lo: 2; x = x_hi * 2 + x_lo), y: 4, z: 4, core: 2. Of those that a mesh axis runs over, the one named last changes fastest.
Arguments:
- mesh_latent: bfloat16 [8192, 512], P('space'), may hold values from -6 to 6
- grid_embed: bfloat16 [65536, 512], P('space'), may hold values from -6 to 6
- weather_state: float32 [84, 65536], P(None, 'space'), may hold values from -6 to 6
- target: float32 [84, 65536], P(None, 'space'), may hold values from -6 to 6
- cell_area: float32 [65536], P('space'), may hold values from 0.2 to 2
- member_noise: float32 [2, 32], P('member'), may hold values from -5 to 5
- mesh_nbrs: int32 [16, 8192], P(None, 'space'), may hold values from 0 to 8191, as said below
- mesh_bias: float32 [16, 8192], P(None, 'space'), may hold values from -2 to 300
- grid_nbrs: int32 [3, 65536], P(None, 'space'), may hold values from 0 to 8191, as said below
- grid_bias: float32 [3, 65536], P(None, 'space'), may hold values from -2 to 300
- grid_counts: int32 [64], P('space'), may hold values from 512 to 1024, as said below
- cond_scale: float32 [32, 512], replicated, may hold values from -0.5 to 0.5
- cond_shift: float32 [32, 512], replicated, may hold values from -0.5 to 0.5
- attn_qkv: bfloat16 [512, 1536], replicated, may hold values from -0.25 to 0.25
- attn_out: bfloat16 [512, 512], replicated, may hold values from -0.25 to 0.25
- dec_query: bfloat16 [512, 512], replicated, may hold values from -0.25 to 0.25
- dec_kv: bfloat16 [512, 1024], replicated, may hold values from -0.25 to 0.25
- dec_out: bfloat16 [512, 512], replicated, may hold values from -0.25 to 0.25
- head_out: bfloat16 [84, 512], replicated, may hold values from -0.25 to 0.25
Outputs:
- prediction: float32 [2, 84, 65536], P('member', None, 'space')
- grad_cond_scale: float32 [32, 512], replicated
- grad_cond_shift: float32 [32, 512], replicated
- grad_attn_qkv: float32 [512, 1536], replicated
- grad_attn_out: float32 [512, 512], replicated
- grad_dec_query: float32 [512, 512], replicated
- grad_dec_kv: float32 [512, 1024], replicated
- grad_dec_out: float32 [512, 512], replicated
- grad_head_out: float32 [84, 512], replicated
- loss: float32 [], replicated
Inputs may be any that keep to these rules, and one draw needn't show every extreme that they name: `mesh_nbrs`: row 0 of column i is i itself. For the mesh nodes of the k-th aligned block of 128, every entry lies in the cyclic window of mesh nodes from k * 128 - 64 to (k + 1) * 128 + 63, modulo 8192. `grid_nbrs`: for the grid slots of the k-th aligned block of 1024, every entry lies in the cyclic window of mesh nodes from k * 128 - 64 to (k + 1) * 128 + 63, modulo 8192. `grid_counts`: entry k counts the live slots of the k-th aligned block of 1024 grid slots, which are its first ones; some entry equals 1024.
All inputs are finite; a program needn't handle non-finite values.
Results may differ from a plain program's by a relative error of at most 0.033.
Values may be sent and summed in bfloat16 or wider, within the bound.
No kernel may reach another device: no remote copies, remote signals or barrier semaphores. Data moves between devices by JAX's collectives and lax.ppermute only.
A program may use at most 128 MiB of HBM per device.

v0:
```python
import math

import jax
import jax.numpy as jnp
from jax import lax
from jax.sharding import PartitionSpec as P

HEAD = 128


EPSILON = 1e-05
LOSS_SCALE = 65536.0
SMOOTHING = 0.0625


def extended(value, sides, width):
    for axis, dim in sides:
        size, length = (lax.axis_size(axis), value.shape[dim])
        up = [(i, (i + 1) % size) for i in range(size)]
        down = [(j, i) for i, j in up]
        last = lax.slice_in_dim(value, length - width, length, axis=dim)
        first = lax.slice_in_dim(value, 0, width, axis=dim)
        before = lax.ppermute(last, axis, up)
        after = lax.ppermute(first, axis, down)
        value = jnp.concatenate([before, value, after], axis=dim)
    return value


def partner(value, axis, distance):
    mask = 2**distance
    pairs = [(source, source ^ mask) for source in range(lax.axis_size(axis))]
    return lax.ppermute(value, axis, pairs)


def smooth_size(values):
    return jnp.sqrt(values * values + SMOOTHING)


def smooth_slope(values):
    return values / jnp.sqrt(values * values + SMOOTHING)


def normalize(values):
    values = values.astype(jnp.float32)
    center = values - jnp.mean(values, axis=-1, keepdims=True)
    spread = jnp.mean(center * center, axis=-1, keepdims=True)
    return center * lax.rsqrt(spread + EPSILON)


def normalize_back(values, grad_out):
    return jax.vjp(normalize, values.astype(jnp.float32))[1](grad_out)[0]


def left_product(first, second):
    return lax.dot_general(
        first, second, (((0,), (0,)), ((), ())), preferred_element_type=jnp.float32
    )


def right_product(first, second):
    return lax.dot_general(
        first, second, (((1,), (1,)), ((), ())), preferred_element_type=jnp.float32
    )


def project_rows(left_rows, weight):
    return jnp.dot(left_rows, weight, preferred_element_type=jnp.float32).astype(jnp.bfloat16)


def split_heads(queries, gathered):
    row_count, feature_dim = queries.shape
    nbr_count = gathered.shape[0]
    head_count = feature_dim // HEAD
    query_heads = queries.reshape(row_count, head_count, HEAD)
    key_heads = gathered[:, :, :feature_dim].reshape(nbr_count, row_count, head_count, HEAD)
    value_heads = gathered[:, :, feature_dim:].reshape(nbr_count, row_count, head_count, HEAD)
    return (query_heads, key_heads, value_heads)


def attend(queries, gathered, bias_rows):
    row_count, feature_dim = queries.shape
    query_heads, key_heads, value_heads = split_heads(queries, gathered)
    scores = (
        jnp.einsum("rhe,jrhe->jrh", query_heads, key_heads, preferred_element_type=jnp.float32)
        / math.sqrt(HEAD)
        + bias_rows[:, :, None]
    )
    row_max = jnp.max(scores, axis=0, keepdims=True)
    exp_terms = jnp.exp(scores - row_max)
    attn_probs = exp_terms / jnp.sum(exp_terms, axis=0, keepdims=True)
    attn_weights = attn_probs.astype(jnp.bfloat16)
    mixed_rows = jnp.einsum(
        "jrh,jrhe->rhe", attn_weights, value_heads, preferred_element_type=jnp.float32
    )
    return (
        mixed_rows.astype(jnp.bfloat16).reshape(row_count, feature_dim),
        attn_probs,
        attn_weights,
    )


def attend_back(queries, gathered, attn_probs, attn_weights, grad_mixed):
    row_count, feature_dim = queries.shape
    nbr_count = gathered.shape[0]
    head_count = feature_dim // HEAD
    query_heads, key_heads, value_heads = split_heads(queries, gathered)
    grad_heads = grad_mixed.reshape(row_count, head_count, HEAD)
    grad_weights = jnp.einsum(
        "rhe,jrhe->jrh", grad_heads, value_heads, preferred_element_type=jnp.float32
    )
    grad_values = jnp.einsum(
        "jrh,rhe->jrhe", attn_weights, grad_heads, preferred_element_type=jnp.float32
    )
    grad_scores = (
        attn_probs
        * (grad_weights - jnp.sum(attn_probs * grad_weights, axis=0, keepdims=True))
        / math.sqrt(HEAD)
    )
    grad_scores = grad_scores.astype(jnp.bfloat16)
    grad_queries = jnp.einsum(
        "jrh,jrhe->rhe", grad_scores, key_heads, preferred_element_type=jnp.float32
    ).reshape(row_count, feature_dim)
    grad_keys = jnp.einsum(
        "jrh,rhe->jrhe", grad_scores, query_heads, preferred_element_type=jnp.float32
    )
    grad_gathered = jnp.concatenate(
        [
            grad_keys.reshape(nbr_count, row_count, feature_dim),
            grad_values.reshape(nbr_count, row_count, feature_dim),
        ],
        axis=2,
    )
    return (grad_queries, grad_gathered)


def send_rims(own_rows, halo_rows):
    return extended(own_rows, (("space", 0),), halo_rows)


def return_rims(grad_window, halo_rows, mesh_rows):
    edges = jnp.concatenate([grad_window[:halo_rows], grad_window[halo_rows + mesh_rows :]], axis=0)
    arrived = extended(edges.astype(jnp.bfloat16), (("space", 0),), halo_rows).astype(edges.dtype)
    own_grad = grad_window[halo_rows : halo_rows + mesh_rows]
    own_grad = own_grad.at[:halo_rows].add(arrived[:halo_rows])
    own_grad = own_grad.at[mesh_rows - halo_rows :].add(arrived[arrived.shape[0] - halo_rows :])
    return own_grad


def per_device(
    mesh_latent,
    grid_embed,
    weather_state,
    target,
    cell_area,
    member_noise,
    mesh_nbrs,
    mesh_bias,
    grid_nbrs,
    grid_bias,
    grid_counts,
    cond_scale,
    cond_shift,
    attn_qkv,
    attn_out,
    dec_query,
    dec_kv,
    dec_out,
    head_out,
):
    highest = lax.Precision.HIGHEST
    mesh_rows, feature_dim = mesh_latent.shape
    halo_rows = mesh_rows // 2
    space_size = lax.axis_size("space")
    grid_slots = grid_embed.shape[0]
    channel_count = weather_state.shape[0]
    total_mesh = mesh_rows * space_size
    window_start = lax.axis_index("space") * mesh_rows - halo_rows
    mesh_local = (mesh_nbrs - window_start) % total_mesh
    grid_local = (grid_nbrs - window_start) % total_mesh
    noise_row = member_noise[0]
    live_slots = (jnp.arange(grid_slots, dtype=jnp.int32) < grid_counts[0]).astype(jnp.float32)
    weighting = cell_area * live_slots
    scale_den = 2.0 * channel_count * grid_slots * space_size
    latent_norm = normalize(mesh_latent)
    gain_row = 1.0 + jnp.dot(noise_row, cond_scale, precision=highest)
    shift_row = jnp.dot(noise_row, cond_shift, precision=highest)
    activation = (latent_norm * gain_row + shift_row).astype(jnp.bfloat16)
    qkv_rows = project_rows(activation, attn_qkv)
    query_rows = qkv_rows[:, :feature_dim]
    kv_own = qkv_rows[:, feature_dim:]
    kv_window = send_rims(kv_own, halo_rows)
    mesh_gathered = kv_window[mesh_local]
    mesh_mixed, mesh_probs, mesh_weights = attend(query_rows, mesh_gathered, mesh_bias)
    mesh_out = (
        mesh_latent.astype(jnp.float32)
        + jnp.dot(mesh_mixed, attn_out, preferred_element_type=jnp.float32)
    ).astype(jnp.bfloat16)
    mesh_norm = normalize(mesh_out).astype(jnp.bfloat16)
    dec_own = project_rows(mesh_norm, dec_kv)
    dec_window = send_rims(dec_own, halo_rows)
    grid_norm = normalize(grid_embed).astype(jnp.bfloat16)
    grid_query = project_rows(grid_norm, dec_query)
    grid_gathered = dec_window[grid_local]
    grid_mixed, grid_probs, grid_weights = attend(grid_query, grid_gathered, grid_bias)
    grid_out = (
        grid_embed.astype(jnp.float32)
        + jnp.dot(grid_mixed, dec_out, preferred_element_type=jnp.float32)
    ).astype(jnp.bfloat16)
    grid_final = normalize(grid_out).astype(jnp.bfloat16)
    change = right_product(head_out, grid_final)
    prediction = weather_state + live_slots * change
    partner_pred = partner(prediction, "member", 0)
    loss_part = (
        jnp.sum(
            weighting
            * (smooth_size(prediction - target) - 0.5 * smooth_size(prediction - partner_pred))
        )
        / scale_den
    )
    grad_change = (
        LOSS_SCALE
        * weighting
        * (smooth_slope(prediction - target) - smooth_slope(prediction - partner_pred))
        / scale_den
    ).astype(jnp.bfloat16)
    grad_head_out = jnp.dot(grad_change, grid_final, preferred_element_type=jnp.float32)
    grad_final = left_product(grad_change, head_out)
    grad_grid_out = normalize_back(grid_out, grad_final).astype(jnp.bfloat16)
    grad_dec_out = left_product(grid_mixed, grad_grid_out)
    grad_grid_mixed = right_product(grad_grid_out, dec_out).astype(jnp.bfloat16)
    grad_grid_query, grad_grid_gathered = attend_back(
        grid_query, grid_gathered, grid_probs, grid_weights, grad_grid_mixed
    )
    grad_dec_query = left_product(grid_norm, grad_grid_query.astype(jnp.bfloat16))
    grad_dec_window = (
        jnp.zeros(dec_window.shape, jnp.float32)
        .at[grid_local.reshape(-1)]
        .add(grad_grid_gathered.reshape(-1, 2 * feature_dim))
    )
    grad_dec_own = return_rims(grad_dec_window, halo_rows, mesh_rows).astype(jnp.bfloat16)
    grad_dec_kv = left_product(mesh_norm, grad_dec_own)
    grad_mesh_norm = right_product(grad_dec_own, dec_kv)
    grad_mesh_out = normalize_back(mesh_out, grad_mesh_norm).astype(jnp.bfloat16)
    grad_attn_out = left_product(mesh_mixed, grad_mesh_out)
    grad_mesh_mixed = right_product(grad_mesh_out, attn_out).astype(jnp.bfloat16)
    grad_query_rows, grad_mesh_gathered = attend_back(
        query_rows, mesh_gathered, mesh_probs, mesh_weights, grad_mesh_mixed
    )
    grad_kv_window = (
        jnp.zeros(kv_window.shape, jnp.float32)
        .at[mesh_local.reshape(-1)]
        .add(grad_mesh_gathered.reshape(-1, 2 * feature_dim))
    )
    grad_kv_own = return_rims(grad_kv_window, halo_rows, mesh_rows)
    grad_qkv = jnp.concatenate([grad_query_rows, grad_kv_own], axis=1).astype(jnp.bfloat16)
    grad_attn_qkv = left_product(activation, grad_qkv)
    grad_act = right_product(grad_qkv, attn_qkv)
    grad_gain = jnp.sum(grad_act * latent_norm, axis=0)
    grad_shift = jnp.sum(grad_act, axis=0)
    grad_cond_scale = noise_row[:, None] * grad_gain[None, :]
    grad_cond_shift = noise_row[:, None] * grad_shift[None, :]
    summed = lax.psum(
        (
            grad_cond_scale,
            grad_cond_shift,
            grad_attn_qkv,
            grad_attn_out,
            grad_dec_query,
            grad_dec_kv,
            grad_dec_out,
            grad_head_out,
            loss_part,
        ),
        ("member", "space"),
    )
    return (
        prediction[None],
        summed[0],
        summed[1],
        summed[2],
        summed[3],
        summed[4],
        summed[5],
        summed[6],
        summed[7],
        summed[8],
    )


def solution(mesh):
    in_specs = (
        P("space", None),
        P("space", None),
        P(None, "space"),
        P(None, "space"),
        P("space"),
        P("member", None),
        P(None, "space"),
        P(None, "space"),
        P(None, "space"),
        P(None, "space"),
        P("space"),
        P(),
        P(),
        P(),
        P(),
        P(),
        P(),
        P(),
        P(),
    )
    out_specs = (P("member", None, "space"), P(), P(), P(), P(), P(), P(), P(), P(), P())
    return jax.shard_map(
        per_device, mesh=mesh, in_specs=in_specs, out_specs=out_specs, check_vma=False
    )
```

profile of v0, /device:TPU:1, one launch (start us, length us, event | category | flops | bytes accessed | tf_op | source)
XLA Modules:
  0.0 471.0 jit_solution(14115375172542685047)
XLA Ops:
  7.2 1.1 convert_reduce_fusion.2
  11.6 1.3 convolution_convert_fusion
  12.9 2.7 collective-permute-start
  17.1 1.5 copy.39
  20.1 1.7 convolution_convert_fusion.2
  23.4 9.7 %gather_fusion = bf16[2048,1024]{1,0:T(8,128)(2,1)} fusion(bf16[256,1024]{1,0:T(8,128)(2,1)S(1)} %pad_maximum_fusion, s32[2048]{0:T(1024)S(1)} %get-tuple-element.96), kind=kCustom, calls=%fused_computation | custom fusion | bytes 8396800 | tf_op jit(solution)/shard_map/gather | solution.py:192
  33.1 4.7 fusion.123
  37.8 4.0 reshape.327
  41.8 4.1 reshape.325
  45.9 3.0 fusion.33
  49.9 3.1 fusion.29
  54.2 1.7 collective-permute-start.2
  56.0 4.6 collective-permute-start.3
  61.3 2.6 copy.76
  64.0 14.0 %gather_fusion.1 = bf16[3072,1024]{1,0:T(8,128)(2,1)} fusion(bf16[256,1024]{1,0:T(8,128)(2,1)S(1)} %pad_maximum_fusion.1, s32[3072]{0:T(1024)S(1)} %broadcast_clamp_fusion), kind=kCustom, calls=%fused_computation.1 | custom fusion | bytes 12595200 | tf_op jit(solution)/shard_map/gather | solution.py:203
  78.0 6.3 %fusion.122 = (bf16[3,1024,512]{2,1,0:T(8,128)(2,1)}, bf16[3,1024,512]{2,1,0:T(8,128)(2,1)}) fusion(bf16[3,1024,1024]{2,1,0:T(8,128)(2,1)} %bitcast.177), kind=kLoop, calls=%fused_computation.207 | loop fusion | bytes 12582912 | tf_op jit(solution)/shard_map/slice | solution.py:76
  84.4 5.5 %reshape.331 = bf16[3,1024,4,128]{3,2,1,0:T(4,128)(2,1)} reshape(bf16[3,1024,512]{2,1,0:T(8,128)(2,1)} %get-tuple-element.98) | data formatting | bytes 6291456 | tf_op jit(solution)/shard_map/reshape | solution.py:76
  89.9 5.5 %reshape.329 = bf16[3,1024,4,128]{3,2,1,0:T(4,128)(2,1)} reshape(bf16[3,1024,512]{2,1,0:T(8,128)(2,1)} %get-tuple-element.99) | data formatting | bytes 6291456 | tf_op jit(solution)/shard_map/reshape | solution.py:75
  95.4 5.9 %multiply_reduce_fusion.1 = f32[1024,4,3]{1,0,2:T(8,128)S(1)} fusion(f32[1024,4,128]{2,1,0:T(4,128)} %copy.76, bf16[3,1024,4,128]{3,2,1,0:T(4,128)(2,1)} %reshape.329), kind=kLoop, calls=%fused_computation.18 | loop fusion | flops 4706304 | bytes 5292032
  101.3 1.3 broadcast_multiply_fusion.4
  102.6 1.9 copy.89
  104.6 4.0 copy.60
  108.6 8.3 %fusion.13 = f32[1024,4,1,128]{3,2,1,0:T(1,128)} fusion(bf16[3,1024,4,1]{0,3,2,1:T(2,128)(2,1)} %copy.60, bf16[3,1024,4,128]{3,2,1,0:T(4,128)(2,1)} %reshape.331), kind=kOutput, calls=%fused_computation.23 | convolution fusion | flops 3145728 | bytes 5267456 | tf_op jit(solution)/shard_map/jrh,jrhe->rhe/dot_general | solution.py:92
  116.9 2.1 convert_element_type.115
  120.9 2.5 collective-permute-start.4
  124.0 1.3 copy.45
  125.3 1.8 copy.43
  127.1 1.7 collective-permute-done.4
  128.8 2.1 multiply_reduce_fusion.2
  130.9 1.4 fusion.25
  134.2 1.8 fusion.49
  135.9 1.7 convolution_convert_fusion.1
  137.6 2.8 copy.77
  140.4 11.9 %multiply_reduce_fusion = (f32[1024,4,3]{1,0,2:T(8,128)}, f32[1024,4,128,3]{2,1,0,3:T(4,128)}) fusion(f32[1024,4,128]{2,1,0:T(4,128)} %copy.77, bf16[3,1024,4,128]{3,2,1,0:T(4,128)(2,1)} %reshape.331, f32[1024,4,3]{1,0,2:T(8,128)} %copy.43), kind=kLoop, calls=%fused_computation.17 | loop fusion | flops 6279168 | bytes 11632640
  152.3 1.9 copy.68
  154.2 1.7 copy.41
  155.9 6.4 %broadcast_multiply_fusion.1 = f32[1024,4,128,3]{2,1,0,3:T(4,128)} fusion(f32[1024,4,128]{2,1,0:T(4,128)} %copy.76, f32[1024,4,3]{1,0,2:T(8,128)} %copy.41), kind=kLoop, calls=%fused_computation.26 | loop fusion | flops 1572864 | bytes 8437760 | tf_op jit(solution)/shard_map/jrh,rhe->jrhe/dot_general | solution.py:123
  162.2 10.7 %copy_bitcast_fusion = (f32[3072,512]{1,0:T(8,128)}, f32[3072,512]{1,0:T(8,128)}) fusion(f32[384,8,4,128]{3,2,1,0:T(4,128)} %bitcast.175, f32[384,8,4,128]{3,2,1,0:T(4,128)} %bitcast.176), kind=kLoop, calls=%fused_computation.15 | loop fusion | bytes 25165824 | tf_op jit(solution)/shard_map/concatenate | solution.py:126
  172.9 27.8 %scatter_custom_fusion = f32[256,1024]{1,0:T(8,128)} fusion(s32[3072]{0:T(1024)} %bitcast.204, f32[3072,512]{1,0:T(8,128)} %get-tuple-element.128, f32[]{:T(128)} %constant.176.clone.1, f32[3072,512]{1,0:T(8,128)} %get-tuple-element.129, f32[]{:T(128)} %constant.164.clone.1), kind=kCustom, calls=%fused_computation.7 | custom fusion | flops 6291456 | bytes 13632512 | tf_op jit(solution)/shard_map/scatter-add | solution.py:238
  200.7 2.1 convert.55
  202.8 4.2 copy.73
  207.0 8.3 %fusion.11 = f32[1024,4,1,128]{3,2,1,0:T(1,128)} fusion(bf16[3,1024,4,1]{0,3,2,1:T(2,128)(2,1)} %copy.73, bf16[3,1024,4,128]{3,2,1,0:T(4,128)(2,1)} %reshape.329), kind=kOutput, calls=%fused_computation.21 | convolution fusion | flops 3145728 | bytes 5267456 | tf_op jit(solution)/shard_map/jrh,jrhe->rhe/dot_general | solution.py:120
  215.3 2.0 convert_element_type.129
  217.4 1.8 fusion.46
  219.3 1.5 collective-permute-start.5
  220.7 5.8 %collective-permute-start.6 = (bf16[64,1024]{1,0:T(8,128)(2,1)S(1)}, bf16[64,1024]{1,0:T(8,128)(2,1)S(1)}, u32[]{:S(2)}, u32[]{:S(2)}) collective-permute-start(bf16[64,1024]{1,0:T(8,128)(2,1)S(1)} %get-tuple-element.109), channel_id=1, source_target_pairs={{1,0},{2,1},{3,2},{4,3},{5,4},{6,5},{7,6},{8,7},{9,8},{10,9},{11,1... | collective-permute-start | bytes 393224 | tf_op jit(solution)/shard_map/ppermute | solution.py:24
  226.5 1.1 fusion.55
  229.8 1.9 fusion.79
  231.6 1.5 fusion.27
  233.7 2.6 broadcast_multiply_fusion.3
  236.3 2.5 copy.132
  238.8 2.5 broadcast_multiply_fusion.2
  241.3 2.4 copy.131
  243.7 18.7 %scatter_custom_fusion.1 = f32[256,1024]{1,0:T(8,128)S(1)} fusion(s32[2048]{0:T(1024)} %bitcast.206, f32[2048,512]{1,0:T(8,128)} %bitcast.180, f32[]{:T(128)} %constant.176.clone.1, f32[2048,512]{1,0:T(8,128)} %bitcast.179, f32[]{:T(128)} %constant.164.clone.1), kind=kCustom, calls=%fused_computation.11 | custom fusion | flops 4194304 | bytes 9438208 | tf_op jit(solution)/shard_map/scatter-add | solution.py:252
  263.4 3.2 fusion.31
  266.8 7.6 %collective-permute-start.8 = (bf16[64,1024]{1,0:T(8,128)(2,1)S(1)}, bf16[64,1024]{1,0:T(8,128)(2,1)S(1)}, u32[]{:S(2)}, u32[]{:S(2)}) collective-permute-start(bf16[64,1024]{1,0:T(8,128)(2,1)S(1)} %get-tuple-element.107), channel_id=1, source_target_pairs={{1,0},{2,1},{3,2},{4,3},{5,4},{6,5},{7,6},{8,7},{9,8},{10,9},{11,1... | collective-permute-start | bytes 393224 | tf_op jit(solution)/shard_map/ppermute | solution.py:24
  274.4 1.3 fusion.76
  276.7 2.4 fusion.74
  281.8 74.2 %psum.71 = f32[]{:T(128)} all-reduce(f32[]{:T(128)S(6)} %div.127), channel_id=1, replica_groups=mesh['member'=2,'space'=64] {'member','space'}, use_global_device_ids=true, to_apply=%region_31.32 | all-reduce | flops 1 | bytes 8 | tf_op jit(solution)/shard_map/psum | solution.py:262
  356.0 95.3 %all-reduce.3.cloned.1.call-done = (f32[32,512]{1,0:T(8,128)}, f32[32,512]{1,0:T(8,128)}, f32[512,1536]{1,0:T(8,128)}, f32[512,512]{1,0:T(8,128)}, f32[512,512]{...) async-done(((f32[32,512]{1,0:T(8,128)}, f32[32,512]{1,0:T(8,128)}, f32[512,1536]{1,0:T(8,128)}, f32[512,512]{1,0:T(8,128)}, ...) | async-done | bytes 8691728 | tf_op jit(solution)/shard_map/psum | solution.py:262
  451.3 1.5 copy.147
  452.8 1.5 copy.148
  454.3 3.9 copy.149
  460.2 1.3 copy.152
  (234 shorter events, 25.4 us)
Async XLA Ops:
  7.2 4.4 copy-start
  7.2 9.2 %copy-start.44 = (s32[3,1024]{1,0:T(4,128)S(1)}, s32[3,1024]{1,0:T(4,128)}, u32[]{:S(2)}) copy-start(s32[3,1024]{1,0:T(4,128)} %param.35) | copy-start | bytes 36868
  7.2 444.1 %all-reduce.3.cloned.1.call-start = ((), (), s32[]{:S(2)}) async-start(), calls=%async_computation | async-start | bytes 17399808 | tf_op jit(solution)/shard_map/psum | solution.py:262
  8.4 8.0 %copy-start.49 = (f32[128]{0:T(128)}, f32[128]{0:T(128)S(1)}, u32[]{:S(2)}) copy-start(f32[128]{0:T(128)S(1)} %broadcast_multiply_fusion.11) | copy-start | bytes 1540
  9.5 6.9 %copy-start.58 = (f32[128]{0:T(128)}, f32[128]{0:T(128)S(1)}, u32[]{:S(2)}) copy-start(f32[128]{0:T(128)S(1)} %add_rsqrt_fusion.1) | copy-start | bytes 1540
  10.5 5.1 %copy-start.42 = (f32[512]{0:T(512)}, f32[512]{0:T(512)S(1)}, u32[]{:S(2)}) copy-start(f32[512]{0:T(512)S(1)} %broadcast_add_fusion) | copy-start | bytes 6148
  11.5 4.1 copy-start.40
  12.9 5.9 %copy-start.11 = (bf16[128,1536]{1,0:T(8,128)(2,1)}, bf16[128,1536]{1,0:T(8,128)(2,1)S(1)}, u32[]{:S(2)}) copy-start(bf16[128,1536]{1,0:T(8,128)(2,1)S(1)} %convolution_convert_fusion) | copy-start | bytes 1179652
  12.9 9.5 %collective-permute-start = (bf16[64,1024]{1,0:T(8,128)(2,1)S(1)}, bf16[64,1024]{1,0:T(8,128)(2,1)}, u32[]{:S(2)}, u32[]{:S(2)}) collective-permute-start(bf16[64,1024]{1,0:T(8,128)(2,1)S(1)} %get-tuple-element.110), channel_id=1, source_target_pairs={{0,1},{1,2},{2,3},{3,4},{4,5},{5,6},{6,7},{7,8},{8,9},{9,10},{10,1... | collective-permute-start | bytes 393224 | tf_op jit(solution)/shard_map/ppermute | solution.py:23
  15.6 6.8 %collective-permute-start.1 = (bf16[64,1024]{1,0:T(8,128)(2,1)S(1)}, bf16[64,1024]{1,0:T(8,128)(2,1)}, u32[]{:S(2)}, u32[]{:S(2)}) collective-permute-start(bf16[64,1024]{1,0:T(8,128)(2,1)S(1)} %get-tuple-element.111), channel_id=1, source_target_pairs={{1,0},{2,1},{3,2},{4,3},{5,4},{6,5},{7,6},{8,7},{9,8},{10,9},{11,1... | collective-permute-start | bytes 393224 | tf_op jit(solution)/shard_map/ppermute | solution.py:24
  18.6 3.2 copy-start.1
  18.6 1.4 copy-start.62
  19.2 2.6 copy-start.47
  19.2 3.2 slice-start.2
  45.9 3.2 copy-start.66
  48.9 4.2 copy-start.10
  48.9 4.2 copy-start.16
  49.9 3.8 copy-start.7
  53.0 7.5 %copy-start.53 = (f32[1024]{0:T(1024)S(1)}, f32[1024]{0:T(1024)}, u32[]{:S(2)}) copy-start(f32[1024]{0:T(1024)} %param.31) | copy-start | bytes 12292
  53.0 7.5 %copy-start.22 = (bf16[128,512]{1,0:T(8,128)(2,1)S(1)}, bf16[128,512]{1,0:T(8,128)(2,1)}, u32[]{:S(2)}) copy-start(bf16[128,512]{1,0:T(8,128)(2,1)} %copy-done.21) | copy-start | bytes 393220
  53.1 10.8 %copy-start.23 = (bf16[128,4,128]{2,1,0:T(4,128)(2,1)}, bf16[128,4,128]{2,1,0:T(4,128)(2,1)S(1)}, u32[]{:S(2)}) copy-start(bf16[128,4,128]{2,1,0:T(4,128)(2,1)S(1)} %convert_element_type.107) | copy-start | bytes 393220
  53.6 10.3 %copy-start.60 = (f32[128]{0:T(128)}, f32[128]{0:T(128)S(1)}, u32[]{:S(2)}) copy-start(f32[128]{0:T(128)S(1)} %multiply_reduce_fusion.4) | copy-start | bytes 1540
  54.2 9.7 %collective-permute-start.2 = (bf16[64,1024]{1,0:T(8,128)(2,1)S(1)}, bf16[64,1024]{1,0:T(8,128)(2,1)S(1)}, u32[]{:S(2)}, u32[]{:S(2)}) collective-permute-start(bf16[64,1024]{1,0:T(8,128)(2,1)S(1)} %get-tuple-element.112), channel_id=1, source_target_pairs={{0,1},{1,2},{2,3},{3,4},{4,5},{5,6},{6,7},{7,8},{8,9},{9,10},{10,1... | collective-permute-start | bytes 393224 | tf_op jit(solution)/shard_map/ppermute | solution.py:23
  56.0 8.0 %collective-permute-start.3 = (bf16[64,1024]{1,0:T(8,128)(2,1)S(1)}, bf16[64,1024]{1,0:T(8,128)(2,1)S(1)}, u32[]{:S(2)}, u32[]{:S(2)}) collective-permute-start(bf16[64,1024]{1,0:T(8,128)(2,1)S(1)} %get-tuple-element.113), channel_id=1, source_target_pairs={{1,0},{2,1},{3,2},{4,3},{5,4},{6,5},{7,6},{8,7},{9,8},{10,9},{11,1... | collective-permute-start | bytes 393224 | tf_op jit(solution)/shard_map/ppermute | solution.py:24
  101.3 3.2 copy-start.34
  116.9 2.1 copy-start.2
  116.9 2.1 copy-start.63
  120.0 3.4 copy-start.39
  120.0 4.0 copy-start.35
  120.9 11.5 %copy-start.18 = (f32[84,1024]{1,0:T(8,128)}, f32[84,1024]{1,0:T(8,128)S(1)}, u32[]{:S(2)}) copy-start(f32[84,1024]{1,0:T(8,128)S(1)} %fusion.36) | copy-start | bytes 1032196
  120.9 8.0 %collective-permute-start.4 = (f32[84,1024]{1,0:T(8,128)S(1)}, f32[84,1024]{1,0:T(8,128)}, u32[]{:S(2)}, u32[]{:S(2)}) collective-permute-start(f32[84,1024]{1,0:T(8,128)S(1)} %fusion.36), channel_id=1, source_target_pairs={{0,64},{64,0},{1,65},{65,1},{2,66},{66,2},{3,67},{67,3},{4,68},{68... | collective-permute-start | bytes 1032200 | tf_op jit(solution)/shard_map/ppermute | solution.py:32
  130.9 1.5 copy-start.31
  134.2 1.8 copy-start.64
  215.3 2.0 copy-start.3
  215.3 2.1 copy-start.55
  217.4 1.8 copy-start.20
  217.4 9.1 %copy-start.32 = (bf16[84,1024]{1,0:T(8,128)(2,1)S(1)}, bf16[84,1024]{1,0:T(8,128)(2,1)}, u32[]{:S(2)}) copy-start(bf16[84,1024]{1,0:T(8,128)(2,1)} %copy-done.31) | copy-start | bytes 516100
  219.2 8.4 %copy-start.6 = (f32[256,1024]{1,0:T(8,128)S(1)}, f32[256,1024]{1,0:T(8,128)}, u32[]{:S(2)}) copy-start(f32[256,1024]{1,0:T(8,128)} %scatter_custom_fusion) | copy-start | bytes 3145732
  219.2 8.4 %slice-start.1 = ((f32[256,1024]{1,0:T(8,128)}), f32[128,1024]{1,0:T(8,128)S(1)}, s32[]{:S(2)}) async-start(f32[256,1024]{1,0:T(8,128)} %scatter_custom_fusion), calls=%async_computation.2 | async-start | bytes 1048576 | tf_op jit(solution)/shard_map/slice | solution.py:143
  219.2 8.5 %copy-start.8 = (bf16[512,1024]{1,0:T(8,128)(2,1)S(1)}, bf16[512,1024]{1,0:T(8,128)(2,1)}, u32[]{:S(2)}) copy-start(bf16[512,1024]{1,0:T(8,128)(2,1)} %param.43) | copy-start | bytes 3145732
  219.3 8.5 %copy-start.46 = (f32[128]{0:T(128)S(1)}, f32[128]{0:T(128)}, u32[]{:S(2)}) copy-start(f32[128]{0:T(128)} %copy-done.45) | copy-start | bytes 1540
  219.3 8.4 %collective-permute-start.5 = (bf16[64,1024]{1,0:T(8,128)(2,1)S(1)}, bf16[64,1024]{1,0:T(8,128)(2,1)S(1)}, u32[]{:S(2)}, u32[]{:S(2)}) collective-permute-start(bf16[64,1024]{1,0:T(8,128)(2,1)S(1)} %get-tuple-element.108), channel_id=1, source_target_pairs={{0,1},{1,2},{2,3},{3,4},{4,5},{5,6},{6,7},{7,8},{8,9},{9,10},{10,1... | collective-permute-start | bytes 393224 | tf_op jit(solution)/shard_map/ppermute | solution.py:23
  220.7 6.9 %collective-permute-start.6 = (bf16[64,1024]{1,0:T(8,128)(2,1)S(1)}, bf16[64,1024]{1,0:T(8,128)(2,1)S(1)}, u32[]{:S(2)}, u32[]{:S(2)}) collective-permute-start(bf16[64,1024]{1,0:T(8,128)(2,1)S(1)} %get-tuple-element.109), channel_id=1, source_target_pairs={{1,0},{2,1},{3,2},{4,3},{5,4},{6,5},{7,6},{8,7},{9,8},{10,9},{11,1... | collective-permute-start | bytes 393224 | tf_op jit(solution)/shard_map/ppermute | solution.py:24
  227.7 1.6 copy-start.17
  228.6 3.0 copy-start.56
  229.7 1.9 copy-start.14
  231.6 1.6 copy-start.37
  231.6 2.0 copy-start.30
  236.3 2.5 copy-start.9
  262.3 4.2 copy-start.4
  263.4 11.1 %copy-start.13 = (f32[128,512]{1,0:T(8,128)S(1)}, f32[128,512]{1,0:T(8,128)}, u32[]{:S(2)}) copy-start(f32[128,512]{1,0:T(8,128)} %copy-done.12) | copy-start | bytes 786436
  263.4 11.1 %copy-start.24 = (bf16[128,4,128]{2,1,0:T(4,128)(2,1)S(1)}, bf16[128,4,128]{2,1,0:T(4,128)(2,1)}, u32[]{:S(2)}) copy-start(bf16[128,4,128]{2,1,0:T(4,128)(2,1)} %copy-done.23) | copy-start | bytes 393220
  263.4 11.1 %copy-start.57 = (f32[128]{0:T(128)S(1)}, f32[128]{0:T(128)}, u32[]{:S(2)}) copy-start(f32[128]{0:T(128)} %copy-done.56) | copy-start | bytes 1540
  266.6 9.2 %copy-start.5 = (f32[256,1024]{1,0:T(8,128)S(1)}, f32[256,1024]{1,0:T(8,128)}, u32[]{:S(2)}) copy-start(f32[256,1024]{1,0:T(8,128)} %copy-done.4) | copy-start | bytes 3145732
  266.6 9.2 %slice-start = ((f32[256,1024]{1,0:T(8,128)}), f32[128,1024]{1,0:T(8,128)S(1)}, s32[]{:S(2)}) async-start(f32[256,1024]{1,0:T(8,128)} %copy-done.4), calls=%async_computation.1 | async-start | bytes 1048576 | tf_op jit(solution)/shard_map/slice | solution.py:143
  266.7 9.1 %collective-permute-start.7 = (bf16[64,1024]{1,0:T(8,128)(2,1)S(1)}, bf16[64,1024]{1,0:T(8,128)(2,1)S(1)}, u32[]{:S(2)}, u32[]{:S(2)}) collective-permute-start(bf16[64,1024]{1,0:T(8,128)(2,1)S(1)} %get-tuple-element.106), channel_id=1, source_target_pairs={{0,1},{1,2},{2,3},{3,4},{4,5},{5,6},{6,7},{7,8},{8,9},{9,10},{10,1... | collective-permute-start | bytes 393224 | tf_op jit(solution)/shard_map/ppermute | solution.py:23
  266.8 9.2 %copy-start.50 = (f32[128]{0:T(128)S(1)}, f32[128]{0:T(128)}, u32[]{:S(2)}) copy-start(f32[128]{0:T(128)} %copy-done.49) | copy-start | bytes 1540
  266.8 9.2 %copy-start.59 = (f32[128]{0:T(128)S(1)}, f32[128]{0:T(128)}, u32[]{:S(2)}) copy-start(f32[128]{0:T(128)} %copy-done.58) | copy-start | bytes 1540
  266.8 9.0 %collective-permute-start.8 = (bf16[64,1024]{1,0:T(8,128)(2,1)S(1)}, bf16[64,1024]{1,0:T(8,128)(2,1)S(1)}, u32[]{:S(2)}, u32[]{:S(2)}) collective-permute-start(bf16[64,1024]{1,0:T(8,128)(2,1)S(1)} %get-tuple-element.107), channel_id=1, source_target_pairs={{1,0},{2,1},{3,2},{4,3},{5,4},{6,5},{7,6},{8,7},{9,8},{10,9},{11,1... | collective-permute-start | bytes 393224 | tf_op jit(solution)/shard_map/ppermute | solution.py:24
  276.6 2.4 copy-start.48
  454.3 3.9 copy-start.29
  454.3 4.9 %copy-start.28 = (f32[512,512]{1,0:T(8,128)S(1)}, f32[512,512]{1,0:T(8,128)}, u32[]{:S(2)}) copy-start(f32[512,512]{1,0:T(8,128)} %get-tuple-element.135) | copy-start | bytes 3145732
  458.2 2.0 copy-start.15
  460.2 2.0 copy-start.27
  (16 other events, 14.6 us)
Sparse Core Ops, SparseCore 0:
  279.9 171.4 all-reduce.2
where the time goes:
time: 479 us; the launch traced here: 471 us
  local copies, waits for them, and re-layouts  112 us (23%)
  waiting for transfers between devices  97.1 us (20%)
  other arithmetic  95.6 us (20%)
  blocking collectives  74.2 us (15%)
  matrix products  49.3 us (10%)
  starting transfers between devices  26.5 us (6%)
  between operations  16.7 us (3%)
    psum x1, waiting for transfers between devices, per_device(): lax.psum((grad_cond_scale, grad_cond_shift, grad_attn_qkv, grad_attn_out,...  95.3 us
    psum x1, blocking collectives, per_device(): lax.psum((grad_cond_scale, grad_cond_shift, grad_attn_qkv, grad_attn_out,...  74.2 us
    unnamed x151, local copies, waits for them, and re-layouts  30.4 us
    scatter-add x1, other arithmetic, per_device(): grad_dec_window = jnp.zeros(dec_window.shape, jnp.float32).at[grid_local....  27.8 us
    scatter-add x1, other arithmetic, per_device(): grad_kv_window = jnp.zeros(kv_window.shape, jnp.float32).at[mesh_local.re...  18.7 us
    ppermute x4, starting transfers between devices, extended(): after = lax.ppermute(first, axis, down)  18 us
    unnamed x3, other arithmetic  17.8 us
    gather x1, local copies, waits for them, and re-layouts, per_device(): grid_gathered = dec_window[grid_local]  14 us
  transfers between devices with their start and end apart: 10, of which 2 were waited for; matrix products, arithmetic and copies ran while one was open for 3% of the time, Pallas kernels for 0%

commit v1 on v0

v1 whole, which is shorter than its diff:
```python
import math

import jax
import jax.numpy as jnp
from jax import lax
from jax.experimental import pallas as pl
from jax.experimental.pallas import tpu as pltpu
from jax.sharding import PartitionSpec as P

HEAD = 128
EPSILON = 1e-05
LOSS_SCALE = 65536.0
SMOOTHING = 0.0625
FAR = -1e30

F32 = jnp.float32
BF16 = jnp.bfloat16


def nn(first, second):
    return lax.dot_general(first, second, (((1,), (0,)), ((), ())), preferred_element_type=F32)


def nt(first, second):
    return lax.dot_general(first, second, (((1,), (1,)), ((), ())), preferred_element_type=F32)


def tn(first, second):
    return lax.dot_general(first, second, (((0,), (0,)), ((), ())), preferred_element_type=F32)


def normalize(values, axis):
    center = values - jnp.mean(values, axis=axis, keepdims=True)
    spread = jnp.mean(center * center, axis=axis, keepdims=True)
    scale = lax.rsqrt(spread + EPSILON)
    return center * scale, scale


def normalize_back(values, grad_out, axis):
    unit, scale = normalize(values, axis)
    mean_grad = jnp.mean(grad_out, axis=axis, keepdims=True)
    mean_unit = jnp.mean(grad_out * unit, axis=axis, keepdims=True)
    return scale * (grad_out - mean_grad - unit * mean_unit)


def spread_bias(slots, bias, rows):
    entries, width = slots.shape
    row_ids = lax.broadcasted_iota(jnp.int32, (rows, width), 0)
    logits = jnp.full((rows, width), FAR, F32)
    for entry in range(entries):
        same = slots == slots[entry : entry + 1]
        top = jnp.max(jnp.where(same, bias, FAR), axis=0, keepdims=True)
        terms = jnp.sum(jnp.where(same, jnp.exp(bias - top), 0.0), axis=0, keepdims=True)
        logits = jnp.where(row_ids == slots[entry : entry + 1], top + jnp.log(terms), logits)
    return logits


def softmax_rows(scores):
    terms = jnp.exp(scores - jnp.max(scores, axis=0, keepdims=True))
    return terms * (1.0 / jnp.sum(terms, axis=0, keepdims=True))


def score_back(probs, grad_probs):
    probs = probs.astype(F32)
    inner = jnp.sum(probs * grad_probs, axis=0, keepdims=True)
    return (probs * (grad_probs - inner) * (1.0 / math.sqrt(HEAD))).astype(BF16)


def prepare_kernel(
    place, embed, nbrs, bias, dec_query, embed_t, norm_t, query_t, logits, *, rows, halo, total
):
    values = embed[...].T
    embed_t[...] = values
    norm = normalize(values.astype(F32), 0)[0].astype(BF16)
    norm_t[...] = norm
    query_t[...] = tn(dec_query[...], norm).astype(BF16)
    local = (nbrs[...] - place[1]) & (total - 1)
    slots = jnp.where(local < halo, local + rows, jnp.where(local < halo + rows, local - halo, local))
    logits[...] = spread_bias(slots, bias[...], rows + 2 * halo)


def window_order(values, rows, halo):
    first = 2 * halo + halo
    return jnp.concatenate(
        [
            values[first : first + rows],
            values[first - halo : first],
            values[first + rows : first + rows + halo],
        ],
        axis=0,
    )


def step_kernel(
    place,
    own,
    before,
    after,
    before2,
    after2,
    edges,
    edges_before,
    edges_after,
    noise,
    embed_t,
    norm_t,
    query_t,
    grid_logits,
    weather,
    target,
    area,
    cond_scale,
    cond_shift,
    attn_qkv,
    attn_out,
    dec_kv,
    dec_out,
    head_out,
    pred_own,
    pred_other,
    grads,
    latent,
    unit_t,
    unit_q_t,
    mesh_logits,
    mesh_query,
    mesh_kv,
    mesh_probs,
    mesh_mixed,
    mesh_out,
    mesh_norm,
    dec_keys,
    grid_probs,
    grid_mixed,
    grid_out,
    grid_final,
    change,
    grad_change,
    head_pad,
    grad_dec,
    grad_kv,
    *,
    total,
    scale_den,
):
    rows, dim = own.shape
    halo = rows // 2
    window = rows + 2 * halo
    heads = dim // HEAD
    members = 2
    channels = weather.shape[0]
    slots = embed_t.shape[1]
    inv_sqrt = 1.0 / math.sqrt(HEAD)

    latent[0:halo] = before2[...]
    latent[halo : halo + rows] = before[...]
    latent[halo + rows : halo + 2 * rows] = own[...]
    latent[halo + 2 * rows : halo + 3 * rows] = after[...]
    latent[halo + 3 * rows :] = after2[...]
    unit = normalize(latent[...].astype(F32), 1)[0]
    unit_t[...] = unit.astype(BF16).T
    unit_q_t[...] = window_order(unit, rows, halo).astype(BF16).T

    lane = lax.broadcasted_iota(jnp.int32, edges.shape, 1)
    ends = pltpu.roll(jnp.where(lane >= halo, edges_before[...], edges_after[...]), halo, 1)
    entries = edges.shape[0] // 2
    lane = lane[:entries]
    own_slots = (edges[:entries].astype(jnp.int32) - place[1]) & (total - 1)
    end_start = place[1] + jnp.where(lane < halo, -rows, rows)
    end_slots = (ends[:entries].astype(jnp.int32) - end_start) & (total - 1)
    mesh_logits[...] = spread_bias(
        jnp.concatenate([own_slots, end_slots], axis=1),
        jnp.concatenate([edges[entries:], ends[entries:]], axis=1),
        window,
    )
    is_before = lax.broadcasted_iota(jnp.int32, (window, rows), 1) < halo

    def split_ends(values):
        values = values.astype(F32)
        return jnp.concatenate(
            [jnp.where(is_before, values, 0.0), jnp.where(is_before, 0.0, values)], axis=0
        ).astype(BF16)

    def window_scores(keys, queries):
        mid = nn(keys[rows : rows + window], queries[:, :rows])
        ends = nn(keys, queries[:, rows:])
        return jnp.concatenate([mid, jnp.where(is_before, ends[:window], ends[window:])], axis=1)

    gains = []
    shifts = []
    for m in range(members):
        noise_col = noise[:, m : m + 1]
        gains.append(1.0 + jnp.sum(noise_col * cond_scale[...], axis=0, keepdims=True))
        shifts.append(jnp.sum(noise_col * cond_shift[...], axis=0, keepdims=True))

    for m in range(members):
        act = (unit * gains[m] + shifts[m]).astype(BF16)
        mesh_kv[m] = nn(act, attn_qkv[:, dim:]).astype(BF16)
        act_q = window_order(act, rows, halo)
        mesh_query[m] = nn(act_q, attn_qkv[:, :dim]).astype(BF16).T
        for h in range(heads):
            cols = slice(h * HEAD, (h + 1) * HEAD)
            value_cols = slice(dim + h * HEAD, dim + (h + 1) * HEAD)
            scores = window_scores(mesh_kv[m, :, cols], mesh_query[m, cols, :])
            probs = softmax_rows(scores * inv_sqrt + mesh_logits[...]).astype(BF16)
            mesh_probs[m, h] = probs
            values = mesh_kv[m, :, value_cols]
            mid = tn(values[rows : rows + window], probs[:, :rows])
            ends = tn(values, split_ends(probs[:, rows:]))
            mesh_mixed[m, cols, :] = jnp.concatenate([mid, ends], axis=1).astype(BF16)
        residual = window_order(latent[...].astype(F32), rows, halo)
        out = (residual + nn(mesh_mixed[m].T, attn_out[...])).astype(BF16)
        mesh_out[m] = out
        norm = normalize(out.astype(F32), 1)[0].astype(BF16)
        mesh_norm[m] = norm
        dec_keys[m] = nn(norm, dec_kv[...]).astype(BF16)

    head_pad[...] = jnp.zeros_like(head_pad)
    head_pad[:channels] = head_out[...]
    for m in range(members):
        for h in range(heads):
            cols = slice(h * HEAD, (h + 1) * HEAD)
            value_cols = slice(dim + h * HEAD, dim + (h + 1) * HEAD)
            scores = nn(dec_keys[m, :, cols], query_t[cols, :])
            probs = softmax_rows(scores * inv_sqrt + grid_logits[...]).astype(BF16)
            grid_probs[m, h] = probs
            grid_mixed[m, cols, :] = tn(dec_keys[m, :, value_cols], probs).astype(BF16)
        out = (embed_t[...].astype(F32) + tn(dec_out[...], grid_mixed[m])).astype(BF16)
        grid_out[m] = out
        final = normalize(out.astype(F32), 0)[0].astype(BF16)
        grid_final[m] = final
        change[m] = nn(head_pad[...], final)

    slot = lax.broadcasted_iota(jnp.int32, (1, slots), 1) + place[0] * slots
    live = jnp.where(slot < place[2], 1.0, 0.0)
    weighting = live * area[...]
    first = weather[...] + live * change[0, :channels]
    second = weather[...] + live * change[1, :channels]
    pred_own[...] = first
    pred_other[...] = second

    def smooth(values):
        square = values * values + SMOOTHING
        inverse = lax.rsqrt(square)
        return square * inverse, values * inverse

    size_first, slope_first = smooth(first - target[...])
    size_second, slope_second = smooth(second - target[...])
    size_pair, slope_pair = smooth(first - second)
    loss = jnp.sum(weighting * (size_first + size_second - size_pair)) / scale_den
    factor = weighting * (LOSS_SCALE / scale_den)
    grad_change[...] = jnp.zeros_like(grad_change)
    grad_change[0, :channels] = (factor * (slope_first - slope_pair)).astype(BF16)
    grad_change[1, :channels] = (factor * (slope_second + slope_pair)).astype(BF16)

    grad_head = None
    grad_dec_out = None
    grad_query = None
    for m in range(members):
        g_change = grad_change[m]
        term = nt(g_change, grid_final[m])
        grad_head = term if m == 0 else grad_head + term
        g_final = tn(head_pad[...], g_change)
        g_out = normalize_back(grid_out[m].astype(F32), g_final, 0).astype(BF16)
        term = nt(grid_mixed[m], g_out)
        grad_dec_out = term if m == 0 else grad_dec_out + term
        g_mixed = nn(dec_out[...], g_out).astype(BF16)
        terms = []
        for h in range(heads):
            cols = slice(h * HEAD, (h + 1) * HEAD)
            value_cols = slice(dim + h * HEAD, dim + (h + 1) * HEAD)
            g_head = g_mixed[cols, :]
            probs = grid_probs[m, h]
            g_scores = score_back(probs, nn(dec_keys[m, :, value_cols], g_head))
            terms.append(tn(dec_keys[m, :, cols], g_scores))
            grad_dec[m, :, cols] = nt(g_scores, query_t[cols, :]).astype(BF16)
            grad_dec[m, :, value_cols] = nt(probs, g_head).astype(BF16)
        term = jnp.concatenate(terms, axis=0)
        grad_query = term if m == 0 else grad_query + term
    grad_dec_query = nt(norm_t[...], grad_query.astype(BF16))

    grad_dec_kv = None
    grad_attn_out = None
    grad_qkv = None
    grad_scale = None
    grad_shift = None
    for m in range(members):
        g_dec = grad_dec[m]
        term = tn(mesh_norm[m], g_dec)
        grad_dec_kv = term if m == 0 else grad_dec_kv + term
        g_norm = nt(g_dec, dec_kv[...])
        g_out = normalize_back(mesh_out[m].astype(F32), g_norm, 1).astype(BF16)
        term = nn(mesh_mixed[m], g_out)
        grad_attn_out = term if m == 0 else grad_attn_out + term
        g_mixed = nt(attn_out[...], g_out).astype(BF16)
        g_queries = []
        for h in range(heads):
            cols = slice(h * HEAD, (h + 1) * HEAD)
            value_cols = slice(dim + h * HEAD, dim + (h + 1) * HEAD)
            g_head = g_mixed[cols, :]
            probs = mesh_probs[m, h]
            keys = mesh_kv[m, :, cols]
            g_scores = score_back(probs, window_scores(mesh_kv[m, :, value_cols], g_head))
            g_ends = split_ends(g_scores[:, rows:])
            mid = tn(keys[rows : rows + window], g_scores[:, :rows])
            ends = tn(keys, g_ends)
            g_queries.append(jnp.concatenate([mid, ends], axis=1))
            queries = mesh_query[m, cols, :]
            grad_kv[:, cols] = nt(g_ends, queries[:, rows:])
            grad_kv[rows : rows + window, cols] += nt(g_scores[:, :rows], queries[:, :rows])
            grad_kv[:, value_cols] = nt(split_ends(probs[:, rows:]), g_head[:, rows:])
            grad_kv[rows : rows + window, value_cols] += nt(probs[:, :rows], g_head[:, :rows])
        g_kv = grad_kv[...].astype(BF16)
        g_query = jnp.concatenate(g_queries, axis=0).astype(BF16).T
        moment = jnp.concatenate([nn(unit_q_t[...], g_query), nn(unit_t[...], g_kv)], axis=1)
        col_sum = jnp.concatenate(
            [
                jnp.sum(g_query.astype(F32), axis=0, keepdims=True),
                jnp.sum(g_kv.astype(F32), axis=0, keepdims=True),
            ],
            axis=1,
        )
        gain_col = jnp.broadcast_to(gains[m], (HEAD, dim)).T[:, :1]
        shift_col = jnp.broadcast_to(shifts[m], (HEAD, dim)).T[:, :1]
        term = gain_col * moment + shift_col * col_sum
        grad_qkv = term if m == 0 else grad_qkv + term
        weight = attn_qkv[...].astype(F32)
        g_gain = jnp.sum(weight * moment, axis=1, keepdims=True)
        g_shift = jnp.sum(weight * col_sum, axis=1, keepdims=True)
        noise_col = noise[:, m : m + 1]
        spread = noise.shape[0]
        term = noise_col * jnp.broadcast_to(g_gain, (dim, HEAD)).T[:spread]
        grad_scale = term if m == 0 else grad_scale + term
        term = noise_col * jnp.broadcast_to(g_shift, (dim, HEAD)).T[:spread]
        grad_shift = term if m == 0 else grad_shift + term

    row = 0
    for block in (
        grad_qkv[:, :dim],
        grad_qkv[:, dim : 2 * dim],
        grad_qkv[:, 2 * dim :],
        grad_attn_out,
        grad_dec_query,
        grad_dec_kv[:, :dim],
        grad_dec_kv[:, dim:],
        grad_dec_out,
        grad_scale,
        grad_shift,
        grad_head,
    ):
        grads[row : row + block.shape[0]] = block.astype(grads.dtype)
        row += block.shape[0]
    rest = grads.shape[0] - row
    tail_row = lax.broadcasted_iota(jnp.int32, (rest, dim), 0)
    grads[row:] = jnp.where(tail_row == 0, loss, 0.0).astype(grads.dtype)


def whole(shape):
    return pl.BlockSpec(shape, lambda *_: (0,) * len(shape))


def per_device(
    mesh_latent,
    grid_embed,
    weather_state,
    target,
    cell_area,
    member_noise,
    mesh_nbrs,
    mesh_bias,
    grid_nbrs,
    grid_bias,
    grid_counts,
    cond_scale,
    cond_shift,
    attn_qkv,
    attn_out,
    dec_query,
    dec_kv,
    dec_out,
    head_out,
):
    rows, dim = mesh_latent.shape
    halo = rows // 2
    window = rows + 2 * halo
    outer = 2 * window
    size = lax.axis_size("space")
    grid_slots = grid_embed.shape[0]
    slots = grid_slots // 2
    channels = weather_state.shape[0]
    total = rows * size
    heads = dim // HEAD
    noise_size = member_noise.shape[1]
    entries = grid_nbrs.shape[0]
    scale_den = 2.0 * channels * grid_slots * size

    member = lax.axis_index("member")
    start = lax.axis_index("space") * rows - halo
    place = jnp.stack([member, start, grid_counts[0]]).astype(jnp.int32)

    def shift(value, hops):
        pairs = [(i, (i + hops) % size) for i in range(size)]
        return lax.ppermute(value, "space", pairs)

    swap = [(0, 1), (1, 0)]
    edges = jnp.concatenate([mesh_nbrs.astype(F32), mesh_bias], axis=0)
    before = shift(mesh_latent, 1)
    after = shift(mesh_latent, -1)
    before2 = shift(mesh_latent[halo:], 2)
    after2 = shift(mesh_latent[:halo], -2)
    edges_before = shift(edges, 1)
    edges_after = shift(edges, -1)
    other_noise = lax.ppermute(member_noise, "member", swap)
    noise = jnp.concatenate([member_noise, other_noise], axis=0).T

    part = pl.BlockSpec((slots, dim), lambda i, place: (place[0], 0))
    lists = pl.BlockSpec((entries, slots), lambda i, place: (0, place[0]))
    square = (dim, slots)
    embed_t, norm_t, query_t, grid_logits = pl.pallas_call(
        lambda *refs: prepare_kernel(*refs, rows=rows, halo=halo, total=total),
        grid_spec=pltpu.PrefetchScalarGridSpec(
            num_scalar_prefetch=1,
            grid=(1,),
            in_specs=[part, lists, lists, whole((dim, dim))],
            out_specs=[whole(square), whole(square), whole(square), whole((window, slots))],
        ),
        out_shape=[
            jax.ShapeDtypeStruct(square, BF16),
            jax.ShapeDtypeStruct(square, BF16),
            jax.ShapeDtypeStruct(square, BF16),
            jax.ShapeDtypeStruct((window, slots), F32),
        ],
        compiler_params=pltpu.CompilerParams(vmem_limit_bytes=40 * 2**20),
        cost_estimate=pl.CostEstimate(
            flops=2 * dim * dim * slots, bytes_accessed=3 * 2**20, transcendentals=0
        ),
        name="prepare",
    )(place, grid_embed, grid_nbrs, grid_bias, dec_query)

    channel_pad = -(-channels // 32) * 32
    grad_rows = 8 * dim + 2 * noise_size + channel_pad + 16
    grad_rows = -(-grad_rows // 256) * 256
    fields = pl.BlockSpec((channels, slots), lambda i, place: (0, place[0]))
    operands = (
        mesh_latent,
        before,
        after,
        before2,
        after2,
        edges,
        edges_before,
        edges_after,
        noise,
        embed_t,
        norm_t,
        query_t,
        grid_logits,
        weather_state,
        target,
        cell_area[None, :],
        cond_scale,
        cond_shift,
        attn_qkv,
        attn_out,
        dec_kv,
        dec_out,
        head_out,
    )
    specs = [whole(value.shape) for value in operands]
    specs[13] = fields
    specs[14] = fields
    specs[15] = pl.BlockSpec((1, slots), lambda i, place: (0, place[0]))
    pred_own, pred_other, grads = pl.pallas_call(
        lambda *refs: step_kernel(*refs, total=total, scale_den=scale_den),
        grid_spec=pltpu.PrefetchScalarGridSpec(
            num_scalar_prefetch=1,
            grid=(1,),
            in_specs=specs,
            out_specs=[
                whole((channels, slots)),
                whole((channels, slots)),
                whole((grad_rows, dim)),
            ],
            scratch_shapes=[
                pltpu.VMEM((outer, dim), BF16),
                pltpu.VMEM((dim, outer), BF16),
                pltpu.VMEM((dim, window), BF16),
                pltpu.VMEM((window, window), F32),
                pltpu.VMEM((2, dim, window), BF16),
                pltpu.VMEM((2, outer, 2 * dim), BF16),
                pltpu.VMEM((2, heads, window, window), BF16),
                pltpu.VMEM((2, dim, window), BF16),
                pltpu.VMEM((2, window, dim), BF16),
                pltpu.VMEM((2, window, dim), BF16),
                pltpu.VMEM((2, window, 2 * dim), BF16),
                pltpu.VMEM((2, heads, window, slots), BF16),
                pltpu.VMEM((2, dim, slots), BF16),
                pltpu.VMEM((2, dim, slots), BF16),
                pltpu.VMEM((2, dim, slots), BF16),
                pltpu.VMEM((2, channel_pad, slots), F32),
                pltpu.VMEM((2, channel_pad, slots), BF16),
                pltpu.VMEM((channel_pad, dim), BF16),
                pltpu.VMEM((2, window, 2 * dim), BF16),
                pltpu.VMEM((outer, 2 * dim), F32),
            ],
        ),
        out_shape=[
            jax.ShapeDtypeStruct((channels, slots), F32),
            jax.ShapeDtypeStruct((channels, slots), F32),
            jax.ShapeDtypeStruct((grad_rows, dim), BF16),
        ],
        compiler_params=pltpu.CompilerParams(vmem_limit_bytes=56 * 2**20),
        cost_estimate=pl.CostEstimate(
            flops=10**10, bytes_accessed=12 * 2**20, transcendentals=2**21
        ),
        name="step",
    )(place, *operands)

    arrived = lax.ppermute(pred_other, "member", swap)
    lower = jnp.where(member == 0, pred_own, arrived)
    upper = jnp.where(member == 0, arrived, pred_own)
    prediction = jnp.concatenate([lower, upper], axis=1)[None]

    axes = ("member", "space")
    summed = lax.psum(grads, axes).astype(F32)
    blocks = [summed[i * dim : (i + 1) * dim] for i in range(8)]
    row = 8 * dim
    scale_grad = summed[row : row + noise_size]
    shift_grad = summed[row + noise_size : row + 2 * noise_size]
    row += 2 * noise_size
    head_grad = summed[row : row + channels]
    loss = summed[row + channel_pad, 0]
    return (
        prediction,
        scale_grad,
        shift_grad,
        jnp.concatenate(blocks[:3], axis=1),
        blocks[3],
        blocks[4],
        jnp.concatenate(blocks[5:7], axis=1),
        blocks[7],
        head_grad,
        loss,
    )


def solution(mesh):
    in_specs = (
        P("space", None),
        P("space", None),
        P(None, "space"),
        P(None, "space"),
        P("space"),
        P("member", None),
        P(None, "space"),
        P(None, "space"),
        P(None, "space"),
        P(None, "space"),
        P("space"),
        P(),
        P(),
        P(),
        P(),
        P(),
        P(),
        P(),
        P(),
    )
    out_specs = (P("member", None, "space"), P(), P(), P(), P(), P(), P(), P(), P(), P())
    return jax.shard_map(
        per_device, mesh=mesh, in_specs=in_specs, out_specs=out_specs, check_vma=False
    )
```

time: 479 us -> 251 us (0.52); the launches traced: 471 us -> 250 us
  local copies, waits for them, and re-layouts: 112 us -> 19.7 us
  other arithmetic: 95.6 us -> 5.51 us
  blocking collectives: 74.2 us -> 0 us
  waiting for transfers between devices: 97.1 us -> 152 us
  matrix products: 49.3 us -> 0 us
  Pallas kernels: 0 us -> 34.4 us
    psum x1 -> x0, blocking collectives: 74.2 us -> none  [per_device(): lax.psum((grad_cond_scale, grad_cond_shift, grad_attn_qkv, grad_attn_out,...]
    dot_general x25 -> x0, matrix products: 49.3 us -> none  [the longest x2 11.5 us: attend_back(): jnp.einsum('jrh,jrhe->rhe', grad_scores, key_heads, preferred_element_typ...]
    scatter-add x6 -> x0, other arithmetic: 46.6 us -> none  [the longest x1 27.8 us: per_device(): grad_dec_window = jnp.zeros(dec_window.shape, jnp.float32).at[grid_local....]
    psum x1, waiting for transfers between devices: 95.3 us -> 142 us  [per_device(): summed = lax.psum(grads, axes).astype(F32)]
    pallas_call x0 -> x2, Pallas kernels: none -> 34.4 us  [the longest x1 32.7 us: per_device(): pl.pallas_call(lambda *refs: step_kernel(*refs, total=total, scale_den=sc...]
    gather x2 -> x0, local copies, waits for them, and re-layouts: 23.7 us -> none  [the longest x1 14 us: per_device(): grid_gathered = dec_window[grid_local]]
    unnamed x151 -> x37, local copies, waits for them, and re-layouts: 30.4 us -> 9.51 us
    reshape x8 -> x0, local copies, waits for them, and re-layouts: 19.2 us -> none  [the longest x2 9.54 us: split_heads(): gathered[:, :, :feature_dim].reshape(nbr_count, row_count, head_count, HEAD)]
  transfers between devices with their start and end apart: 10 -> 9, of which waited for: 2 -> 3; matrix products, arithmetic and copies ran while one was open for 3% -> 1% of each run, Pallas kernels for 0% -> 1%
where the time goes in v1:
time: 251 us; the launch traced here: 250 us
  waiting for transfers between devices  152 us (61%)
  Pallas kernels  34.4 us (14%)
  starting transfers between devices  23.5 us (9%)
  local copies, waits for them, and re-layouts  19.7 us (8%)
  between operations  14.8 us (6%)
  other arithmetic  5.51 us (2%)
    psum x1, waiting for transfers between devices, per_device(): summed = lax.psum(grads, axes).astype(F32)  142 us
    pallas_call x1, Pallas kernels, per_device(): pl.pallas_call(lambda *refs: step_kernel(*refs, total=total, scale_den=sc...  32.7 us
    ppermute x6, starting transfers between devices, shift(): return lax.ppermute(value, 'space', pairs)  19.3 us
    unnamed x37, local copies, waits for them, and re-layouts  9.51 us
    ppermute x6, waiting for transfers between devices, shift(): return lax.ppermute(value, 'space', pairs)  5.97 us
  transfers between devices with their start and end apart: 9, of which 3 were waited for; matrix products, arithmetic and copies ran while one was open for 1% of the time, Pallas kernels for 1%

profile of v1, /device:TPU:1, one launch (start us, length us, event | category | flops | bytes accessed | tf_op | source)
XLA Modules:
  0.0 250.0 jit_solution(16691087912132948373)
XLA Ops:
  7.2 0.0 all-reduce.2.cloned.1.call-start
  7.2 0.7 convert_element_type.6
  7.9 0.7 pad_maximum_fusion.2.refs_6_
  8.6 0.0 copy-start.10
  8.6 1.4 collective-permute-start.5
  10.0 1.2 collective-permute-start.4
  11.2 5.8 %collective-permute-start.1 = (bf16[128,512]{1,0:T(8,128)(2,1)}, bf16[128,512]{1,0:T(8,128)(2,1)S(1)}, u32[]{:S(2)}, u32[]{:S(2)}) collective-permute-start(bf16[128,512]{1,0:T(8,128)(2,1)} %refs_1_.3), channel_id=1, source_target_pairs={{0,63},{1,0},{2,1},{3,2},{4,3},{5,4},{6,5},{7,6},{8,7},{9,8},{10,9... | collective-permute-start | bytes 393224 | tf_op jit(solution)/shard_map/ppermute | solution.py:403
  17.0 0.0 collective-permute-start
  17.0 2.5 collective-permute-start.6
  19.4 0.9 fusion.2
  21.0 0.1 pad_add_fusion.refs_0_
  21.1 1.2 copy-done
  22.3 0.0 copy-start.1
  22.3 1.0 copy-done.1
  23.3 0.0 copy-start.2
  23.3 0.7 copy-done.2
  24.0 0.0 copy-start.3
  24.0 0.7 copy-done.3
  24.8 0.0 copy-start.4
  24.8 1.7 prepare.1
  26.4 0.0 copy-start.5
  26.4 0.8 copy-done.5
  27.2 0.0 copy-start.6
  27.2 0.8 copy-done.6
  28.0 0.0 copy-start.7
  28.0 0.8 copy-done.7
  28.8 0.0 copy-start.8
  28.8 0.8 copy-done.8
  29.6 0.0 collective-permute-done.6
  29.6 10.9 %collective-permute-start.3 = (bf16[64,512]{1,0:T(8,128)(2,1)S(1)}, bf16[64,512]{1,0:T(8,128)(2,1)S(1)}, u32[]{:S(2)}, u32[]{:S(2)}) collective-permute-start(bf16[64,512]{1,0:T(8,128)(2,1)S(1)} %get-tuple-element.56), channel_id=1, source_target_pairs={{0,62},{1,63},{2,0},{3,1},{4,2},{5,3},{6,4},{7,5},{8,6},{9,7},{10,... | collective-permute-start | bytes 196616 | tf_op jit(solution)/shard_map/ppermute | solution.py:403
  40.5 0.0 collective-permute-done.5.refs_8_
  40.5 0.0 collective-permute-start.2
  40.5 0.7 pad_maximum_fusion.3
  41.2 0.7 copy.32
  41.9 0.0 collective-permute-done.4.refs_7_
  41.9 0.0 collective-permute-done.3.refs_5_
  41.9 0.0 copy-start.14
  41.9 6.0 %collective-permute-done.2.refs_4_ = bf16[64,512]{1,0:T(8,128)(2,1)S(1)} collective-permute-done((bf16[64,512]{1,0:T(8,128)(2,1)S(1)}, bf16[64,512]{1,0:T(8,128)(2,1)S(1)}, u32[]{:S(2)}, u32[]{:S(2)}) %collective-permute-start.2) | collective-permute-done | bytes 65568 | tf_op jit(solution)/shard_map/ppermute | solution.py:403
  47.9 0.0 collective-permute-done.1.refs_3_
  47.9 0.0 collective-permute-done.refs_2_
  47.9 0.0 copy-start.13
  47.9 0.0 copy-done.10
  47.9 0.0 copy-done.4
  47.9 0.0 copy-done.16
  47.9 0.0 copy-done.17
  47.9 0.0 copy-done.14
  48.0 0.6 copy-done.15
  48.5 0.0 copy-done.12
  48.5 0.0 copy-done.13
  48.6 32.7 %step.1 = (f32[84,512]{1,0:T(8,128)}, f32[84,512]{1,0:T(8,128)}, bf16[4352,512]{1,0:T(8,128)(2,1)}) custom-call(s32[3]{0:T(128)} %copy-done.4, bf16[128,512]{1,0:T(8,128)(2,1)} %refs_1_.3, bf16[128,512]{1,0:T(8,128)(2,1)} %copy-done.13, bf16[128,512]{1,0:T(8,128)(2,1)} %copy-done.12, bf16[64,512]{1,0:T(8,128)(2,1)} %copy-done.15, ...), custom_call_target="tpu_custom_call" | custom-call | flops 10000000000 | bytes 12582912 | tf_op jit(solution)/shard_map/step/pallas_call | solution.py:473
  81.3 0.0 copy-start.9
  81.3 0.0 all-reduce.2.cloned.1.call-update
  81.4 0.9 copy-done.11
  82.3 1.7 collective-permute-start.7
  84.0 4.4 %collective-permute-done.7 = f32[84,512]{1,0:T(8,128)S(1)} collective-permute-done((f32[84,512]{1,0:T(8,128)S(1)}, f32[84,512]{1,0:T(8,128)S(1)}, u32[]{:S(2)}, u32[]{:S(2)}) %collective-permute-start.7) | collective-permute-done | bytes 172064 | tf_op jit(solution)/shard_map/ppermute | solution.py:519
  88.4 0.0 copy-done.9
  88.5 1.1 copy.33
  89.6 141.6 %all-reduce.2.cloned.1.call-done = bf16[4352,512]{1,0:T(8,128)(2,1)} async-done(((bf16[4352,512]{1,0:T(8,128)(2,1)}), bf16[4352,512]{1,0:T(8,128)(2,1)}) %all-reduce.2.cloned.1.call-update) | async-done | bytes 4456464 | tf_op jit(solution)/shard_map/psum | solution.py:525
  231.2 4.4 %fusion = (f32[512,512]{1,0:T(8,128)}, f32[512,512]{1,0:T(8,128)S(1)}, f32[512,512]{1,0:T(8,128)S(1)}, f32[512,512]{1,0:T(8,128)}, f32[512,512]{1,0:T(8,128)}, /...) fusion(bf16[4352,512]{1,0:T(8,128)(2,1)} %all-reduce.2.cloned.1.call-done), kind=kLoop, calls=%fused_computation.8 | loop fusion | bytes 16777216 | tf_op jit(solution)/shard_map/slice | solution.py:526
  235.6 1.5 pad_maximum_fusion.1
  237.1 1.9 pad_maximum_fusion
  238.9 1.2 slice.67
  240.1 1.4 fusion.1
  241.6 1.6 slice.66
  (8 shorter events, 0.1 us)
Async XLA Ops:
  7.2 224.0 %all-reduce.2.cloned.1.call-start = ((), (), s32[]{:S(2)}) async-start(), calls=%async_computation | async-start | bytes 8912896 | tf_op jit(solution)/shard_map/psum | solution.py:525
  8.6 39.3 %copy-start.10 = (f32[32,128]{1,0:T(8,128)}, f32[32,128]{1,0:T(8,128)S(1)}, u32[]{:S(2)}) copy-start(f32[32,128]{1,0:T(8,128)S(1)} %pad_maximum_fusion.2.refs_6_) | copy-start | bytes 49156
  8.6 31.9 %collective-permute-start.5 = (f32[32,128]{1,0:T(8,128)S(1)}, f32[32,128]{1,0:T(8,128)S(1)}, u32[]{:S(2)}, u32[]{:S(2)}) collective-permute-start(f32[32,128]{1,0:T(8,128)S(1)} %pad_maximum_fusion.2.refs_6_), channel_id=1, source_target_pairs={{0,63},{1,0},{2,1},{3,2},{4,3},{5,4},{6,5},{7,6},{8,7},{9,8},{10,9... | collective-permute-start | bytes 49160 | tf_op jit(solution)/shard_map/ppermute | solution.py:403
  10.0 31.9 %collective-permute-start.4 = (f32[32,128]{1,0:T(8,128)S(1)}, f32[32,128]{1,0:T(8,128)S(1)}, u32[]{:S(2)}, u32[]{:S(2)}) collective-permute-start(f32[32,128]{1,0:T(8,128)S(1)} %pad_maximum_fusion.2.refs_6_), channel_id=1, source_target_pairs={{0,1},{1,2},{2,3},{3,4},{4,5},{5,6},{6,7},{7,8},{8,9},{9,10},{10,1... | collective-permute-start | bytes 49160 | tf_op jit(solution)/shard_map/ppermute | solution.py:403
  11.2 36.7 %collective-permute-start.1 = (bf16[128,512]{1,0:T(8,128)(2,1)}, bf16[128,512]{1,0:T(8,128)(2,1)S(1)}, u32[]{:S(2)}, u32[]{:S(2)}) collective-permute-start(bf16[128,512]{1,0:T(8,128)(2,1)} %refs_1_.3), channel_id=1, source_target_pairs={{0,63},{1,0},{2,1},{3,2},{4,3},{5,4},{6,5},{7,6},{8,7},{9,8},{10,9... | collective-permute-start | bytes 393224 | tf_op jit(solution)/shard_map/ppermute | solution.py:403
  17.0 30.9 %collective-permute-start = (bf16[128,512]{1,0:T(8,128)(2,1)}, bf16[128,512]{1,0:T(8,128)(2,1)S(1)}, u32[]{:S(2)}, u32[]{:S(2)}) collective-permute-start(bf16[128,512]{1,0:T(8,128)(2,1)} %refs_1_.3), channel_id=1, source_target_pairs={{0,1},{1,2},{2,3},{3,4},{4,5},{5,6},{6,7},{7,8},{8,9},{9,10},{10,1... | collective-permute-start | bytes 393224 | tf_op jit(solution)/shard_map/ppermute | solution.py:403
  17.0 12.6 %collective-permute-start.6 = (f32[1,32]{1,0:T(1,128)}, f32[1,32]{1,0:T(1,128)S(1)}, u32[]{:S(2)}, u32[]{:S(2)}) collective-permute-start(f32[1,32]{1,0:T(1,128)} %param.24), channel_id=1, source_target_pairs={{0,64},{64,0},{1,65},{65,1},{2,66},{66,2},{3,67},{67,3},{4,68},{68... | collective-permute-start | bytes 392 | tf_op jit(solution)/shard_map/ppermute | solution.py:413
  21.1 1.2 copy-start
  22.3 1.0 copy-start.1
  23.3 0.7 copy-start.2
  24.0 0.7 copy-start.3
  24.8 23.2 %copy-start.4 = (s32[3]{0:T(128)}, s32[3]{0:T(128)S(1)}, u32[]{:S(2)}) copy-start(s32[3]{0:T(128)S(1)} %pad_add_fusion.refs_0_) | copy-start | bytes 40
  26.4 0.8 copy-start.5
  27.2 0.8 copy-start.6
  28.0 0.8 copy-start.7
  28.8 0.8 copy-start.8
  29.6 12.3 %collective-permute-start.3 = (bf16[64,512]{1,0:T(8,128)(2,1)S(1)}, bf16[64,512]{1,0:T(8,128)(2,1)S(1)}, u32[]{:S(2)}, u32[]{:S(2)}) collective-permute-start(bf16[64,512]{1,0:T(8,128)(2,1)S(1)} %get-tuple-element.56), channel_id=1, source_target_pairs={{0,62},{1,63},{2,0},{3,1},{4,2},{5,3},{6,4},{7,5},{8,6},{9,7},{10,... | collective-permute-start | bytes 196616 | tf_op jit(solution)/shard_map/ppermute | solution.py:403
  40.5 7.4 %copy-start.16 = (f32[32,128]{1,0:T(8,128)}, f32[32,128]{1,0:T(8,128)S(1)}, u32[]{:S(2)}) copy-start(f32[32,128]{1,0:T(8,128)S(1)} %collective-permute-done.5.refs_8_) | copy-start | bytes 49156
  40.5 7.3 %collective-permute-start.2 = (bf16[64,512]{1,0:T(8,128)(2,1)S(1)}, bf16[64,512]{1,0:T(8,128)(2,1)S(1)}, u32[]{:S(2)}, u32[]{:S(2)}) collective-permute-start(bf16[64,512]{1,0:T(8,128)(2,1)S(1)} %get-tuple-element.57), channel_id=1, source_target_pairs={{0,2},{1,3},{2,4},{3,5},{4,6},{5,7},{6,8},{7,9},{8,10},{9,11},{10,... | collective-permute-start | bytes 196616 | tf_op jit(solution)/shard_map/ppermute | solution.py:403
  41.9 6.0 %copy-start.17 = (f32[32,128]{1,0:T(8,128)}, f32[32,128]{1,0:T(8,128)S(1)}, u32[]{:S(2)}) copy-start(f32[32,128]{1,0:T(8,128)S(1)} %collective-permute-done.4.refs_7_) | copy-start | bytes 49156
  41.9 6.0 %copy-start.14 = (bf16[64,512]{1,0:T(8,128)(2,1)}, bf16[64,512]{1,0:T(8,128)(2,1)S(1)}, u32[]{:S(2)}) copy-start(bf16[64,512]{1,0:T(8,128)(2,1)S(1)} %collective-permute-done.3.refs_5_) | copy-start | bytes 196612
  47.9 0.6 copy-start.15
  47.9 0.7 copy-start.12
  47.9 0.7 copy-start.13
  81.3 0.9 copy-start.11
  81.3 7.1 %copy-start.9 = (f32[84,512]{1,0:T(8,128)S(1)}, f32[84,512]{1,0:T(8,128)}, u32[]{:S(2)}) copy-start(f32[84,512]{1,0:T(8,128)} %get-tuple-element.21) | copy-start | bytes 516100
  82.3 6.2 %collective-permute-start.7 = (f32[84,512]{1,0:T(8,128)S(1)}, f32[84,512]{1,0:T(8,128)S(1)}, u32[]{:S(2)}, u32[]{:S(2)}) collective-permute-start(f32[84,512]{1,0:T(8,128)S(1)} %copy-done.11), channel_id=1, source_target_pairs={{0,64},{64,0},{1,65},{65,1},{2,66},{66,2},{3,67},{67,3},{4,68},{68... | collective-permute-start | bytes 516104 | tf_op jit(solution)/shard_map/ppermute | solution.py:519
Sparse Core Ops, SparseCore 0:
  81.5 149.6 all-reduce.1

commit v2 on v1

--- a/solution.py
+++ b/solution.py
@@ -64,6 +64,32 @@
     probs = probs.astype(F32)
     inner = jnp.sum(probs * grad_probs, axis=0, keepdims=True)
     return (probs * (grad_probs - inner) * (1.0 / math.sqrt(HEAD))).astype(BF16)
+
+
+def split_terms(values):
+    high = values.astype(BF16)
+    rest = values - high.astype(F32)
+    middle = rest.astype(BF16)
+    low = (rest - middle.astype(F32)).astype(BF16)
+    return high, middle, low
+
+
+def joined_terms(high, middle, low):
+    return high.astype(F32) + (middle.astype(F32) + low.astype(F32))
+
+
+def pack_kernel(place, latent, nbrs, bias, noise, packet, upward, *, total):
+    rows = latent.shape[0]
+    halo = rows // 2
+    packet[:rows] = latent[...]
+    slots = ((nbrs[...] - place[1]) & (total - 1)).astype(F32).astype(BF16)
+    packet[rows:] = jnp.concatenate([slots, *split_terms(bias[...])], axis=1)
+    upward[:halo] = latent[halo:]
+    spare = jnp.zeros((1, rows - noise.shape[1]), F32)
+    padded = jnp.concatenate([noise[...], spare], axis=1)
+    padded = jnp.broadcast_to(padded, (upward.shape[0] - halo, rows))
+    terms = split_terms(padded)
+    upward[halo:] = jnp.concatenate([*terms, jnp.zeros_like(terms[0])], axis=1)
 
 
 def prepare_kernel(
@@ -94,14 +120,31 @@
 def step_kernel(
     place,
     own,
-    before,
-    after,
-    before2,
-    after2,
     edges,
-    edges_before,
-    edges_after,
-    noise,
+    twin,
+    beside,
+    below,
+    above,
+    noise_own,
+    embed_hbm,
+    norm_hbm,
+    query_hbm,
+    logits_hbm,
+    weather_hbm,
+    target_hbm,
+    area_hbm,
+    scale_hbm,
+    shift_hbm,
+    qkv_hbm,
+    attn_out_hbm,
+    dec_kv_hbm,
+    dec_out_hbm,
+    head_hbm,
+    pred_own_hbm,
+    pred_other_hbm,
+    keep_hbm,
+    send_hbm,
+    noise_out,
     embed_t,
     norm_t,
     query_t,
@@ -116,8 +159,7 @@
     dec_kv,
     dec_out,
     head_out,
-    pred_own,
-    pred_other,
+    pred,
     grads,
     latent,
     unit_t,
@@ -139,8 +181,9 @@
     head_pad,
     grad_dec,
     grad_kv,
+    load_sems,
+    store_sems,
     *,
-    total,
     scale_den,
 ):
     rows, dim = own.shape
@@ -151,28 +194,64 @@
     channels = weather.shape[0]
     slots = embed_t.shape[1]
     inv_sqrt = 1.0 / math.sqrt(HEAD)
-
-    latent[0:halo] = before2[...]
-    latent[halo : halo + rows] = before[...]
+    member = place[0]
+    core = place[3]
+    here = pl.ds(pl.multiple_of(member * slots, slots), slots)
+
+    loads = {}
+
+    def load(name, source, target_ref):
+        loads[name] = pltpu.make_async_copy(source, target_ref, load_sems.at[len(loads)])
+        loads[name].start()
+
+    load("scale", scale_hbm, cond_scale)
+    load("shift", shift_hbm, cond_shift)
+    load("qkv", qkv_hbm, attn_qkv)
+    load("attn_out", attn_out_hbm, attn_out)
+    load("dec_kv", dec_kv_hbm, dec_kv)
+    load("query", query_hbm, query_t)
+    load("logits", logits_hbm, grid_logits)
+    load("embed", embed_hbm, embed_t)
+    load("dec_out", dec_out_hbm, dec_out)
+    load("head", head_hbm, head_out)
+    load("weather", weather_hbm.at[:, here], weather)
+    load("target", target_hbm.at[:, here], target)
+    load("area", area_hbm.at[:, here], area)
+    load("norm", norm_hbm, norm_t)
+
+    odd = core == 1
+    latent[0:halo] = below[:halo]
+    latent[halo : halo + rows] = jnp.where(odd, twin[:rows], beside[:rows])
     latent[halo + rows : halo + 2 * rows] = own[...]
-    latent[halo + 2 * rows : halo + 3 * rows] = after[...]
-    latent[halo + 3 * rows :] = after2[...]
+    latent[halo + 2 * rows : halo + 3 * rows] = jnp.where(odd, beside[:rows], twin[:rows])
+    latent[halo + 3 * rows :] = above[...]
     unit = normalize(latent[...].astype(F32), 1)[0]
     unit_t[...] = unit.astype(BF16).T
     unit_q_t[...] = window_order(unit, rows, halo).astype(BF16).T
 
-    lane = lax.broadcasted_iota(jnp.int32, edges.shape, 1)
-    ends = pltpu.roll(jnp.where(lane >= halo, edges_before[...], edges_after[...]), halo, 1)
-    entries = edges.shape[0] // 2
-    lane = lane[:entries]
-    own_slots = (edges[:entries].astype(jnp.int32) - place[1]) & (total - 1)
-    end_start = place[1] + jnp.where(lane < halo, -rows, rows)
-    end_slots = (ends[:entries].astype(jnp.int32) - end_start) & (total - 1)
+    lane = lax.broadcasted_iota(jnp.int32, (edges.shape[0], rows), 1)
+    late = (lane >= halo) == odd
+    ends = jnp.where(
+        jnp.concatenate([late] * 4, axis=1), twin[rows:].astype(F32), beside[rows:].astype(F32)
+    )
+    lists = edges[...].astype(F32)
+
+    def listed(part):
+        return [
+            lists[:, part * rows : (part + 1) * rows],
+            pltpu.roll(ends[:, part * rows : (part + 1) * rows], halo, 1),
+        ]
+
     mesh_logits[...] = spread_bias(
-        jnp.concatenate([own_slots, end_slots], axis=1),
-        jnp.concatenate([edges[entries:], ends[entries:]], axis=1),
+        jnp.concatenate(listed(0), axis=1).astype(jnp.int32),
+        joined_terms(*(jnp.concatenate(listed(part), axis=1) for part in (1, 2, 3))),
         window,
     )
+    noise_row = joined_terms(*(below[halo:, part * rows : (part + 1) * rows] for part in (0, 1, 2)))
+    spread = cond_scale.shape[0]
+    noise_other = jnp.broadcast_to(noise_row[:1], (rows, rows)).T[:spread, :1]
+    noise = [noise_own[...], noise_other]
+    noise_out[...] = noise_other
     is_before = lax.broadcasted_iota(jnp.int32, (window, rows), 1) < halo
 
     def split_ends(values):
@@ -186,13 +265,15 @@
         ends = nn(keys, queries[:, rows:])
         return jnp.concatenate([mid, jnp.where(is_before, ends[:window], ends[window:])], axis=1)
 
+    loads["scale"].wait()
+    loads["shift"].wait()
     gains = []
     shifts = []
     for m in range(members):
-        noise_col = noise[:, m : m + 1]
-        gains.append(1.0 + jnp.sum(noise_col * cond_scale[...], axis=0, keepdims=True))
-        shifts.append(jnp.sum(noise_col * cond_shift[...], axis=0, keepdims=True))
-
+        gains.append(1.0 + jnp.sum(noise[m] * cond_scale[...], axis=0, keepdims=True))
+        shifts.append(jnp.sum(noise[m] * cond_shift[...], axis=0, keepdims=True))
+
+    loads["qkv"].wait()
     for m in range(members):
         act = (unit * gains[m] + shifts[m]).astype(BF16)
         mesh_kv[m] = nn(act, attn_qkv[:, dim:]).astype(BF16)
@@ -208,6 +289,9 @@
             mid = tn(values[rows : rows + window], probs[:, :rows])
             ends = tn(values, split_ends(probs[:, rows:]))
             mesh_mixed[m, cols, :] = jnp.concatenate([mid, ends], axis=1).astype(BF16)
+        if m == 0:
+            loads["attn_out"].wait()
+            loads["dec_kv"].wait()
         residual = window_order(latent[...].astype(F32), rows, halo)
         out = (residual + nn(mesh_mixed[m].T, attn_out[...])).astype(BF16)
         mesh_out[m] = out
@@ -215,6 +299,8 @@
         mesh_norm[m] = norm
         dec_keys[m] = nn(norm, dec_kv[...]).astype(BF16)
 
+    for name in ("query", "logits", "embed", "dec_out", "head"):
+        loads[name].wait()
     head_pad[...] = jnp.zeros_like(head_pad)
     head_pad[:channels] = head_out[...]
     for m in range(members):
@@ -231,13 +317,21 @@
         grid_final[m] = final
         change[m] = nn(head_pad[...], final)
 
+    for name in ("weather", "target", "area", "norm"):
+        loads[name].wait()
     slot = lax.broadcasted_iota(jnp.int32, (1, slots), 1) + place[0] * slots
     live = jnp.where(slot < place[2], 1.0, 0.0)
     weighting = live * area[...]
     first = weather[...] + live * change[0, :channels]
     second = weather[...] + live * change[1, :channels]
-    pred_own[...] = first
-    pred_other[...] = second
+    pred[0] = first
+    pred[1] = second
+    stores = [
+        pltpu.make_async_copy(pred.at[0], pred_own_hbm, store_sems.at[0]),
+        pltpu.make_async_copy(pred.at[1], pred_other_hbm, store_sems.at[1]),
+    ]
+    for store in stores:
+        store.start()
 
     def smooth(values):
         square = values * values + SMOOTHING
@@ -282,8 +376,7 @@
     grad_dec_kv = None
     grad_attn_out = None
     grad_qkv = None
-    grad_scale = None
-    grad_shift = None
+    grad_cond = None
     for m in range(members):
         g_dec = grad_dec[m]
         term = tn(mesh_norm[m], g_dec)
@@ -327,15 +420,16 @@
         weight = attn_qkv[...].astype(F32)
         g_gain = jnp.sum(weight * moment, axis=1, keepdims=True)
         g_shift = jnp.sum(weight * col_sum, axis=1, keepdims=True)
-        noise_col = noise[:, m : m + 1]
-        spread = noise.shape[0]
-        term = noise_col * jnp.broadcast_to(g_gain, (dim, HEAD)).T[:spread]
-        grad_scale = term if m == 0 else grad_scale + term
-        term = noise_col * jnp.broadcast_to(g_shift, (dim, HEAD)).T[:spread]
-        grad_shift = term if m == 0 else grad_shift + term
-
-    row = 0
-    for block in (
+        mine = member if m == 0 else 1 - member
+        row_id = lax.broadcasted_iota(jnp.int32, (16, dim), 0)
+        term = jnp.where(row_id == mine, jnp.broadcast_to(g_gain, (dim, HEAD)).T[:16], 0.0)
+        term += jnp.where(row_id == mine + 2, jnp.broadcast_to(g_shift, (dim, HEAD)).T[:16], 0.0)
+        grad_cond = term if m == 0 else grad_cond + term
+
+    row_id = lax.broadcasted_iota(jnp.int32, (16, dim), 0)
+    grad_cond += jnp.where(row_id == 4, loss, 0.0)
+    grads[:, :, HEAD:, :] = jnp.zeros((2, 64, 16, HEAD), BF16)
+    blocks = (
         grad_qkv[:, :dim],
         grad_qkv[:, dim : 2 * dim],
         grad_qkv[:, 2 * dim :],
@@ -344,15 +438,115 @@
         grad_dec_kv[:, :dim],
         grad_dec_kv[:, dim:],
         grad_dec_out,
-        grad_scale,
-        grad_shift,
-        grad_head,
-    ):
-        grads[row : row + block.shape[0]] = block.astype(grads.dtype)
-        row += block.shape[0]
-    rest = grads.shape[0] - row
-    tail_row = lax.broadcasted_iota(jnp.int32, (rest, dim), 0)
-    grads[row:] = jnp.where(tail_row == 0, loss, 0.0).astype(grads.dtype)
+    )
+    tall = HEAD * HEAD // dim
+    for i, block in enumerate(blocks):
+        first_chunk = i % 4 * (dim // tall)
+        for c in range(dim // tall):
+            for t in range(heads):
+                grads[i // 4, first_chunk + c, t * tall : (t + 1) * tall, :] = block[
+                    c * tall : (c + 1) * tall, t * HEAD : (t + 1) * HEAD
+                ].astype(BF16)
+    extras = jnp.concatenate([grad_head, grad_cond], axis=0)
+    for i in range(extras.shape[0] // 16):
+        for t in range(heads):
+            grads[0, i * heads + t, HEAD:, :] = extras[
+                i * 16 : (i + 1) * 16, t * HEAD : (t + 1) * HEAD
+            ].astype(BF16)
+    keep = pltpu.make_async_copy(grads.at[core], keep_hbm, store_sems.at[2])
+    send = pltpu.make_async_copy(grads.at[1 - core], send_hbm, store_sems.at[3])
+    keep.start()
+    send.start()
+    stores += [keep, send]
+    for store in stores:
+        store.wait()
+
+
+def sum_kernel(parts, result):
+    total = jnp.sum(parts[...].astype(F32), axis=0, keepdims=True)
+    result[...] = jnp.broadcast_to(total.astype(BF16), result.shape)
+
+
+def unpack_kernel(
+    place,
+    mine_hbm,
+    theirs_hbm,
+    noise_own,
+    noise_other,
+    pred_own_hbm,
+    pred_arrived_hbm,
+    pred_hbm,
+    grad_scale,
+    grad_shift,
+    grad_qkv,
+    grad_attn_out,
+    grad_dec_query,
+    grad_dec_kv,
+    grad_dec_out,
+    grad_head,
+    loss,
+    grads,
+    sems,
+):
+    member = place[0]
+    core = place[3]
+    channels, slots = pred_own_hbm.shape
+    dim = grad_attn_out.shape[0]
+    heads = dim // HEAD
+    here = pl.ds(pl.multiple_of(member * slots, slots), slots)
+    there = pl.ds(pl.multiple_of((1 - member) * slots, slots), slots)
+    copies = [
+        pltpu.make_async_copy(mine_hbm, grads.at[core], sems.at[0]),
+        pltpu.make_async_copy(theirs_hbm, grads.at[1 - core], sems.at[1]),
+        pltpu.make_async_copy(pred_own_hbm, pred_hbm.at[0, :, here], sems.at[2]),
+        pltpu.make_async_copy(pred_arrived_hbm, pred_hbm.at[0, :, there], sems.at[3]),
+    ]
+    for copy in copies:
+        copy.start()
+    copies[0].wait()
+    copies[1].wait()
+    tall = HEAD * HEAD // dim
+    targets = (
+        (grad_qkv, 0),
+        (grad_qkv, dim),
+        (grad_qkv, 2 * dim),
+        (grad_attn_out, 0),
+        (grad_dec_query, 0),
+        (grad_dec_kv, 0),
+        (grad_dec_kv, dim),
+        (grad_dec_out, 0),
+    )
+    for i, (ref, col) in enumerate(targets):
+        first_chunk = i % 4 * (dim // tall)
+        for c in range(dim // tall):
+            for t in range(heads):
+                ref[c * tall : (c + 1) * tall, col + t * HEAD : col + (t + 1) * HEAD] = grads[
+                    i // 4, first_chunk + c, t * tall : (t + 1) * tall, :
+                ].astype(F32)
+
+    def extra(i):
+        return jnp.concatenate(
+            [grads[0, i * heads + t, HEAD:, :].astype(F32) for t in range(heads)], axis=1
+        )
+
+    head_blocks = -(-channels // 16)
+    for i in range(head_blocks):
+        count = min(16, channels - i * 16)
+        grad_head[i * 16 : i * 16 + count] = extra(i)[:count]
+    cond = extra(2 * (-(-channels // 32)))
+    first = cond[0:1]
+    second = cond[1:2]
+    grad_scale[...] = noise_own[...] * jnp.where(member == 0, first, second) + noise_other[
+        ...
+    ] * jnp.where(member == 0, second, first)
+    first = cond[2:3]
+    second = cond[3:4]
+    grad_shift[...] = noise_own[...] * jnp.where(member == 0, first, second) + noise_other[
+        ...
+    ] * jnp.where(member == 0, second, first)
+    loss[...] = cond[4:5, :HEAD]
+    copies[2].wait()
+    copies[3].wait()
 
 
 def whole(shape):
@@ -395,23 +589,33 @@
     scale_den = 2.0 * channels * grid_slots * size
 
     member = lax.axis_index("member")
-    start = lax.axis_index("space") * rows - halo
-    place = jnp.stack([member, start, grid_counts[0]]).astype(jnp.int32)
-
-    def shift(value, hops):
-        pairs = [(i, (i + hops) % size) for i in range(size)]
-        return lax.ppermute(value, "space", pairs)
-
-    swap = [(0, 1), (1, 0)]
-    edges = jnp.concatenate([mesh_nbrs.astype(F32), mesh_bias], axis=0)
-    before = shift(mesh_latent, 1)
-    after = shift(mesh_latent, -1)
-    before2 = shift(mesh_latent[halo:], 2)
-    after2 = shift(mesh_latent[:halo], -2)
-    edges_before = shift(edges, 1)
-    edges_after = shift(edges, -1)
-    other_noise = lax.ppermute(member_noise, "member", swap)
-    noise = jnp.concatenate([member_noise, other_noise], axis=0).T
+    space = lax.axis_index("space")
+    start = space * rows - halo
+    place = jnp.stack([member, start, grid_counts[0], space % 2]).astype(jnp.int32)
+    axes = ("member", "space")
+
+    def permute(value, target_of):
+        pairs = []
+        for m in range(2):
+            for k in range(size):
+                to_m, to_k = target_of(m, k)
+                pairs.append((m * size + k, to_m * size + to_k % size))
+        return lax.ppermute(value, axes, pairs)
+
+    smem = pl.BlockSpec(memory_space=pltpu.SMEM)
+    packet, upward = pl.pallas_call(
+        lambda *refs: pack_kernel(*refs, total=total),
+        in_specs=[smem] + [pl.BlockSpec(memory_space=pltpu.VMEM)] * 4,
+        out_shape=[
+            jax.ShapeDtypeStruct((rows + mesh_nbrs.shape[0], dim), BF16),
+            jax.ShapeDtypeStruct((halo + 16, dim), BF16),
+        ],
+        name="pack",
+    )(place, mesh_latent, mesh_nbrs, mesh_bias, member_noise)
+    beside = permute(packet, lambda m, k: (m, k + 1 if k % 2 else k - 1))
+    below = permute(upward, lambda m, k: (1 - m, k + 2))
+    above = permute(mesh_latent[:halo], lambda m, k: (m, k - 2))
+    twin = permute(packet, lambda m, k: (m, k ^ 1))
 
     part = pl.BlockSpec((slots, dim), lambda i, place: (place[0], 0))
     lists = pl.BlockSpec((entries, slots), lambda i, place: (0, place[0]))
@@ -438,19 +642,18 @@
     )(place, grid_embed, grid_nbrs, grid_bias, dec_query)
 
     channel_pad = -(-channels // 32) * 32
-    grad_rows = 8 * dim + 2 * noise_size + channel_pad + 16
-    grad_rows = -(-grad_rows // 256) * 256
-    fields = pl.BlockSpec((channels, slots), lambda i, place: (0, place[0]))
-    operands = (
+    chunks = size
+    half_shape = (chunks, HEAD + 16, HEAD)
+    hbm = pl.BlockSpec(memory_space=pl.ANY)
+    vmem = pl.BlockSpec(memory_space=pltpu.VMEM)
+    step_in = (
         mesh_latent,
-        before,
-        after,
-        before2,
-        after2,
-        edges,
-        edges_before,
-        edges_after,
-        noise,
+        packet[rows:],
+        twin,
+        beside,
+        below,
+        above,
+        member_noise.reshape(noise_size, 1),
         embed_t,
         norm_t,
         query_t,
@@ -466,82 +669,111 @@
         dec_out,
         head_out,
     )
-    specs = [whole(value.shape) for value in operands]
-    specs[13] = fields
-    specs[14] = fields
-    specs[15] = pl.BlockSpec((1, slots), lambda i, place: (0, place[0]))
-    pred_own, pred_other, grads = pl.pallas_call(
-        lambda *refs: step_kernel(*refs, total=total, scale_den=scale_den),
-        grid_spec=pltpu.PrefetchScalarGridSpec(
-            num_scalar_prefetch=1,
-            grid=(1,),
-            in_specs=specs,
-            out_specs=[
-                whole((channels, slots)),
-                whole((channels, slots)),
-                whole((grad_rows, dim)),
-            ],
-            scratch_shapes=[
-                pltpu.VMEM((outer, dim), BF16),
-                pltpu.VMEM((dim, outer), BF16),
-                pltpu.VMEM((dim, window), BF16),
-                pltpu.VMEM((window, window), F32),
-                pltpu.VMEM((2, dim, window), BF16),
-                pltpu.VMEM((2, outer, 2 * dim), BF16),
-                pltpu.VMEM((2, heads, window, window), BF16),
-                pltpu.VMEM((2, dim, window), BF16),
-                pltpu.VMEM((2, window, dim), BF16),
-                pltpu.VMEM((2, window, dim), BF16),
-                pltpu.VMEM((2, window, 2 * dim), BF16),
-                pltpu.VMEM((2, heads, window, slots), BF16),
-                pltpu.VMEM((2, dim, slots), BF16),
-                pltpu.VMEM((2, dim, slots), BF16),
-                pltpu.VMEM((2, dim, slots), BF16),
-                pltpu.VMEM((2, channel_pad, slots), F32),
-                pltpu.VMEM((2, channel_pad, slots), BF16),
-                pltpu.VMEM((channel_pad, dim), BF16),
-                pltpu.VMEM((2, window, 2 * dim), BF16),
-                pltpu.VMEM((outer, 2 * dim), F32),
-            ],
-        ),
+    pred_own, pred_other, keep, send, other_noise = pl.pallas_call(
+        lambda *refs: step_kernel(*refs, scale_den=scale_den),
+        in_specs=[smem] + [vmem] * 7 + [hbm] * 14,
+        out_specs=[hbm] * 4 + [vmem],
+        scratch_shapes=[
+            pltpu.VMEM(square, BF16),
+            pltpu.VMEM(square, BF16),
+            pltpu.VMEM(square, BF16),
+            pltpu.VMEM((window, slots), F32),
+            pltpu.VMEM((channels, slots), F32),
+            pltpu.VMEM((channels, slots), F32),
+            pltpu.VMEM((1, slots), F32),
+            pltpu.VMEM(cond_scale.shape, F32),
+            pltpu.VMEM(cond_shift.shape, F32),
+            pltpu.VMEM(attn_qkv.shape, BF16),
+            pltpu.VMEM(attn_out.shape, BF16),
+            pltpu.VMEM(dec_kv.shape, BF16),
+            pltpu.VMEM(dec_out.shape, BF16),
+            pltpu.VMEM(head_out.shape, BF16),
+            pltpu.VMEM((2, channels, slots), F32),
+            pltpu.VMEM((2, *half_shape), BF16),
+            pltpu.VMEM((outer, dim), BF16),
+            pltpu.VMEM((dim, outer), BF16),
+            pltpu.VMEM((dim, window), BF16),
+            pltpu.VMEM((window, window), F32),
+            pltpu.VMEM((2, dim, window), BF16),
+            pltpu.VMEM((2, outer, 2 * dim), BF16),
+            pltpu.VMEM((2, heads, window, window), BF16),
+            pltpu.VMEM((2, dim, window), BF16),
+            pltpu.VMEM((2, window, dim), BF16),
+            pltpu.VMEM((2, window, dim), BF16),
+            pltpu.VMEM((2, window, 2 * dim), BF16),
+            pltpu.VMEM((2, heads, window, slots), BF16),
+            pltpu.VMEM((2, dim, slots), BF16),
+            pltpu.VMEM((2, dim, slots), BF16),
+            pltpu.VMEM((2, dim, slots), BF16),
+            pltpu.VMEM((2, channel_pad, slots), F32),
+            pltpu.VMEM((2, channel_pad, slots), BF16),
+            pltpu.VMEM((channel_pad, dim), BF16),
+            pltpu.VMEM((2, window, 2 * dim), BF16),
+            pltpu.VMEM((outer, 2 * dim), F32),
+            pltpu.SemaphoreType.DMA((14,)),
+            pltpu.SemaphoreType.DMA((4,)),
+        ],
         out_shape=[
             jax.ShapeDtypeStruct((channels, slots), F32),
             jax.ShapeDtypeStruct((channels, slots), F32),
-            jax.ShapeDtypeStruct((grad_rows, dim), BF16),
+            jax.ShapeDtypeStruct(half_shape, BF16),
+            jax.ShapeDtypeStruct(half_shape, BF16),
+            jax.ShapeDtypeStruct((noise_size, 1), F32),
         ],
         compiler_params=pltpu.CompilerParams(vmem_limit_bytes=56 * 2**20),
         cost_estimate=pl.CostEstimate(
             flops=10**10, bytes_accessed=12 * 2**20, transcendentals=2**21
         ),
         name="step",
-    )(place, *operands)
-
-    arrived = lax.ppermute(pred_other, "member", swap)
-    lower = jnp.where(member == 0, pred_own, arrived)
-    upper = jnp.where(member == 0, arrived, pred_own)
-    prediction = jnp.concatenate([lower, upper], axis=1)[None]
-
-    axes = ("member", "space")
-    summed = lax.psum(grads, axes).astype(F32)
-    blocks = [summed[i * dim : (i + 1) * dim] for i in range(8)]
-    row = 8 * dim
-    scale_grad = summed[row : row + noise_size]
-    shift_grad = summed[row + noise_size : row + 2 * noise_size]
-    row += 2 * noise_size
-    head_grad = summed[row : row + channels]
-    loss = summed[row + channel_pad, 0]
-    return (
-        prediction,
-        scale_grad,
-        shift_grad,
-        jnp.concatenate(blocks[:3], axis=1),
-        blocks[3],
-        blocks[4],
-        jnp.concatenate(blocks[5:7], axis=1),
-        blocks[7],
-        head_grad,
-        loss,
-    )
+    )(place, *step_in)
+
+    def twin_swap(value):
+        return permute(value, lambda m, k: (m, k ^ 1))
+
+    groups = [
+        [m * size + k for m in range(2) for k in range(size) if k % 2 == c] for c in range(2)
+    ]
+
+    def over_chips(value):
+        return lax.all_to_all(value, axes, 0, 0, axis_index_groups=groups)
+
+    arrived_pred = permute(pred_other, lambda m, k: (1 - m, k))
+    pair = (keep.astype(F32) + twin_swap(send).astype(F32)).astype(BF16)
+    parts = over_chips(pair)
+    shared = pl.pallas_call(
+        sum_kernel,
+        in_specs=[vmem],
+        out_specs=vmem,
+        out_shape=jax.ShapeDtypeStruct(half_shape, BF16),
+        compiler_params=pltpu.CompilerParams(vmem_limit_bytes=32 * 2**20),
+        name="sum",
+    )(parts)
+    mine = over_chips(shared)
+    theirs = twin_swap(mine)
+    grad_shapes = [
+        jax.ShapeDtypeStruct(shape, F32)
+        for shape in (
+            cond_scale.shape,
+            cond_shift.shape,
+            attn_qkv.shape,
+            attn_out.shape,
+            dec_query.shape,
+            dec_kv.shape,
+            dec_out.shape,
+            head_out.shape,
+            (1, HEAD),
+        )
+    ]
+    outputs = pl.pallas_call(
+        unpack_kernel,
+        in_specs=[smem, hbm, hbm, vmem, vmem, hbm, hbm],
+        out_specs=[hbm] + [vmem] * 9,
+        out_shape=[jax.ShapeDtypeStruct((1, channels, grid_slots), F32)] + grad_shapes,
+        scratch_shapes=[pltpu.VMEM((2, *half_shape), BF16), pltpu.SemaphoreType.DMA((4,))],
+        compiler_params=pltpu.CompilerParams(vmem_limit_bytes=40 * 2**20),
+        name="unpack",
+    )(place, mine, theirs, step_in[6], other_noise, pred_own, arrived_pred)
+    return (*outputs[:9], outputs[9][0, 0])
 
 
 def solution(mesh):

time: 251 us -> 162 us (0.65)
  waiting for transfers between devices: 152 us -> 10.5 us
  blocking collectives: 0 us -> 73.4 us
  between operations: 14.8 us -> 1.46 us
  local copies, waits for them, and re-layouts: 19.7 us -> 12.8 us
  Pallas kernels: 34.4 us -> 40.4 us
  starting transfers between devices: 23.5 us -> 19.8 us
  other arithmetic: 5.51 us -> 2.94 us
    psum x1 -> x0, waiting for transfers between devices: 142 us -> none  [per_device(): summed = lax.psum(grads, axes).astype(F32)]
    all_to_all x0 -> x2, blocking collectives: none -> 73.4 us  [over_chips(): return lax.all_to_all(value, axes, 0, 0, axis_index_groups=groups)]
    slice x5 -> x2, local copies, waits for them, and re-layouts: 9.51 us -> 2.17 us  [the longest x1 1.32 us: per_device(): packet[rows:]]
    pallas_call x1 -> x4, Pallas kernels: 32.7 us -> 38.7 us  [the longest x1 31.7 us: per_device(): pl.pallas_call(lambda *refs: step_kernel(*refs, scale_den=scale_den), in_...]
    concatenate x4 -> x0, other arithmetic: 4.69 us -> none  [the longest x1 1.87 us: per_device(): jnp.concatenate(blocks[:3], axis=1)]
    ppermute x8 -> x7, starting transfers between devices: 23.5 us -> 19.8 us  [permute(): return lax.ppermute(value, axes, pairs)]
    ppermute x8 -> x7, waiting for transfers between devices: 10.4 us -> 10.5 us  [permute(): return lax.ppermute(value, axes, pairs)]
  transfers between devices with their start and end apart: 9 -> 7, of which waited for: 3 -> 2; matrix products, arithmetic and copies ran while one was open for 1% -> 2% of each run, Pallas kernels for 1% -> 1%
where the time goes in v2:
time: 162 us; the launch traced here: 161 us
  blocking collectives  73.4 us (45%)
  Pallas kernels  40.4 us (25%)
  starting transfers between devices  19.8 us (12%)
  local copies, waits for them, and re-layouts  12.8 us (8%)
  waiting for transfers between devices  10.5 us (6%)
  other arithmetic  2.94 us (2%)
    all_to_all x2, blocking collectives, over_chips(): return lax.all_to_all(value, axes, 0, 0, axis_index_groups=groups)  73.4 us
    pallas_call x1, Pallas kernels, per_device(): pl.pallas_call(lambda *refs: step_kernel(*refs, scale_den=scale_den), in_...  31.7 us
    ppermute x7, starting transfers between devices, permute(): return lax.ppermute(value, axes, pairs)  19.8 us
    ppermute x7, waiting for transfers between devices, permute(): return lax.ppermute(value, axes, pairs)  10.5 us
    unnamed x37, local copies, waits for them, and re-layouts  9.35 us
    pallas_call x1, Pallas kernels, per_device(): pl.pallas_call(unpack_kernel, in_specs=[smem, hbm, hbm, vmem, vmem, hbm,...  4.99 us
  transfers between devices with their start and end apart: 7, of which 2 were waited for; matrix products, arithmetic and copies ran while one was open for 2% of the time, Pallas kernels for 1%

profile of v2, /device:TPU:1, one launch (start us, length us, event | category | flops | bytes accessed | tf_op | source)
XLA Modules:
  0.0 161.3 jit_solution(15055491788511542725)
XLA Ops:
  1.3 0.7 pad_add_fusion.refs_0_.place
  2.0 1.6 %pack.1 = (bf16[144,512]{1,0:T(8,128)(2,1)}, bf16[80,512]{1,0:T(8,128)(2,1)}) custom-call(s32[4]{0:T(128)} %pad_add_fusion.refs_0_.place, bf16[128,512]{1,0:T(8,128)(2,1)} %refs_1_.5, s32[16,128]{1,0:T(8,128)} %refs_2_.2, f32[16,128]{1,0:T(8,128)} %refs_3_.2, f32[1,32]{1,0:T(1,128)} %refs_4_.2), custom_call_target="tpu_custom_call" | custom-call | tf_op jit(solution)/shard_map/pack/pallas_call | solution.py:606
  3.6 2.6 %collective-permute-start.1 = (bf16[144,512]{1,0:T(8,128)(2,1)}, bf16[144,512]{1,0:T(8,128)(2,1)S(1)}, u32[]{:S(2)}, u32[]{:S(2)}) collective-permute-start(bf16[144,512]{1,0:T(8,128)(2,1)} %get-tuple-element.31), channel_id=1, source_target_pairs={{0,63},{1,2},{2,1},{3,4},{4,3},{5,6},{6,5},{7,8},{8,7},{9,10},{10,... | collective-permute-start | bytes 442376 | tf_op jit(solution)/shard_map/ppermute | solution.py:603
  6.2 5.8 %collective-permute-start = (bf16[144,512]{1,0:T(8,128)(2,1)}, bf16[144,512]{1,0:T(8,128)(2,1)S(1)}, u32[]{:S(2)}, u32[]{:S(2)}) collective-permute-start(bf16[144,512]{1,0:T(8,128)(2,1)} %get-tuple-element.31), channel_id=1, source_target_pairs={{0,1},{1,0},{2,3},{3,2},{4,5},{5,4},{6,7},{7,6},{8,9},{9,8},{10,11... | collective-permute-start | bytes 442376 | tf_op jit(solution)/shard_map/ppermute | solution.py:603
  12.0 0.0 collective-permute-start.2
  12.0 0.8 slice.10
  12.8 6.3 %collective-permute-start.3 = (bf16[64,512]{1,0:T(8,128)(2,1)S(1)}, bf16[64,512]{1,0:T(8,128)(2,1)S(1)}, u32[]{:S(2)}, u32[]{:S(2)}) collective-permute-start(bf16[64,512]{1,0:T(8,128)(2,1)S(1)} %slice.10), channel_id=1, source_target_pairs={{0,62},{1,63},{2,0},{3,1},{4,2},{5,3},{6,4},{7,5},{8,6},{9,7},{10,... | collective-permute-start | bytes 196616 | tf_op jit(solution)/shard_map/ppermute | solution.py:603
  19.1 1.3 slice.9.refs_2_
  20.5 1.3 copy.29.refs_7_.noise_own
  21.8 0.0 copy-start
  21.8 1.2 copy-done
  23.0 0.0 copy-start.1
  23.0 1.0 copy-done.1
  24.1 0.0 copy-start.4
  24.1 0.7 copy-done.4
  24.8 0.0 copy-start.5
  24.8 0.7 copy-done.5
  25.5 0.0 copy-start.7
  25.5 0.7 copy-done.7
  26.2 1.7 %prepare.1 = (bf16[512,512]{1,0:T(8,128)(2,1)S(1)}, bf16[512,512]{1,0:T(8,128)(2,1)S(1)}, bf16[512,512]{1,0:T(8,128)(2,1)S(1)}, f32[256,512]{1,0:T(8,128)S(1)}) custom-call(s32[4]{0:T(128)S(1)} %copy-done.7, bf16[1024,512]{1,0:T(8,128)(2,1)S(1)} %copy-done, s32[3,1024]{1,0:T(4,128)S(1)} %copy-done.4, f32[3,1024]{1,0:T(4,128)S(1)} %copy-done.5, ...), custom_call_target="tpu_custom_call" | custom-call | flops 268435456 | bytes 3145728 | tf_op jit(solution)/shard_map/prepare/pallas_call | solution.py:623
  27.9 0.0 copy-start.9
  27.9 0.8 copy-done.9
  28.7 0.0 copy-start.10
  28.7 0.8 copy-done.10
  29.4 0.0 copy-start.11
  29.4 0.8 copy-done.11
  30.2 0.0 copy-start.12
  30.2 0.8 copy-done.12
  31.0 0.0 collective-permute-done.3.refs_6_
  31.0 0.0 copy-start.17
  31.0 0.0 collective-permute-done.2.refs_5_
  31.0 0.0 copy-start.16
  31.1 0.0 collective-permute-done.1.refs_4_
  31.1 0.0 copy-start.14
  31.1 0.0 collective-permute-done.refs_3_
  31.1 0.0 copy-start.15
  31.1 0.6 copy-done.17
  31.7 0.0 copy-done.16
  31.7 0.1 copy-done.14
  31.7 0.0 copy-done.15
  31.8 31.7 %step.1 = (f32[84,512]{1,0:T(8,128)}, f32[84,512]{1,0:T(8,128)}, bf16[64,144,128]{2,1,0:T(8,128)(2,1)}, bf16[64,144,128]{2,1,0:T(8,128)(2,1)}, f32[32,1]{1,0:T(8,128)}) custom-call(s32[4]{0:T(128)} %pad_add_fusion.refs_0_.place, bf16[128,512]{1,0:T(8,128)(2,1)} %refs_1_.5, bf16[16,512]{1,0:T(8,128)(2,1)} %slice.9.refs_2_, bf16[144,512]{1,0:T(8,128)(2,1)} %copy-done.15, ...), custom_call_target="tpu_custom_call" | custom-call | flops 10000000000 | bytes 12582912 | tf_op jit(solution)/shard_map/step/pallas_call | solution.py:672
  63.5 0.9 collective-permute-start.4
  64.3 4.4 %collective-permute-done.4 = bf16[64,144,128]{2,1,0:T(8,128)(2,1)S(1)} collective-permute-done((bf16[64,144,128]{2,1,0:T(8,128)(2,1)}, bf16[64,144,128]{2,1,0:T(8,128)(2,1)S(1)}, u32[]{:S(2)}, u32[]{:S(2)}) %collective-permute-start.4) | collective-permute-done | bytes 2359328 | tf_op jit(solution)/shard_map/ppermute | solution.py:603
  68.7 2.3 %add_convert_fusion = bf16[64,144,128]{2,1,0:T(8,128)(2,1)S(1)} fusion(bf16[64,144,128]{2,1,0:T(8,128)(2,1)S(1)} %collective-permute-done.4, bf16[64,144,128]{2,1,0:T(8,128)(2,1)} %get-tuple-element.37), kind=kLoop, calls=%fused_computation | loop fusion | flops 4718592 | bytes 7077888 | tf_op jit(solution)/shard_map/convert_element_type | solution.py:741
  71.0 35.5 %all_to_all.10.parts = bf16[64,144,128]{2,1,0:T(8,128)(2,1)S(1)} all-to-all(bf16[64,144,128]{2,1,0:T(8,128)(2,1)S(1)} %add_convert_fusion), channel_id=1, replica_groups={{0,2,4,6,8,10,12,14,16,18,20,22,24,26,28,30,32,34,36,38,40,42,44,46,48,..., dimensions={0} | all-to-all | bytes 4718592 | tf_op jit(solution)/shard_map/all_to_all | solution.py:738
  106.5 0.4 sum.1
  106.9 0.0 copy-start.13
  106.9 0.0 copy-start.2
  106.9 0.0 copy-start.3
  106.9 0.0 copy-start.6
  107.0 0.0 copy-start.8
  107.0 37.8 %all_to_all.11.mine_hbm = bf16[64,144,128]{2,1,0:T(8,128)(2,1)S(1)} all-to-all(bf16[64,144,128]{2,1,0:T(8,128)(2,1)S(1)} %sum.1), channel_id=1, replica_groups={{0,2,4,6,8,10,12,14,16,18,20,22,24,26,28,30,32,34,36,38,40,42,44,46,48,..., dimensions={0} | all-to-all | bytes 4718592 | tf_op jit(solution)/shard_map/all_to_all | solution.py:738
  144.8 2.7 %collective-permute-start.5 = (bf16[64,144,128]{2,1,0:T(8,128)(2,1)S(1)}, bf16[64,144,128]{2,1,0:T(8,128)(2,1)S(1)}, u32[]{:S(2)}, u32[]{:S(2)}) collective-permute-start(bf16[64,144,128]{2,1,0:T(8,128)(2,1)S(1)} %all_to_all.11.mine_hbm), channel_id=1, source_target_pairs={{0,1},{1,0},{2,3},{3,2},{4,5},{5,4},{6,7},{7,6},{8,9},{9,8},{10,11... | collective-permute-start | bytes 7077896 | tf_op jit(solution)/shard_map/ppermute | solution.py:603
  147.5 0.0 copy-done.13
  147.5 1.6 collective-permute-start.6
  149.1 6.1 %collective-permute-done.6.pred_arrived_hbm = f32[84,512]{1,0:T(8,128)S(1)} collective-permute-done((f32[84,512]{1,0:T(8,128)S(1)}, f32[84,512]{1,0:T(8,128)S(1)}, u32[]{:S(2)}, u32[]{:S(2)}) %collective-permute-start.6) | collective-permute-done | bytes 172064 | tf_op jit(solution)/shard_map/ppermute | solution.py:603
  155.2 0.0 collective-permute-done.5.theirs_hbm
  155.2 0.0 copy-done.2
  155.2 0.0 copy-done.3
  155.2 0.0 copy-done.6
  155.2 0.0 copy-done.8
  155.2 5.0 %unpack.1 = (f32[1,84,1024]{2,1,0:T(8,128)S(1)}, f32[32,512]{1,0:T(8,128)}, f32[32,512]{1,0:T(8,128)}, f32[512,1536]{1,0:T(8,128)}, f32[512,512]{1,0:T(8,128)}, ...) custom-call(s32[4]{0:T(128)S(1)} %copy-done.8, ...), custom_call_target="tpu_custom_call" | custom-call | tf_op jit(solution)/shard_map/unpack/pallas_call | solution.py:767
  160.2 1.1 copy.31
Async XLA Ops:
  3.6 27.5 %collective-permute-start.1 = (bf16[144,512]{1,0:T(8,128)(2,1)}, bf16[144,512]{1,0:T(8,128)(2,1)S(1)}, u32[]{:S(2)}, u32[]{:S(2)}) collective-permute-start(bf16[144,512]{1,0:T(8,128)(2,1)} %get-tuple-element.31), channel_id=1, source_target_pairs={{0,63},{1,2},{2,1},{3,4},{4,3},{5,6},{6,5},{7,8},{8,7},{9,10},{10,... | collective-permute-start | bytes 442376 | tf_op jit(solution)/shard_map/ppermute | solution.py:603
  6.2 24.9 %collective-permute-start = (bf16[144,512]{1,0:T(8,128)(2,1)}, bf16[144,512]{1,0:T(8,128)(2,1)S(1)}, u32[]{:S(2)}, u32[]{:S(2)}) collective-permute-start(bf16[144,512]{1,0:T(8,128)(2,1)} %get-tuple-element.31), channel_id=1, source_target_pairs={{0,1},{1,0},{2,3},{3,2},{4,5},{5,4},{6,7},{7,6},{8,9},{9,8},{10,11... | collective-permute-start | bytes 442376 | tf_op jit(solution)/shard_map/ppermute | solution.py:603
  12.0 19.1 %collective-permute-start.2 = (bf16[80,512]{1,0:T(8,128)(2,1)}, bf16[80,512]{1,0:T(8,128)(2,1)S(1)}, u32[]{:S(2)}, u32[]{:S(2)}) collective-permute-start(bf16[80,512]{1,0:T(8,128)(2,1)} %get-tuple-element.32), channel_id=1, source_target_pairs={{0,66},{1,67},{2,68},{3,69},{4,70},{5,71},{6,72},{7,73},{8,74},{9,... | collective-permute-start | bytes 245768 | tf_op jit(solution)/shard_map/ppermute | solution.py:603
  12.8 18.2 %collective-permute-start.3 = (bf16[64,512]{1,0:T(8,128)(2,1)S(1)}, bf16[64,512]{1,0:T(8,128)(2,1)S(1)}, u32[]{:S(2)}, u32[]{:S(2)}) collective-permute-start(bf16[64,512]{1,0:T(8,128)(2,1)S(1)} %slice.10), channel_id=1, source_target_pairs={{0,62},{1,63},{2,0},{3,1},{4,2},{5,3},{6,4},{7,5},{8,6},{9,7},{10,... | collective-permute-start | bytes 196616 | tf_op jit(solution)/shard_map/ppermute | solution.py:603
  21.8 1.2 copy-start
  23.0 1.0 copy-start.1
  24.1 0.7 copy-start.4
  24.8 0.7 copy-start.5
  25.5 0.7 copy-start.7
  27.9 0.8 copy-start.9
  28.7 0.8 copy-start.10
  29.4 0.8 copy-start.11
  30.2 0.8 copy-start.12
  31.0 0.6 copy-start.17
  31.0 0.6 copy-start.16
  31.1 0.7 copy-start.14
  31.1 0.7 copy-start.15
  63.5 5.2 %collective-permute-start.4 = (bf16[64,144,128]{2,1,0:T(8,128)(2,1)}, bf16[64,144,128]{2,1,0:T(8,128)(2,1)S(1)}, u32[]{:S(2)}, u32[]{:S(2)}) collective-permute-start(bf16[64,144,128]{2,1,0:T(8,128)(2,1)} %get-tuple-element.38), channel_id=1, source_target_pairs={{0,1},{1,0},{2,3},{3,2},{4,5},{5,4},{6,7},{7,6},{8,9},{9,8},{10,11... | collective-permute-start | bytes 7077896 | tf_op jit(solution)/shard_map/ppermute | solution.py:603
  106.9 40.6 %copy-start.13 = (f32[84,512]{1,0:T(8,128)S(1)}, f32[84,512]{1,0:T(8,128)}, u32[]{:S(2)}) copy-start(f32[84,512]{1,0:T(8,128)} %get-tuple-element.41) | copy-start | bytes 516100
  106.9 48.3 %copy-start.2 = (f32[84,512]{1,0:T(8,128)S(1)}, f32[84,512]{1,0:T(8,128)}, u32[]{:S(2)}) copy-start(f32[84,512]{1,0:T(8,128)} %get-tuple-element.40.pred_own_hbm) | copy-start | bytes 516100
  106.9 48.3 %copy-start.3 = (f32[32,1]{1,0:T(8,128)S(1)}, f32[32,1]{1,0:T(8,128)}, u32[]{:S(2)}) copy-start(f32[32,1]{1,0:T(8,128)} %copy.29.refs_7_.noise_own) | copy-start | bytes 388
  106.9 48.3 %copy-start.6 = (f32[32,1]{1,0:T(8,128)S(1)}, f32[32,1]{1,0:T(8,128)}, u32[]{:S(2)}) copy-start(f32[32,1]{1,0:T(8,128)} %get-tuple-element.39.noise_other) | copy-start | bytes 388
  107.0 48.3 %copy-start.8 = (s32[4]{0:T(128)S(1)}, s32[4]{0:T(128)}, u32[]{:S(2)}) copy-start(s32[4]{0:T(128)} %pad_add_fusion.refs_0_.place) | copy-start | bytes 52
  144.8 10.4 %collective-permute-start.5 = (bf16[64,144,128]{2,1,0:T(8,128)(2,1)S(1)}, bf16[64,144,128]{2,1,0:T(8,128)(2,1)S(1)}, u32[]{:S(2)}, u32[]{:S(2)}) collective-permute-start(bf16[64,144,128]{2,1,0:T(8,128)(2,1)S(1)} %all_to_all.11.mine_hbm), channel_id=1, source_target_pairs={{0,1},{1,0},{2,3},{3,2},{4,5},{5,4},{6,7},{7,6},{8,9},{9,8},{10,11... | collective-permute-start | bytes 7077896 | tf_op jit(solution)/shard_map/ppermute | solution.py:603
  147.5 7.7 %collective-permute-start.6 = (f32[84,512]{1,0:T(8,128)S(1)}, f32[84,512]{1,0:T(8,128)S(1)}, u32[]{:S(2)}, u32[]{:S(2)}) collective-permute-start(f32[84,512]{1,0:T(8,128)S(1)} %copy-done.13), channel_id=1, source_target_pairs={{0,64},{1,65},{2,66},{3,67},{4,68},{5,69},{6,70},{7,71},{8,72},{9,... | collective-permute-start | bytes 516104 | tf_op jit(solution)/shard_map/ppermute | solution.py:603

commit v3 on v2

--- a/solution.py
+++ b/solution.py
@@ -12,6 +12,7 @@
 LOSS_SCALE = 65536.0
 SMOOTHING = 0.0625
 FAR = -1e30
+ALL_VMEM = 62 * 2**20
 
 F32 = jnp.float32
 BF16 = jnp.bfloat16
@@ -78,11 +79,16 @@
     return high.astype(F32) + (middle.astype(F32) + low.astype(F32))
 
 
-def pack_kernel(place, latent, nbrs, bias, noise, packet, upward, *, total):
+def window_start(rows):
+    return lax.axis_index("space") * rows - rows // 2
+
+
+def pack_kernel(latent, nbrs, bias, noise, packet, upward, downward, *, total):
     rows = latent.shape[0]
     halo = rows // 2
     packet[:rows] = latent[...]
-    slots = ((nbrs[...] - place[1]) & (total - 1)).astype(F32).astype(BF16)
+    downward[...] = latent[:halo]
+    slots = ((nbrs[...] - window_start(rows)) & (total - 1)).astype(F32).astype(BF16)
     packet[rows:] = jnp.concatenate([slots, *split_terms(bias[...])], axis=1)
     upward[:halo] = latent[halo:]
     spare = jnp.zeros((1, rows - noise.shape[1]), F32)
@@ -93,16 +99,48 @@
 
 
 def prepare_kernel(
-    place, embed, nbrs, bias, dec_query, embed_t, norm_t, query_t, logits, *, rows, halo, total
+    embed_hbm,
+    nbrs_hbm,
+    bias_hbm,
+    weight_hbm,
+    embed_t,
+    norm_t,
+    query_t,
+    logits,
+    embed,
+    nbrs,
+    bias,
+    dec_query,
+    sems,
+    *,
+    rows,
+    halo,
+    total,
 ):
+    slots = embed.shape[0]
+    here = pl.ds(pl.multiple_of(lax.axis_index("member") * slots, slots), slots)
+    copies = [
+        pltpu.make_async_copy(embed_hbm.at[here, :], embed, sems.at[0]),
+        pltpu.make_async_copy(nbrs_hbm.at[:, here], nbrs, sems.at[1]),
+        pltpu.make_async_copy(bias_hbm.at[:, here], bias, sems.at[2]),
+        pltpu.make_async_copy(weight_hbm, dec_query, sems.at[3]),
+    ]
+    for copy in copies:
+        copy.start()
+    copies[0].wait()
     values = embed[...].T
     embed_t[...] = values
     norm = normalize(values.astype(F32), 0)[0].astype(BF16)
     norm_t[...] = norm
+    copies[1].wait()
+    copies[2].wait()
+    local = (nbrs[...] - window_start(rows)) & (total - 1)
+    places = jnp.where(
+        local < halo, local + rows, jnp.where(local < halo + rows, local - halo, local)
+    )
+    logits[...] = spread_bias(places, bias[...], rows + 2 * halo)
+    copies[3].wait()
     query_t[...] = tn(dec_query[...], norm).astype(BF16)
-    local = (nbrs[...] - place[1]) & (total - 1)
-    slots = jnp.where(local < halo, local + rows, jnp.where(local < halo + rows, local - halo, local))
-    logits[...] = spread_bias(slots, bias[...], rows + 2 * halo)
 
 
 def window_order(values, rows, halo):
@@ -118,9 +156,8 @@
 
 
 def step_kernel(
-    place,
-    own,
-    edges,
+    counts,
+    packet,
     twin,
     beside,
     below,
@@ -186,16 +223,18 @@
     *,
     scale_den,
 ):
-    rows, dim = own.shape
-    halo = rows // 2
+    halo, dim = above.shape
+    rows = 2 * halo
     window = rows + 2 * halo
+    own = packet[:rows]
+    edges = packet[rows:]
     heads = dim // HEAD
     members = 2
     channels = weather.shape[0]
     slots = embed_t.shape[1]
     inv_sqrt = 1.0 / math.sqrt(HEAD)
-    member = place[0]
-    core = place[3]
+    member = lax.axis_index("member")
+    core = lax.rem(lax.axis_index("space"), 2)
     here = pl.ds(pl.multiple_of(member * slots, slots), slots)
 
     loads = {}
@@ -222,7 +261,7 @@
     odd = core == 1
     latent[0:halo] = below[:halo]
     latent[halo : halo + rows] = jnp.where(odd, twin[:rows], beside[:rows])
-    latent[halo + rows : halo + 2 * rows] = own[...]
+    latent[halo + rows : halo + 2 * rows] = own
     latent[halo + 2 * rows : halo + 3 * rows] = jnp.where(odd, beside[:rows], twin[:rows])
     latent[halo + 3 * rows :] = above[...]
     unit = normalize(latent[...].astype(F32), 1)[0]
@@ -234,7 +273,7 @@
     ends = jnp.where(
         jnp.concatenate([late] * 4, axis=1), twin[rows:].astype(F32), beside[rows:].astype(F32)
     )
-    lists = edges[...].astype(F32)
+    lists = edges.astype(F32)
 
     def listed(part):
         return [
@@ -249,9 +288,12 @@
     )
     noise_row = joined_terms(*(below[halo:, part * rows : (part + 1) * rows] for part in (0, 1, 2)))
     spread = cond_scale.shape[0]
-    noise_other = jnp.broadcast_to(noise_row[:1], (rows, rows)).T[:spread, :1]
-    noise = [noise_own[...], noise_other]
-    noise_out[...] = noise_other
+    own_row = jnp.concatenate([noise_own[...], jnp.zeros((1, rows - spread), F32)], axis=1)
+    noise = []
+    for m, row in enumerate((own_row, noise_row[:1])):
+        columns = jnp.broadcast_to(row, (rows, rows)).T[:spread]
+        noise_out[m] = columns
+        noise.append(columns[:, :1])
     is_before = lax.broadcasted_iota(jnp.int32, (window, rows), 1) < halo
 
     def split_ends(values):
@@ -319,8 +361,8 @@
 
     for name in ("weather", "target", "area", "norm"):
         loads[name].wait()
-    slot = lax.broadcasted_iota(jnp.int32, (1, slots), 1) + place[0] * slots
-    live = jnp.where(slot < place[2], 1.0, 0.0)
+    slot = lax.broadcasted_iota(jnp.int32, (1, slots), 1) + member * slots
+    live = jnp.where(slot < counts[0], 1.0, 0.0)
     weighting = live * area[...]
     first = weather[...] + live * change[0, :channels]
     second = weather[...] + live * change[1, :channels]
@@ -421,14 +463,14 @@
         g_gain = jnp.sum(weight * moment, axis=1, keepdims=True)
         g_shift = jnp.sum(weight * col_sum, axis=1, keepdims=True)
         mine = member if m == 0 else 1 - member
-        row_id = lax.broadcasted_iota(jnp.int32, (16, dim), 0)
-        term = jnp.where(row_id == mine, jnp.broadcast_to(g_gain, (dim, HEAD)).T[:16], 0.0)
-        term += jnp.where(row_id == mine + 2, jnp.broadcast_to(g_shift, (dim, HEAD)).T[:16], 0.0)
+        row_id = lax.broadcasted_iota(jnp.int32, (8, dim), 0)
+        term = jnp.where(row_id == mine, jnp.broadcast_to(g_gain, (dim, HEAD)).T[:8], 0.0)
+        term += jnp.where(row_id == mine + 2, jnp.broadcast_to(g_shift, (dim, HEAD)).T[:8], 0.0)
         grad_cond = term if m == 0 else grad_cond + term
 
-    row_id = lax.broadcasted_iota(jnp.int32, (16, dim), 0)
+    row_id = lax.broadcasted_iota(jnp.int32, (8, dim), 0)
     grad_cond += jnp.where(row_id == 4, loss, 0.0)
-    grads[:, :, HEAD:, :] = jnp.zeros((2, 64, 16, HEAD), BF16)
+    grads[:, :, HEAD:, :] = jnp.zeros((2, 64, 8, HEAD), BF16)
     blocks = (
         grad_qkv[:, :dim],
         grad_qkv[:, dim : 2 * dim],
@@ -448,10 +490,10 @@
                     c * tall : (c + 1) * tall, t * HEAD : (t + 1) * HEAD
                 ].astype(BF16)
     extras = jnp.concatenate([grad_head, grad_cond], axis=0)
-    for i in range(extras.shape[0] // 16):
+    for i in range(extras.shape[0] // 8):
         for t in range(heads):
             grads[0, i * heads + t, HEAD:, :] = extras[
-                i * 16 : (i + 1) * 16, t * HEAD : (t + 1) * HEAD
+                i * 8 : (i + 1) * 8, t * HEAD : (t + 1) * HEAD
             ].astype(BF16)
     keep = pltpu.make_async_copy(grads.at[core], keep_hbm, store_sems.at[2])
     send = pltpu.make_async_copy(grads.at[1 - core], send_hbm, store_sems.at[3])
@@ -462,20 +504,27 @@
         store.wait()
 
 
-def sum_kernel(parts, result):
+def sum_kernel(parts, pred_own_hbm, pred_arrived_hbm, result, pred_hbm, sems):
+    slots = pred_own_hbm.shape[1]
+    member = lax.axis_index("member")
+    here = pl.ds(pl.multiple_of(member * slots, slots), slots)
+    there = pl.ds(pl.multiple_of((1 - member) * slots, slots), slots)
+    copies = [
+        pltpu.make_async_copy(pred_own_hbm, pred_hbm.at[0, :, here], sems.at[0]),
+        pltpu.make_async_copy(pred_arrived_hbm, pred_hbm.at[0, :, there], sems.at[1]),
+    ]
+    for copy in copies:
+        copy.start()
     total = jnp.sum(parts[...].astype(F32), axis=0, keepdims=True)
     result[...] = jnp.broadcast_to(total.astype(BF16), result.shape)
+    for copy in copies:
+        copy.wait()
 
 
 def unpack_kernel(
-    place,
     mine_hbm,
     theirs_hbm,
-    noise_own,
-    noise_other,
-    pred_own_hbm,
-    pred_arrived_hbm,
-    pred_hbm,
+    noise,
     grad_scale,
     grad_shift,
     grad_qkv,
@@ -488,23 +537,19 @@
     grads,
     sems,
 ):
-    member = place[0]
-    core = place[3]
-    channels, slots = pred_own_hbm.shape
+    member = lax.axis_index("member")
+    core = lax.rem(lax.axis_index("space"), 2)
+    channels = grad_head.shape[0]
     dim = grad_attn_out.shape[0]
     heads = dim // HEAD
-    here = pl.ds(pl.multiple_of(member * slots, slots), slots)
-    there = pl.ds(pl.multiple_of((1 - member) * slots, slots), slots)
     copies = [
         pltpu.make_async_copy(mine_hbm, grads.at[core], sems.at[0]),
         pltpu.make_async_copy(theirs_hbm, grads.at[1 - core], sems.at[1]),
-        pltpu.make_async_copy(pred_own_hbm, pred_hbm.at[0, :, here], sems.at[2]),
-        pltpu.make_async_copy(pred_arrived_hbm, pred_hbm.at[0, :, there], sems.at[3]),
     ]
     for copy in copies:
         copy.start()
-    copies[0].wait()
-    copies[1].wait()
+    for copy in copies:
+        copy.wait()
     tall = HEAD * HEAD // dim
     targets = (
         (grad_qkv, 0),
@@ -529,24 +574,21 @@
             [grads[0, i * heads + t, HEAD:, :].astype(F32) for t in range(heads)], axis=1
         )
 
-    head_blocks = -(-channels // 16)
-    for i in range(head_blocks):
-        count = min(16, channels - i * 16)
-        grad_head[i * 16 : i * 16 + count] = extra(i)[:count]
-    cond = extra(2 * (-(-channels // 32)))
+    for i in range(-(-channels // 8)):
+        count = min(8, channels - i * 8)
+        grad_head[i * 8 : i * 8 + count] = extra(i)[:count]
+    cond = extra(4 * (-(-channels // 32)))
     first = cond[0:1]
     second = cond[1:2]
-    grad_scale[...] = noise_own[...] * jnp.where(member == 0, first, second) + noise_other[
-        ...
+    grad_scale[...] = noise[0, :, :1] * jnp.where(member == 0, first, second) + noise[
+        1, :, :1
     ] * jnp.where(member == 0, second, first)
     first = cond[2:3]
     second = cond[3:4]
-    grad_shift[...] = noise_own[...] * jnp.where(member == 0, first, second) + noise_other[
-        ...
+    grad_shift[...] = noise[0, :, :1] * jnp.where(member == 0, first, second) + noise[
+        1, :, :1
     ] * jnp.where(member == 0, second, first)
     loss[...] = cond[4:5, :HEAD]
-    copies[2].wait()
-    copies[3].wait()
 
 
 def whole(shape):
@@ -588,10 +630,6 @@
     entries = grid_nbrs.shape[0]
     scale_den = 2.0 * channels * grid_slots * size
 
-    member = lax.axis_index("member")
-    space = lax.axis_index("space")
-    start = space * rows - halo
-    place = jnp.stack([member, start, grid_counts[0], space % 2]).astype(jnp.int32)
     axes = ("member", "space")
 
     def permute(value, target_of):
@@ -603,57 +641,59 @@
         return lax.ppermute(value, axes, pairs)
 
     smem = pl.BlockSpec(memory_space=pltpu.SMEM)
-    packet, upward = pl.pallas_call(
+    vmem = pl.BlockSpec(memory_space=pltpu.VMEM)
+    hbm = pl.BlockSpec(memory_space=pltpu.HBM)
+    packet, upward, downward = pl.pallas_call(
         lambda *refs: pack_kernel(*refs, total=total),
-        in_specs=[smem] + [pl.BlockSpec(memory_space=pltpu.VMEM)] * 4,
+        in_specs=[vmem] * 4,
         out_shape=[
             jax.ShapeDtypeStruct((rows + mesh_nbrs.shape[0], dim), BF16),
             jax.ShapeDtypeStruct((halo + 16, dim), BF16),
+            jax.ShapeDtypeStruct((halo, dim), BF16),
         ],
+        compiler_params=pltpu.CompilerParams(vmem_limit_bytes=ALL_VMEM),
         name="pack",
-    )(place, mesh_latent, mesh_nbrs, mesh_bias, member_noise)
+    )(mesh_latent, mesh_nbrs, mesh_bias, member_noise)
     beside = permute(packet, lambda m, k: (m, k + 1 if k % 2 else k - 1))
     below = permute(upward, lambda m, k: (1 - m, k + 2))
-    above = permute(mesh_latent[:halo], lambda m, k: (m, k - 2))
+    above = permute(downward, lambda m, k: (m, k - 2))
     twin = permute(packet, lambda m, k: (m, k ^ 1))
 
-    part = pl.BlockSpec((slots, dim), lambda i, place: (place[0], 0))
-    lists = pl.BlockSpec((entries, slots), lambda i, place: (0, place[0]))
     square = (dim, slots)
     embed_t, norm_t, query_t, grid_logits = pl.pallas_call(
         lambda *refs: prepare_kernel(*refs, rows=rows, halo=halo, total=total),
-        grid_spec=pltpu.PrefetchScalarGridSpec(
-            num_scalar_prefetch=1,
-            grid=(1,),
-            in_specs=[part, lists, lists, whole((dim, dim))],
-            out_specs=[whole(square), whole(square), whole(square), whole((window, slots))],
-        ),
+        in_specs=[hbm] * 4,
+        out_specs=[vmem] * 4,
         out_shape=[
             jax.ShapeDtypeStruct(square, BF16),
             jax.ShapeDtypeStruct(square, BF16),
             jax.ShapeDtypeStruct(square, BF16),
             jax.ShapeDtypeStruct((window, slots), F32),
         ],
-        compiler_params=pltpu.CompilerParams(vmem_limit_bytes=40 * 2**20),
+        scratch_shapes=[
+            pltpu.VMEM((slots, dim), BF16),
+            pltpu.VMEM((entries, slots), jnp.int32),
+            pltpu.VMEM((entries, slots), F32),
+            pltpu.VMEM((dim, dim), BF16),
+            pltpu.SemaphoreType.DMA((4,)),
+        ],
+        compiler_params=pltpu.CompilerParams(vmem_limit_bytes=ALL_VMEM),
         cost_estimate=pl.CostEstimate(
             flops=2 * dim * dim * slots, bytes_accessed=3 * 2**20, transcendentals=0
         ),
         name="prepare",
-    )(place, grid_embed, grid_nbrs, grid_bias, dec_query)
+    )(grid_embed, grid_nbrs, grid_bias, dec_query)
 
     channel_pad = -(-channels // 32) * 32
     chunks = size
-    half_shape = (chunks, HEAD + 16, HEAD)
-    hbm = pl.BlockSpec(memory_space=pl.ANY)
-    vmem = pl.BlockSpec(memory_space=pltpu.VMEM)
+    half_shape = (chunks, HEAD + 8, HEAD)
     step_in = (
-        mesh_latent,
-        packet[rows:],
+        packet,
         twin,
         beside,
         below,
         above,
-        member_noise.reshape(noise_size, 1),
+        member_noise,
         embed_t,
         norm_t,
         query_t,
@@ -669,9 +709,9 @@
         dec_out,
         head_out,
     )
-    pred_own, pred_other, keep, send, other_noise = pl.pallas_call(
+    pred_own, pred_other, keep, send, noise = pl.pallas_call(
         lambda *refs: step_kernel(*refs, scale_den=scale_den),
-        in_specs=[smem] + [vmem] * 7 + [hbm] * 14,
+        in_specs=[smem] + [vmem] * 6 + [pl.BlockSpec(memory_space=pl.ANY)] * 4 + [hbm] * 10,
         out_specs=[hbm] * 4 + [vmem],
         scratch_shapes=[
             pltpu.VMEM(square, BF16),
@@ -718,14 +758,14 @@
             jax.ShapeDtypeStruct((channels, slots), F32),
             jax.ShapeDtypeStruct(half_shape, BF16),
             jax.ShapeDtypeStruct(half_shape, BF16),
-            jax.ShapeDtypeStruct((noise_size, 1), F32),
+            jax.ShapeDtypeStruct((2, noise_size, rows), F32),
         ],
-        compiler_params=pltpu.CompilerParams(vmem_limit_bytes=56 * 2**20),
+        compiler_params=pltpu.CompilerParams(vmem_limit_bytes=ALL_VMEM),
         cost_estimate=pl.CostEstimate(
             flops=10**10, bytes_accessed=12 * 2**20, transcendentals=2**21
         ),
         name="step",
-    )(place, *step_in)
+    )(grid_counts, *step_in)
 
     def twin_swap(value):
         return permute(value, lambda m, k: (m, k ^ 1))
@@ -739,15 +779,20 @@
 
     arrived_pred = permute(pred_other, lambda m, k: (1 - m, k))
     pair = (keep.astype(F32) + twin_swap(send).astype(F32)).astype(BF16)
+    pair, arrived_pred = lax.optimization_barrier((pair, arrived_pred))
     parts = over_chips(pair)
-    shared = pl.pallas_call(
+    shared, prediction = pl.pallas_call(
         sum_kernel,
-        in_specs=[vmem],
-        out_specs=vmem,
-        out_shape=jax.ShapeDtypeStruct(half_shape, BF16),
+        in_specs=[vmem, hbm, hbm],
+        out_specs=[vmem, hbm],
+        out_shape=[
+            jax.ShapeDtypeStruct(half_shape, BF16),
+            jax.ShapeDtypeStruct((1, channels, grid_slots), F32),
+        ],
+        scratch_shapes=[pltpu.SemaphoreType.DMA((2,))],
         compiler_params=pltpu.CompilerParams(vmem_limit_bytes=32 * 2**20),
         name="sum",
-    )(parts)
+    )(parts, pred_own, arrived_pred)
     mine = over_chips(shared)
     theirs = twin_swap(mine)
     grad_shapes = [
@@ -766,14 +811,14 @@
     ]
     outputs = pl.pallas_call(
         unpack_kernel,
-        in_specs=[smem, hbm, hbm, vmem, vmem, hbm, hbm],
-        out_specs=[hbm] + [vmem] * 9,
-        out_shape=[jax.ShapeDtypeStruct((1, channels, grid_slots), F32)] + grad_shapes,
-        scratch_shapes=[pltpu.VMEM((2, *half_shape), BF16), pltpu.SemaphoreType.DMA((4,))],
+        in_specs=[pl.BlockSpec(memory_space=pl.ANY)] * 2 + [vmem],
+        out_specs=[vmem] * 9,
+        out_shape=grad_shapes,
+        scratch_shapes=[pltpu.VMEM((2, *half_shape), BF16), pltpu.SemaphoreType.DMA((2,))],
         compiler_params=pltpu.CompilerParams(vmem_limit_bytes=40 * 2**20),
         name="unpack",
-    )(place, mine, theirs, step_in[6], other_noise, pred_own, arrived_pred)
-    return (*outputs[:9], outputs[9][0, 0])
+    )(mine, theirs, noise)
+    return (prediction, *outputs[:8], outputs[8][0, 0])
 
 
 def solution(mesh):

time: 162 us -> 148 us (0.914)
  local copies, waits for them, and re-layouts: 12.8 us -> 1.79 us
  waiting for transfers between devices: 10.5 us -> 6.78 us
    unnamed x37 -> x13, local copies, waits for them, and re-layouts: 9.35 us -> 1.79 us
    ppermute x7, waiting for transfers between devices: 10.5 us -> 6.78 us  [permute(): return lax.ppermute(value, axes, pairs)]
    slice x2 -> x0, local copies, waits for them, and re-layouts: 2.17 us -> none  [the longest x1 1.32 us: per_device(): packet[rows:]]
  transfers between devices with their start and end apart: 7 -> 7, of which waited for: 2 -> 3; matrix products, arithmetic and copies ran while one was open for 2% -> 2% of each run, Pallas kernels for 1% -> 2%
where the time goes in v3:
time: 148 us
  blocking collectives  74.5 us (50%)
  Pallas kernels  40.9 us (28%)
  starting transfers between devices  19.8 us (13%)
  waiting for transfers between devices  6.78 us (5%)
  other arithmetic  2.2 us (1%)
  local copies, waits for them, and re-layouts  1.79 us (1%)
  between operations  1.59 us (1%)
    all_to_all x2, blocking collectives, over_chips(): return lax.all_to_all(value, axes, 0, 0, axis_index_groups=groups)  74.5 us
    pallas_call x1, Pallas kernels, per_device(): pl.pallas_call(lambda *refs: step_kernel(*refs, scale_den=scale_den), in_...  31.5 us
    ppermute x7, starting transfers between devices, permute(): return lax.ppermute(value, axes, pairs)  19.8 us
    ppermute x7, waiting for transfers between devices, permute(): return lax.ppermute(value, axes, pairs)  6.78 us
    pallas_call x1, Pallas kernels, per_device(): pl.pallas_call(unpack_kernel, in_specs=[pl.BlockSpec(memory_space=pl.ANY)...  4.16 us
    pallas_call x1, Pallas kernels, per_device(): pl.pallas_call(lambda *refs: prepare_kernel(*refs, rows=rows, halo=halo,...  3.08 us
  transfers between devices with their start and end apart: 7, of which 3 were waited for; matrix products, arithmetic and copies ran while one was open for 2% of the time, Pallas kernels for 2%

profile of v3, /device:TPU:1, one launch (start us, length us, event | category | flops | bytes accessed | tf_op | source)
XLA Modules:
  0.0 147.5 jit_solution(14510549139949178458)
XLA Ops:
  0.6 1.7 %pack.1 = (bf16[144,512]{1,0:T(8,128)(2,1)}, bf16[80,512]{1,0:T(8,128)(2,1)}, bf16[64,512]{1,0:T(8,128)(2,1)}) custom-call(bf16[128,512]{1,0:T(8,128)(2,1)} %refs_0_.3, s32[16,128]{1,0:T(8,128)} %refs_1_.2, f32[16,128]{1,0:T(8,128)} %refs_2_.2, f32[1,32]{1,0:T(1,128)} %refs_6_.1), custom_call_target="tpu_custom_call" | custom-call | tf_op jit(solution)/shard_map/pack/pallas_call | solution.py:646
  2.3 2.6 %collective-permute-start.1 = (bf16[144,512]{1,0:T(8,128)(2,1)}, bf16[144,512]{1,0:T(8,128)(2,1)S(1)}, u32[]{:S(2)}, u32[]{:S(2)}) collective-permute-start(bf16[144,512]{1,0:T(8,128)(2,1)} %get-tuple-element.35.refs_1_), channel_id=1, source_target_pairs={{0,63},{1,2},{2,1},{3,4},{4,3},{5,6},{6,5},{7,8},{8,7},{9,10},{10,... | collective-permute-start | bytes 442376 | tf_op jit(solution)/shard_map/ppermute | solution.py:641
  4.9 5.8 %collective-permute-start = (bf16[144,512]{1,0:T(8,128)(2,1)}, bf16[144,512]{1,0:T(8,128)(2,1)S(1)}, u32[]{:S(2)}, u32[]{:S(2)}) collective-permute-start(bf16[144,512]{1,0:T(8,128)(2,1)} %get-tuple-element.35.refs_1_), channel_id=1, source_target_pairs={{0,1},{1,0},{2,3},{3,2},{4,5},{5,4},{6,7},{7,6},{8,9},{9,8},{10,11... | collective-permute-start | bytes 442376 | tf_op jit(solution)/shard_map/ppermute | solution.py:641
  10.7 0.0 collective-permute-start.2
  10.7 6.3 %collective-permute-start.3 = (bf16[64,512]{1,0:T(8,128)(2,1)}, bf16[64,512]{1,0:T(8,128)(2,1)S(1)}, u32[]{:S(2)}, u32[]{:S(2)}) collective-permute-start(bf16[64,512]{1,0:T(8,128)(2,1)} %get-tuple-element.37), channel_id=1, source_target_pairs={{0,62},{1,63},{2,0},{3,1},{4,2},{5,3},{6,4},{7,5},{8,6},{9,7},{10,... | collective-permute-start | bytes 196616 | tf_op jit(solution)/shard_map/ppermute | solution.py:641
  17.7 3.1 %prepare.1 = (bf16[512,512]{1,0:T(8,128)(2,1)}, bf16[512,512]{1,0:T(8,128)(2,1)}, bf16[512,512]{1,0:T(8,128)(2,1)}, f32[256,512]{1,0:T(8,128)}) custom-call(bf16[1024,512]{1,0:T(8,128)(2,1)} %refs_0_.4, s32[3,1024]{1,0:T(4,128)} %refs_1_.3, f32[3,1024]{1,0:T(4,128)} %refs_2_.3, bf16[512,512]{1,0:T(8,128)(2,1)} %refs_3_.3), custom_call_target="tpu_custom_call" | custom-call | flops 268435456 | bytes 3145728 | tf_op jit(solution)/shard_map/prepare/pallas_call | solution.py:663
  20.7 0.0 collective-permute-done.3.refs_5_
  20.8 0.0 copy-start.5
  20.8 0.0 collective-permute-done.2.refs_4_
  20.8 0.0 copy-start.4
  20.8 0.0 collective-permute-done.1.refs_3_
  20.8 0.0 copy-start.2
  20.8 0.0 collective-permute-done.refs_2_
  20.8 0.0 copy-start.3
  20.8 0.6 copy-done.5
  21.4 0.0 copy-done.4
  21.4 0.0 copy-done.2
  21.5 0.1 copy-done.3
  21.5 31.5 %step.1 = (f32[84,512]{1,0:T(8,128)}, f32[84,512]{1,0:T(8,128)}, bf16[64,136,128]{2,1,0:T(8,128)(2,1)}, bf16[64,136,128]{2,1,0:T(8,128)(2,1)}, f32[2,32,128]{2,1,0:T(8,128)}) custom-call(s32[1]{0:T(128)S(6)} %copy.30.refs_0_, bf16[144,512]{1,0:T(8,128)(2,1)} %get-tuple-element.35.refs_1_, bf16[144,512]{1,0:T(8,128)(2,1)} %copy-done.3, ...), custom_call_target="tpu_custom_call" | custom-call | flops 10000000000 | bytes 12582912 | tf_op jit(solution)/shard_map/step/pallas_call | solution.py:712
  53.1 0.9 collective-permute-start.4
  53.9 1.7 %collective-permute-start.5 = (f32[84,512]{1,0:T(8,128)}, f32[84,512]{1,0:T(8,128)S(1)}, u32[]{:S(2)}, u32[]{:S(2)}) collective-permute-start(f32[84,512]{1,0:T(8,128)} %get-tuple-element.44), channel_id=1, source_target_pairs={{0,64},{1,65},{2,66},{3,67},{4,68},{5,69},{6,70},{7,71},{8,72},{9,... | collective-permute-start | bytes 516104 | tf_op jit(solution)/shard_map/ppermute | solution.py:641
  55.7 2.5 %collective-permute-done.4 = bf16[64,136,128]{2,1,0:T(8,128)(2,1)S(1)} collective-permute-done((bf16[64,136,128]{2,1,0:T(8,128)(2,1)}, bf16[64,136,128]{2,1,0:T(8,128)(2,1)S(1)}, u32[]{:S(2)}, u32[]{:S(2)}) %collective-permute-start.4) | collective-permute-done | bytes 2228256 | tf_op jit(solution)/shard_map/ppermute | solution.py:641
  58.1 2.2 %add_convert_fusion = bf16[64,136,128]{2,1,0:T(8,128)(2,1)S(1)} fusion(bf16[64,136,128]{2,1,0:T(8,128)(2,1)S(1)} %collective-permute-done.4, bf16[64,136,128]{2,1,0:T(8,128)(2,1)} %get-tuple-element.42), kind=kLoop, calls=%fused_computation | loop fusion | flops 4456448 | bytes 6684672 | tf_op jit(solution)/shard_map/convert_element_type | solution.py:781
  60.3 0.0 copy-start
  60.3 1.4 collective-permute-done.5.pred_arrived_hbm
  61.8 37.3 %all_to_all.10.parts = bf16[64,136,128]{2,1,0:T(8,128)(2,1)S(1)} all-to-all(bf16[64,136,128]{2,1,0:T(8,128)(2,1)S(1)} %add_convert_fusion), channel_id=1, replica_groups={{0,2,4,6,8,10,12,14,16,18,20,22,24,26,28,30,32,34,36,38,40,42,44,46,48,..., dimensions={0} | all-to-all | bytes 4456448 | tf_op jit(solution)/shard_map/all_to_all | solution.py:778
  99.1 0.0 copy-done
  99.1 0.5 sum.1
  99.6 0.0 copy-start.1
  99.6 37.1 %all_to_all.11.mine_hbm = bf16[64,136,128]{2,1,0:T(8,128)(2,1)S(1)} all-to-all(bf16[64,136,128]{2,1,0:T(8,128)(2,1)S(1)} %get-tuple-element.49), channel_id=1, replica_groups={{0,2,4,6,8,10,12,14,16,18,20,22,24,26,28,30,32,34,36,38,40,42,44,46,48,..., dimensions={0} | all-to-all | bytes 4456448 | tf_op jit(solution)/shard_map/all_to_all | solution.py:778
  136.7 2.5 %collective-permute-start.6 = (bf16[64,136,128]{2,1,0:T(8,128)(2,1)S(1)}, bf16[64,136,128]{2,1,0:T(8,128)(2,1)S(1)}, u32[]{:S(2)}, u32[]{:S(2)}) collective-permute-start(bf16[64,136,128]{2,1,0:T(8,128)(2,1)S(1)} %all_to_all.11.mine_hbm), channel_id=1, source_target_pairs={{0,1},{1,0},{2,3},{3,2},{4,5},{5,4},{6,7},{7,6},{8,9},{9,8},{10,11... | collective-permute-start | bytes 6684680 | tf_op jit(solution)/shard_map/ppermute | solution.py:641
  139.2 1.1 copy.29
  140.3 2.9 %collective-permute-done.6.theirs_hbm = bf16[64,136,128]{2,1,0:T(8,128)(2,1)S(1)} collective-permute-done((bf16[64,136,128]{2,1,0:T(8,128)(2,1)S(1)}, bf16[64,136,128]{2,1,0:T(8,128)(2,1)S(1)}, u32[]{:S(2)}, u32[]{:S(2)}) %collective-permute-start.6) | collective-permute-done | bytes 2228256 | tf_op jit(solution)/shard_map/ppermute | solution.py:641
  143.2 0.0 copy-done.1
  143.2 4.2 %unpack.1 = (f32[32,512]{1,0:T(8,128)}, f32[32,512]{1,0:T(8,128)}, f32[512,1536]{1,0:T(8,128)}, f32[512,512]{1,0:T(8,128)}, f32[512,512]{1,0:T(8,128)}, /*index=...) custom-call(bf16[64,136,128]{2,1,0:T(8,128)(2,1)S(1)} %all_to_all.11.mine_hbm, ...), custom_call_target="tpu_custom_call" | custom-call | tf_op jit(solution)/shard_map/unpack/pallas_call | solution.py:812
Async XLA Ops:
  2.3 18.5 %collective-permute-start.1 = (bf16[144,512]{1,0:T(8,128)(2,1)}, bf16[144,512]{1,0:T(8,128)(2,1)S(1)}, u32[]{:S(2)}, u32[]{:S(2)}) collective-permute-start(bf16[144,512]{1,0:T(8,128)(2,1)} %get-tuple-element.35.refs_1_), channel_id=1, source_target_pairs={{0,63},{1,2},{2,1},{3,4},{4,3},{5,6},{6,5},{7,8},{8,7},{9,10},{10,... | collective-permute-start | bytes 442376 | tf_op jit(solution)/shard_map/ppermute | solution.py:641
  4.9 15.9 %collective-permute-start = (bf16[144,512]{1,0:T(8,128)(2,1)}, bf16[144,512]{1,0:T(8,128)(2,1)S(1)}, u32[]{:S(2)}, u32[]{:S(2)}) collective-permute-start(bf16[144,512]{1,0:T(8,128)(2,1)} %get-tuple-element.35.refs_1_), channel_id=1, source_target_pairs={{0,1},{1,0},{2,3},{3,2},{4,5},{5,4},{6,7},{7,6},{8,9},{9,8},{10,11... | collective-permute-start | bytes 442376 | tf_op jit(solution)/shard_map/ppermute | solution.py:641
  10.7 10.1 %collective-permute-start.2 = (bf16[80,512]{1,0:T(8,128)(2,1)}, bf16[80,512]{1,0:T(8,128)(2,1)S(1)}, u32[]{:S(2)}, u32[]{:S(2)}) collective-permute-start(bf16[80,512]{1,0:T(8,128)(2,1)} %get-tuple-element.36), channel_id=1, source_target_pairs={{0,66},{1,67},{2,68},{3,69},{4,70},{5,71},{6,72},{7,73},{8,74},{9,... | collective-permute-start | bytes 245768 | tf_op jit(solution)/shard_map/ppermute | solution.py:641
  10.7 10.1 %collective-permute-start.3 = (bf16[64,512]{1,0:T(8,128)(2,1)}, bf16[64,512]{1,0:T(8,128)(2,1)S(1)}, u32[]{:S(2)}, u32[]{:S(2)}) collective-permute-start(bf16[64,512]{1,0:T(8,128)(2,1)} %get-tuple-element.37), channel_id=1, source_target_pairs={{0,62},{1,63},{2,0},{3,1},{4,2},{5,3},{6,4},{7,5},{8,6},{9,7},{10,... | collective-permute-start | bytes 196616 | tf_op jit(solution)/shard_map/ppermute | solution.py:641
  20.8 0.6 copy-start.5
  20.8 0.6 copy-start.4
  20.8 0.7 copy-start.2
  20.8 0.7 copy-start.3
  53.1 5.0 %collective-permute-start.4 = (bf16[64,136,128]{2,1,0:T(8,128)(2,1)}, bf16[64,136,128]{2,1,0:T(8,128)(2,1)S(1)}, u32[]{:S(2)}, u32[]{:S(2)}) collective-permute-start(bf16[64,136,128]{2,1,0:T(8,128)(2,1)} %get-tuple-element.43), channel_id=1, source_target_pairs={{0,1},{1,0},{2,3},{3,2},{4,5},{5,4},{6,7},{7,6},{8,9},{9,8},{10,11... | collective-permute-start | bytes 6684680 | tf_op jit(solution)/shard_map/ppermute | solution.py:641
  53.9 7.8 %collective-permute-start.5 = (f32[84,512]{1,0:T(8,128)}, f32[84,512]{1,0:T(8,128)S(1)}, u32[]{:S(2)}, u32[]{:S(2)}) collective-permute-start(f32[84,512]{1,0:T(8,128)} %get-tuple-element.44), channel_id=1, source_target_pairs={{0,64},{1,65},{2,66},{3,67},{4,68},{5,69},{6,70},{7,71},{8,72},{9,... | collective-permute-start | bytes 516104 | tf_op jit(solution)/shard_map/ppermute | solution.py:641
  60.3 38.8 %copy-start = (f32[84,512]{1,0:T(8,128)S(1)}, f32[84,512]{1,0:T(8,128)}, u32[]{:S(2)}) copy-start(f32[84,512]{1,0:T(8,128)} %get-tuple-element.46.pred_own_hbm) | copy-start | bytes 516100
  99.6 43.6 %copy-start.1 = (f32[2,32,128]{2,1,0:T(8,128)S(1)}, f32[2,32,128]{2,1,0:T(8,128)}, u32[]{:S(2)}) copy-start(f32[2,32,128]{2,1,0:T(8,128)} %get-tuple-element.50.noise) | copy-start | bytes 98308
  136.7 6.5 %collective-permute-start.6 = (bf16[64,136,128]{2,1,0:T(8,128)(2,1)S(1)}, bf16[64,136,128]{2,1,0:T(8,128)(2,1)S(1)}, u32[]{:S(2)}, u32[]{:S(2)}) collective-permute-start(bf16[64,136,128]{2,1,0:T(8,128)(2,1)S(1)} %all_to_all.11.mine_hbm), channel_id=1, source_target_pairs={{0,1},{1,0},{2,3},{3,2},{4,5},{5,4},{6,7},{7,6},{8,9},{9,8},{10,11... | collective-permute-start | bytes 6684680 | tf_op jit(solution)/shard_map/ppermute | solution.py:641

commit v4 on v3

--- a/solution.py
+++ b/solution.py
@@ -12,6 +12,8 @@
 LOSS_SCALE = 65536.0
 SMOOTHING = 0.0625
 FAR = -1e30
+TILE = 256
+LOG2E = math.log2(math.e)
 ALL_VMEM = 62 * 2**20
 
 F32 = jnp.float32
@@ -52,19 +54,28 @@
         same = slots == slots[entry : entry + 1]
         top = jnp.max(jnp.where(same, bias, FAR), axis=0, keepdims=True)
         terms = jnp.sum(jnp.where(same, jnp.exp(bias - top), 0.0), axis=0, keepdims=True)
-        logits = jnp.where(row_ids == slots[entry : entry + 1], top + jnp.log(terms), logits)
+        logits = jnp.where(row_ids == slots[entry : entry + 1], (top + jnp.log(terms)) * LOG2E, logits)
     return logits
 
 
+def add_entry(slots, bias, entry, logits):
+    place = slots[pl.ds(entry, 1), :]
+    same = slots[...] == place
+    top = jnp.max(jnp.where(same, bias[...], FAR), axis=0, keepdims=True)
+    terms = jnp.sum(jnp.where(same, jnp.exp(bias[...] - top), 0.0), axis=0, keepdims=True)
+    row_ids = lax.broadcasted_iota(jnp.int32, logits.shape, 0)
+    logits[...] = jnp.where(row_ids == place, (top + jnp.log(terms)) * LOG2E, logits[...])
+
+
 def softmax_rows(scores):
-    terms = jnp.exp(scores - jnp.max(scores, axis=0, keepdims=True))
+    terms = jnp.exp2(scores - jnp.max(scores, axis=0, keepdims=True))
     return terms * (1.0 / jnp.sum(terms, axis=0, keepdims=True))
 
 
 def score_back(probs, grad_probs):
     probs = probs.astype(F32)
     inner = jnp.sum(probs * grad_probs, axis=0, keepdims=True)
-    return (probs * (grad_probs - inner) * (1.0 / math.sqrt(HEAD))).astype(BF16)
+    return probs * (grad_probs - inner) * (1.0 / math.sqrt(HEAD))
 
 
 def split_terms(values):
@@ -111,6 +122,7 @@
     nbrs,
     bias,
     dec_query,
+    weight_t,
     sems,
     *,
     rows,
@@ -127,11 +139,6 @@
     ]
     for copy in copies:
         copy.start()
-    copies[0].wait()
-    values = embed[...].T
-    embed_t[...] = values
-    norm = normalize(values.astype(F32), 0)[0].astype(BF16)
-    norm_t[...] = norm
     copies[1].wait()
     copies[2].wait()
     local = (nbrs[...] - window_start(rows)) & (total - 1)
@@ -139,8 +146,18 @@
         local < halo, local + rows, jnp.where(local < halo + rows, local - halo, local)
     )
     logits[...] = spread_bias(places, bias[...], rows + 2 * halo)
+    copies[0].wait()
     copies[3].wait()
-    query_t[...] = tn(dec_query[...], norm).astype(BF16)
+    weight_t[...] = dec_query[...].T
+
+    @pl.loop(0, slots // TILE)
+    def _(i):
+        tile = pl.ds(pl.multiple_of(i * TILE, TILE), TILE)
+        values = embed[tile, :].T
+        embed_t[:, tile] = values
+        norm = normalize(values.astype(F32), 0)[0].astype(BF16)
+        norm_t[:, tile] = norm
+        query_t[:, tile] = nn(weight_t[...], norm).astype(BF16)
 
 
 def window_order(values, rows, halo):
@@ -153,6 +170,14 @@
         ],
         axis=0,
     )
+
+
+def each(count):
+    def run(body):
+        for i in range(count):
+            body(i)
+
+    return run
 
 
 def step_kernel(
@@ -199,24 +224,46 @@
     pred,
     grads,
     latent,
+    latent_q,
+    units,
+    acts,
+    acts_q,
+    affine,
+    affine_t,
+    sums,
+    col_sums,
+    scores,
     unit_t,
     unit_q_t,
+    list_slots,
+    list_bias,
     mesh_logits,
     mesh_query,
     mesh_kv,
     mesh_probs,
+    mesh_grad_scores,
     mesh_mixed,
+    mesh_grad_mixed,
     mesh_out,
+    mesh_grad_out,
     mesh_norm,
+    mesh_norm_t,
     dec_keys,
     grid_probs,
+    grid_grad_scores,
     grid_mixed,
+    grid_grad_out,
+    grid_grad_mixed,
     grid_out,
     grid_final,
     change,
     grad_change,
     head_pad,
+    head_t,
+    dec_out_t,
+    grad_query,
     grad_dec,
+    grad_q,
     grad_kv,
     load_sems,
     store_sems,
@@ -226,13 +273,14 @@
     halo, dim = above.shape
     rows = 2 * halo
     window = rows + 2 * halo
+    outer = 2 * window
     own = packet[:rows]
     edges = packet[rows:]
     heads = dim // HEAD
     members = 2
     channels = weather.shape[0]
     slots = embed_t.shape[1]
-    inv_sqrt = 1.0 / math.sqrt(HEAD)
+    inv_sqrt = LOG2E / math.sqrt(HEAD)
     member = lax.axis_index("member")
     core = lax.rem(lax.axis_index("space"), 2)
     here = pl.ds(pl.multiple_of(member * slots, slots), slots)
@@ -241,11 +289,14 @@
 
     def load(name, source, target_ref):
         loads[name] = pltpu.make_async_copy(source, target_ref, load_sems.at[len(loads)])
-        loads[name].start()
-
+
+    def start(*group):
+        for name in group:
+            loads[name].start()
+
+    load("qkv", qkv_hbm, attn_qkv)
     load("scale", scale_hbm, cond_scale)
     load("shift", shift_hbm, cond_shift)
-    load("qkv", qkv_hbm, attn_qkv)
     load("attn_out", attn_out_hbm, attn_out)
     load("dec_kv", dec_kv_hbm, dec_kv)
     load("query", query_hbm, query_t)
@@ -257,6 +308,7 @@
     load("target", target_hbm.at[:, here], target)
     load("area", area_hbm.at[:, here], area)
     load("norm", norm_hbm, norm_t)
+    start("qkv", "scale", "shift")
 
     odd = core == 1
     latent[0:halo] = below[:halo]
@@ -264,10 +316,6 @@
     latent[halo + rows : halo + 2 * rows] = own
     latent[halo + 2 * rows : halo + 3 * rows] = jnp.where(odd, beside[:rows], twin[:rows])
     latent[halo + 3 * rows :] = above[...]
-    unit = normalize(latent[...].astype(F32), 1)[0]
-    unit_t[...] = unit.astype(BF16).T
-    unit_q_t[...] = window_order(unit, rows, halo).astype(BF16).T
-
     lane = lax.broadcasted_iota(jnp.int32, (edges.shape[0], rows), 1)
     late = (lane >= halo) == odd
     ends = jnp.where(
@@ -281,11 +329,14 @@
             pltpu.roll(ends[:, part * rows : (part + 1) * rows], halo, 1),
         ]
 
-    mesh_logits[...] = spread_bias(
-        jnp.concatenate(listed(0), axis=1).astype(jnp.int32),
-        joined_terms(*(jnp.concatenate(listed(part), axis=1) for part in (1, 2, 3))),
-        window,
-    )
+    list_slots[...] = jnp.concatenate(listed(0), axis=1).astype(jnp.int32)
+    list_bias[...] = joined_terms(*(jnp.concatenate(listed(part), axis=1) for part in (1, 2, 3)))
+    mesh_logits[...] = jnp.full(mesh_logits.shape, FAR, F32)
+
+    @pl.loop(0, list_slots.shape[0])
+    def _(entry):
+        add_entry(list_slots, list_bias, entry, mesh_logits)
+
     noise_row = joined_terms(*(below[halo:, part * rows : (part + 1) * rows] for part in (0, 1, 2)))
     spread = cond_scale.shape[0]
     own_row = jnp.concatenate([noise_own[...], jnp.zeros((1, rows - spread), F32)], axis=1)
@@ -295,17 +346,27 @@
         noise_out[m] = columns
         noise.append(columns[:, :1])
     is_before = lax.broadcasted_iota(jnp.int32, (window, rows), 1) < halo
-
-    def split_ends(values):
-        values = values.astype(F32)
-        return jnp.concatenate(
-            [jnp.where(is_before, values, 0.0), jnp.where(is_before, 0.0, values)], axis=0
-        ).astype(BF16)
-
-    def window_scores(keys, queries):
-        mid = nn(keys[rows : rows + window], queries[:, :rows])
-        ends = nn(keys, queries[:, rows:])
-        return jnp.concatenate([mid, jnp.where(is_before, ends[:window], ends[window:])], axis=1)
+    inner = slice(rows, rows + window)
+
+    def compact(full):
+        return full[inner, :rows], jnp.where(is_before, full[:window, rows:], full[window:, rows:])
+
+    def spread_out(target_ref, middle, ends):
+        target_ref[inner, :rows] = middle.astype(BF16)
+        target_ref[:window, rows:] = jnp.where(is_before, ends, 0.0).astype(BF16)
+        target_ref[window:, rows:] = jnp.where(is_before, 0.0, ends).astype(BF16)
+
+    def tile_of(index, size=TILE, base=0):
+        if isinstance(index, int):
+            return slice(base + index * size, base + (index + 1) * size)
+        return pl.ds(pl.multiple_of(base + index * size, size), size)
+
+    @each(members * heads)
+    def _(i):
+        mesh_probs[i, :rows, :rows] = jnp.zeros((rows, rows), BF16)
+        mesh_probs[i, rows + window :, :rows] = jnp.zeros((rows, rows), BF16)
+        mesh_grad_scores[i, :rows, :rows] = jnp.zeros((rows, rows), BF16)
+        mesh_grad_scores[i, rows + window :, :rows] = jnp.zeros((rows, rows), BF16)
 
     loads["scale"].wait()
     loads["shift"].wait()
@@ -314,60 +375,147 @@
     for m in range(members):
         gains.append(1.0 + jnp.sum(noise[m] * cond_scale[...], axis=0, keepdims=True))
         shifts.append(jnp.sum(noise[m] * cond_shift[...], axis=0, keepdims=True))
-
+        affine[2 * m : 2 * m + 1] = gains[m]
+        affine[2 * m + 1 : 2 * m + 2] = shifts[m]
+
+    @each(outer // rows)
+    def _(i):
+        tile = tile_of(i, rows)
+        unit = normalize(latent[tile, :].astype(F32), 1)[0]
+        units[tile, :] = unit.astype(BF16)
+        unit_t[:dim, tile] = unit.astype(BF16).T
+        for m in range(members):
+            act = unit * affine[2 * m : 2 * m + 1] + affine[2 * m + 1 : 2 * m + 2]
+            acts[tile_of(i, rows, m * outer), :] = act.astype(BF16)
+
+    latent_q[...] = window_order(latent, rows, halo)
+    unit_q_t[:dim] = window_order(units, rows, halo).T
+    unit_q_t[dim:] = jnp.ones((16, window), BF16)
+    unit_t[dim:] = jnp.ones((16, outer), BF16)
+    for m in range(members):
+        acts_q[m * window : (m + 1) * window] = window_order(
+            acts.at[m * outer : (m + 1) * outer], rows, halo
+        )
+
+    start("attn_out", "dec_kv")
     loads["qkv"].wait()
-    for m in range(members):
-        act = (unit * gains[m] + shifts[m]).astype(BF16)
-        mesh_kv[m] = nn(act, attn_qkv[:, dim:]).astype(BF16)
-        act_q = window_order(act, rows, halo)
-        mesh_query[m] = nn(act_q, attn_qkv[:, :dim]).astype(BF16).T
-        for h in range(heads):
-            cols = slice(h * HEAD, (h + 1) * HEAD)
-            value_cols = slice(dim + h * HEAD, dim + (h + 1) * HEAD)
-            scores = window_scores(mesh_kv[m, :, cols], mesh_query[m, cols, :])
-            probs = softmax_rows(scores * inv_sqrt + mesh_logits[...]).astype(BF16)
-            mesh_probs[m, h] = probs
-            values = mesh_kv[m, :, value_cols]
-            mid = tn(values[rows : rows + window], probs[:, :rows])
-            ends = tn(values, split_ends(probs[:, rows:]))
-            mesh_mixed[m, cols, :] = jnp.concatenate([mid, ends], axis=1).astype(BF16)
-        if m == 0:
-            loads["attn_out"].wait()
-            loads["dec_kv"].wait()
-        residual = window_order(latent[...].astype(F32), rows, halo)
-        out = (residual + nn(mesh_mixed[m].T, attn_out[...])).astype(BF16)
-        mesh_out[m] = out
+    start("query", "logits", "embed", "dec_out", "head", "weather", "target", "area", "norm")
+
+    @each(dim // TILE)
+    def _(i):
+        part = nn(acts_q[...], attn_qkv[:, tile_of(i)]).astype(BF16)
+        mesh_query[tile_of(i), :] = part.T
+
+    @each(2 * dim // TILE)
+    def _(i):
+        mesh_kv[:, tile_of(i)] = nn(acts[...], attn_qkv[:, tile_of(i, TILE, dim)]).astype(BF16)
+
+    pairs = [(m * heads + h, m, h) for m in range(members) for h in range(heads)]
+
+    def span(index, size, base=0):
+        return slice(base + index * size, base + (index + 1) * size)
+
+    for i, m, h in pairs:
+        keys = mesh_kv[span(m, outer), span(h, HEAD)]
+        middle, ends = compact(nn(keys, mesh_query[span(h, HEAD), span(m, window)]))
+        scores[i, :, :rows] = middle
+        scores[i, :, rows:window] = ends
+
+    @each(members * heads)
+    def _(i):
+        parts = [
+            softmax_rows(scores[i, :, lanes] * inv_sqrt + mesh_logits[:, lanes])
+            for lanes in (span(0, rows), span(1, rows))
+        ]
+        spread_out(mesh_probs.at[i], *parts)
+
+    for i, m, h in pairs:
+        values = mesh_kv[span(m, outer), span(h, HEAD, dim)]
+        mesh_mixed[span(h, HEAD), span(m, window)] = tn(values, mesh_probs[i]).astype(BF16)
+
+    loads["attn_out"].wait()
+
+    @each(members)
+    def _(m):
+        here_q = tile_of(m, window)
+        mixed = mesh_mixed[:, here_q].T
+        out = (latent_q[...].astype(F32) + nn(mixed, attn_out[...])).astype(BF16)
+        mesh_out[here_q, :] = out
         norm = normalize(out.astype(F32), 1)[0].astype(BF16)
-        mesh_norm[m] = norm
-        dec_keys[m] = nn(norm, dec_kv[...]).astype(BF16)
+        mesh_norm[here_q, :] = norm
+        mesh_norm_t[:, here_q] = norm.T
+
+    loads["dec_kv"].wait()
+
+    @each(2 * dim // TILE)
+    def _(i):
+        dec_keys[:, tile_of(i)] = nn(mesh_norm[...], dec_kv[:, tile_of(i)]).astype(BF16)
 
     for name in ("query", "logits", "embed", "dec_out", "head"):
         loads[name].wait()
     head_pad[...] = jnp.zeros_like(head_pad)
     head_pad[:channels] = head_out[...]
+    head_t[...] = head_pad[...].T
+    dec_out_t[...] = dec_out[...].T
+
+    for i, m, h in pairs:
+        scores[i] = nn(dec_keys[span(m, window), span(h, HEAD)], query_t[span(h, HEAD), :])
+
+    @each(members * heads)
+    def _(i):
+        for t in range(slots // HEAD):
+            lanes = span(t, HEAD)
+            probs = softmax_rows(scores[i, :, lanes] * inv_sqrt + grid_logits[:, lanes])
+            grid_probs[i, :, lanes] = probs.astype(BF16)
+
+    for i, m, h in pairs:
+        values = dec_keys[span(m, window), span(h, HEAD, dim)]
+        grid_mixed[span(h, HEAD), span(m, slots)] = tn(values, grid_probs[i]).astype(BF16)
+
     for m in range(members):
-        for h in range(heads):
-            cols = slice(h * HEAD, (h + 1) * HEAD)
-            value_cols = slice(dim + h * HEAD, dim + (h + 1) * HEAD)
-            scores = nn(dec_keys[m, :, cols], query_t[cols, :])
-            probs = softmax_rows(scores * inv_sqrt + grid_logits[...]).astype(BF16)
-            grid_probs[m, h] = probs
-            grid_mixed[m, cols, :] = tn(dec_keys[m, :, value_cols], probs).astype(BF16)
-        out = (embed_t[...].astype(F32) + tn(dec_out[...], grid_mixed[m])).astype(BF16)
-        grid_out[m] = out
-        final = normalize(out.astype(F32), 0)[0].astype(BF16)
-        grid_final[m] = final
-        change[m] = nn(head_pad[...], final)
+        out = embed_t[...].astype(F32) + nn(dec_out_t[...], grid_mixed[:, span(m, slots)])
+        grid_out[:, span(m, slots)] = out.astype(BF16)
+
+    lane_tiles = members * slots // HEAD
+
+    @each(lane_tiles)
+    def _(i):
+        tile = tile_of(i, HEAD)
+        final = normalize(grid_out[:, tile].astype(F32), 0)[0].astype(BF16)
+        grid_final[:, tile] = final
+
+    change[...] = nn(head_pad[...], grid_final[...])
 
     for name in ("weather", "target", "area", "norm"):
         loads[name].wait()
-    slot = lax.broadcasted_iota(jnp.int32, (1, slots), 1) + member * slots
-    live = jnp.where(slot < counts[0], 1.0, 0.0)
-    weighting = live * area[...]
-    first = weather[...] + live * change[0, :channels]
-    second = weather[...] + live * change[1, :channels]
-    pred[0] = first
-    pred[1] = second
+    def smooth(values):
+        square = values * values + SMOOTHING
+        inverse = lax.rsqrt(square)
+        return square * inverse, values * inverse
+
+    grad_change[...] = jnp.zeros_like(grad_change)
+
+    def compare(i, loss):
+        tile = tile_of(i, HEAD)
+        slot = lax.broadcasted_iota(jnp.int32, (1, HEAD), 1) + (member * slots + i * HEAD)
+        live = jnp.where(slot < counts[0], 1.0, 0.0)
+        weighting = live * area[:, tile]
+        second_tile = tile_of(i, HEAD, slots)
+        first = weather[:, tile] + live * change[:channels, tile]
+        second = weather[:, tile] + live * change[:channels, second_tile]
+        pred[0, :, tile] = first
+        pred[1, :, tile] = second
+        size_first, slope_first = smooth(first - target[:, tile])
+        size_second, slope_second = smooth(second - target[:, tile])
+        size_pair, slope_pair = smooth(first - second)
+        factor = weighting * (LOSS_SCALE / scale_den)
+        grad_change[:channels, tile] = (factor * (slope_first - slope_pair)).astype(BF16)
+        grad_change[:channels, second_tile] = (factor * (slope_second + slope_pair)).astype(BF16)
+        terms = weighting * (size_first + size_second - size_pair)
+        return loss + jnp.sum(terms, axis=0, keepdims=True)
+
+    loss = lax.fori_loop(0, slots // HEAD, compare, jnp.zeros((1, HEAD), F32))
+    loss = jnp.sum(loss) / scale_den
     stores = [
         pltpu.make_async_copy(pred.at[0], pred_own_hbm, store_sems.at[0]),
         pltpu.make_async_copy(pred.at[1], pred_other_hbm, store_sems.at[1]),
@@ -375,131 +523,179 @@
     for store in stores:
         store.start()
 
-    def smooth(values):
-        square = values * values + SMOOTHING
-        inverse = lax.rsqrt(square)
-        return square * inverse, values * inverse
-
-    size_first, slope_first = smooth(first - target[...])
-    size_second, slope_second = smooth(second - target[...])
-    size_pair, slope_pair = smooth(first - second)
-    loss = jnp.sum(weighting * (size_first + size_second - size_pair)) / scale_den
-    factor = weighting * (LOSS_SCALE / scale_den)
-    grad_change[...] = jnp.zeros_like(grad_change)
-    grad_change[0, :channels] = (factor * (slope_first - slope_pair)).astype(BF16)
-    grad_change[1, :channels] = (factor * (slope_second + slope_pair)).astype(BF16)
-
-    grad_head = None
-    grad_dec_out = None
-    grad_query = None
+    tall = HEAD * HEAD // dim
+    per_block = dim // tall
+
+    def pack(index, tile, block):
+        half, chunk = index // 4, index % 4 * per_block
+        for c in range(per_block):
+            for t in range(TILE // HEAD):
+                where = tile_of(tile * (TILE // HEAD) + t, tall)
+                part = block[c * tall : (c + 1) * tall, t * HEAD : (t + 1) * HEAD]
+                grads[half, chunk + c, where, :] = part.astype(BF16)
+
+    col_tiles = dim // TILE
+
+    def pack_extras(half, chunk, values):
+        for i in range(values.shape[0] // 8):
+            for t in range(heads):
+                grads[half, chunk + i * heads + t, HEAD:, :] = values[
+                    i * 8 : (i + 1) * 8, t * HEAD : (t + 1) * HEAD
+                ].astype(BF16)
+
+    def ship(half, first, last, sem):
+        source = grads.at[half, first:last]
+        keep = pltpu.make_async_copy(source, keep_hbm.at[first:last], store_sems.at[sem])
+        send = pltpu.make_async_copy(source, send_hbm.at[first:last], store_sems.at[sem])
+        pl.when(core == half)(keep.start)
+        pl.when(core != half)(send.start)
+        stores.append(keep)
+
+    grads[:, :, HEAD:, :] = jnp.zeros((2, 4 * per_block, 8, HEAD), BF16)
+
+    pack_extras(1, 0, nt(grad_change[...], grid_final[...]))
+
+    @each(lane_tiles)
+    def _(i):
+        tile = tile_of(i, HEAD)
+        g_final = nn(head_t[...], grad_change[:, tile])
+        g_out = normalize_back(grid_out[:, tile].astype(F32), g_final, 0).astype(BF16)
+        grid_grad_out[:, tile] = g_out
+
     for m in range(members):
-        g_change = grad_change[m]
-        term = nt(g_change, grid_final[m])
-        grad_head = term if m == 0 else grad_head + term
-        g_final = tn(head_pad[...], g_change)
-        g_out = normalize_back(grid_out[m].astype(F32), g_final, 0).astype(BF16)
-        term = nt(grid_mixed[m], g_out)
-        grad_dec_out = term if m == 0 else grad_dec_out + term
-        g_mixed = nn(dec_out[...], g_out).astype(BF16)
-        terms = []
-        for h in range(heads):
-            cols = slice(h * HEAD, (h + 1) * HEAD)
-            value_cols = slice(dim + h * HEAD, dim + (h + 1) * HEAD)
-            g_head = g_mixed[cols, :]
-            probs = grid_probs[m, h]
-            g_scores = score_back(probs, nn(dec_keys[m, :, value_cols], g_head))
-            terms.append(tn(dec_keys[m, :, cols], g_scores))
-            grad_dec[m, :, cols] = nt(g_scores, query_t[cols, :]).astype(BF16)
-            grad_dec[m, :, value_cols] = nt(probs, g_head).astype(BF16)
-        term = jnp.concatenate(terms, axis=0)
-        grad_query = term if m == 0 else grad_query + term
-    grad_dec_query = nt(norm_t[...], grad_query.astype(BF16))
-
-    grad_dec_kv = None
-    grad_attn_out = None
-    grad_qkv = None
-    grad_cond = None
+        g_mixed = nn(dec_out[...], grid_grad_out[:, span(m, slots)])
+        grid_grad_mixed[:, span(m, slots)] = g_mixed.astype(BF16)
+
+    @each(col_tiles)
+    def _(i):
+        pack(7, i, nt(grid_mixed[...], grid_grad_out[tile_of(i), :]))
+
+    for i, m, h in pairs:
+        values = dec_keys[span(m, window), span(h, HEAD, dim)]
+        scores[i] = nn(values, grid_grad_mixed[span(h, HEAD), span(m, slots)])
+
+    @each(members * heads)
+    def _(i):
+        here = tile_of(i % heads * members + i // heads, window)
+        for t in range(slots // HEAD):
+            lanes = span(t, HEAD)
+            grid_grad_scores[here, lanes] = score_back(
+                grid_probs[i, :, lanes], scores[i, :, lanes]
+            ).astype(BF16)
+
+    for i, m, h in pairs:
+        g_scores = grid_grad_scores[span(h * members + m, window), :]
+        g_head = grid_grad_mixed[span(h, HEAD), span(m, slots)]
+        probs = grid_probs[i]
+        grad_dec[span(m, window), span(h, HEAD)] = nt(g_scores, query_t[span(h, HEAD), :]).astype(BF16)
+        grad_dec[span(m, window), span(h, HEAD, dim)] = nt(probs, g_head).astype(BF16)
+    for h in range(heads):
+        keys = dec_keys[:, span(h, HEAD)]
+        g_scores = grid_grad_scores[span(h, members * window), :]
+        grad_query[span(h, HEAD), :] = tn(keys, g_scores).astype(BF16)
+
+    @each(col_tiles)
+    def _(i):
+        pack(4, i, nt(norm_t[...], grad_query[tile_of(i), :]))
+
+    @each(2 * col_tiles)
+    def _(i):
+        block = nn(mesh_norm_t[...], grad_dec[:, tile_of(i)])
+        pack(5 + i // col_tiles, i % col_tiles, block)
+
+    ship(1, 0, 4 * per_block, 2)
+
+    @each(members)
+    def _(m):
+        here_q = tile_of(m, window)
+        g_norm = nt(grad_dec[here_q, :], dec_kv[...])
+        g_out = normalize_back(mesh_out[here_q, :].astype(F32), g_norm, 1).astype(BF16)
+        mesh_grad_out[here_q, :] = g_out
+        mesh_grad_mixed[:, here_q] = nt(attn_out[...], g_out).astype(BF16)
+
+    @each(col_tiles)
+    def _(i):
+        pack(3, i, nn(mesh_mixed[...], mesh_grad_out[:, tile_of(i)]))
+
+    for i, m, h in pairs:
+        values = mesh_kv[span(m, outer), span(h, HEAD, dim)]
+        middle, ends = compact(nn(values, mesh_grad_mixed[span(h, HEAD), span(m, window)]))
+        scores[i, :, :rows] = middle
+        scores[i, :, rows:window] = ends
+
+    @each(members * heads)
+    def _(i):
+        parts = [
+            score_back(probs, scores[i, :, lanes])
+            for probs, lanes in zip(compact(mesh_probs[i]), (span(0, rows), span(1, rows)))
+        ]
+        spread_out(mesh_grad_scores.at[i], *parts)
+
+    for i, m, h in pairs:
+        cols = span(h, HEAD)
+        g_scores = mesh_grad_scores[i]
+        g_head = mesh_grad_mixed[cols, span(m, window)]
+        g_query = tn(mesh_kv[span(m, outer), cols], g_scores).astype(BF16)
+        grad_q[span(m, window), cols] = g_query.T
+        grad_kv[span(m, outer), cols] = nt(g_scores, mesh_query[cols, span(m, window)]).astype(BF16)
+        grad_kv[span(m, outer), span(h, HEAD, dim)] = nt(mesh_probs[i], g_head).astype(BF16)
+
     for m in range(members):
-        g_dec = grad_dec[m]
-        term = tn(mesh_norm[m], g_dec)
-        grad_dec_kv = term if m == 0 else grad_dec_kv + term
-        g_norm = nt(g_dec, dec_kv[...])
-        g_out = normalize_back(mesh_out[m].astype(F32), g_norm, 1).astype(BF16)
-        term = nn(mesh_mixed[m], g_out)
-        grad_attn_out = term if m == 0 else grad_attn_out + term
-        g_mixed = nt(attn_out[...], g_out).astype(BF16)
-        g_queries = []
-        for h in range(heads):
-            cols = slice(h * HEAD, (h + 1) * HEAD)
-            value_cols = slice(dim + h * HEAD, dim + (h + 1) * HEAD)
-            g_head = g_mixed[cols, :]
-            probs = mesh_probs[m, h]
-            keys = mesh_kv[m, :, cols]
-            g_scores = score_back(probs, window_scores(mesh_kv[m, :, value_cols], g_head))
-            g_ends = split_ends(g_scores[:, rows:])
-            mid = tn(keys[rows : rows + window], g_scores[:, :rows])
-            ends = tn(keys, g_ends)
-            g_queries.append(jnp.concatenate([mid, ends], axis=1))
-            queries = mesh_query[m, cols, :]
-            grad_kv[:, cols] = nt(g_ends, queries[:, rows:])
-            grad_kv[rows : rows + window, cols] += nt(g_scores[:, :rows], queries[:, :rows])
-            grad_kv[:, value_cols] = nt(split_ends(probs[:, rows:]), g_head[:, rows:])
-            grad_kv[rows : rows + window, value_cols] += nt(probs[:, :rows], g_head[:, :rows])
-        g_kv = grad_kv[...].astype(BF16)
-        g_query = jnp.concatenate(g_queries, axis=0).astype(BF16).T
-        moment = jnp.concatenate([nn(unit_q_t[...], g_query), nn(unit_t[...], g_kv)], axis=1)
-        col_sum = jnp.concatenate(
-            [
-                jnp.sum(g_query.astype(F32), axis=0, keepdims=True),
-                jnp.sum(g_kv.astype(F32), axis=0, keepdims=True),
-            ],
-            axis=1,
+        gain_col = jnp.broadcast_to(gains[m], (HEAD, dim)).T
+        shift_col = jnp.broadcast_to(shifts[m], (HEAD, dim)).T
+        affine_t[2 * m] = gain_col
+        affine_t[2 * m + 1] = shift_col
+    sums[...] = jnp.zeros_like(sums)
+    col_sums[...] = jnp.zeros_like(col_sums)
+
+    def project_back(index, tile, weight_tile, left, parts):
+        weight = attn_qkv[:, weight_tile].astype(F32)
+        total = None
+        for m in range(members):
+            moment = nn(left[...], parts[m])
+            col_sum = moment[dim : dim + 1]
+            moment = moment[:dim]
+            high, middle, low = split_terms(col_sum)
+            for row, value in enumerate((high, middle, low)):
+                col_sums[8 * m + row : 8 * m + row + 1, weight_tile] = value.astype(F32)
+            by_gain = weight * moment
+            sums[m] += by_gain[:, :HEAD] + by_gain[:, HEAD:]
+            terms = []
+            for t in range(TILE // HEAD):
+                lanes = slice(t * HEAD, (t + 1) * HEAD)
+                terms.append(
+                    affine_t[2 * m] * moment[:, lanes] + affine_t[2 * m + 1] * col_sum[:, lanes]
+                )
+            term = jnp.concatenate(terms, axis=1)
+            total = term if m == 0 else total + term
+        pack(index, tile, total)
+
+    @each(2 * col_tiles)
+    def _(i):
+        parts = [grad_kv[m * outer : (m + 1) * outer, tile_of(i)] for m in range(members)]
+        project_back(
+            1 + i // col_tiles, i % col_tiles, tile_of(i, TILE, dim), unit_t, parts
         )
-        gain_col = jnp.broadcast_to(gains[m], (HEAD, dim)).T[:, :1]
-        shift_col = jnp.broadcast_to(shifts[m], (HEAD, dim)).T[:, :1]
-        term = gain_col * moment + shift_col * col_sum
-        grad_qkv = term if m == 0 else grad_qkv + term
-        weight = attn_qkv[...].astype(F32)
-        g_gain = jnp.sum(weight * moment, axis=1, keepdims=True)
-        g_shift = jnp.sum(weight * col_sum, axis=1, keepdims=True)
+
+    ship(0, per_block, 4 * per_block, 3)
+
+    @each(col_tiles)
+    def _(i):
+        parts = [grad_q[m * window : (m + 1) * window, tile_of(i)] for m in range(members)]
+        project_back(0, i, tile_of(i), unit_q_t, parts)
+
+    row_id = lax.broadcasted_iota(jnp.int32, (8, dim), 0)
+    grad_cond = jnp.where(row_id == 4, loss, 0.0)
+    g_shifts = nt(attn_qkv[...], col_sums[...].astype(BF16))
+    for m in range(members):
         mine = member if m == 0 else 1 - member
-        row_id = lax.broadcasted_iota(jnp.int32, (8, dim), 0)
-        term = jnp.where(row_id == mine, jnp.broadcast_to(g_gain, (dim, HEAD)).T[:8], 0.0)
-        term += jnp.where(row_id == mine + 2, jnp.broadcast_to(g_shift, (dim, HEAD)).T[:8], 0.0)
-        grad_cond = term if m == 0 else grad_cond + term
-
-    row_id = lax.broadcasted_iota(jnp.int32, (8, dim), 0)
-    grad_cond += jnp.where(row_id == 4, loss, 0.0)
-    grads[:, :, HEAD:, :] = jnp.zeros((2, 64, 8, HEAD), BF16)
-    blocks = (
-        grad_qkv[:, :dim],
-        grad_qkv[:, dim : 2 * dim],
-        grad_qkv[:, 2 * dim :],
-        grad_attn_out,
-        grad_dec_query,
-        grad_dec_kv[:, :dim],
-        grad_dec_kv[:, dim:],
-        grad_dec_out,
-    )
-    tall = HEAD * HEAD // dim
-    for i, block in enumerate(blocks):
-        first_chunk = i % 4 * (dim // tall)
-        for c in range(dim // tall):
-            for t in range(heads):
-                grads[i // 4, first_chunk + c, t * tall : (t + 1) * tall, :] = block[
-                    c * tall : (c + 1) * tall, t * HEAD : (t + 1) * HEAD
-                ].astype(BF16)
-    extras = jnp.concatenate([grad_head, grad_cond], axis=0)
-    for i in range(extras.shape[0] // 8):
-        for t in range(heads):
-            grads[0, i * heads + t, HEAD:, :] = extras[
-                i * 8 : (i + 1) * 8, t * HEAD : (t + 1) * HEAD
-            ].astype(BF16)
-    keep = pltpu.make_async_copy(grads.at[core], keep_hbm, store_sems.at[2])
-    send = pltpu.make_async_copy(grads.at[1 - core], send_hbm, store_sems.at[3])
-    keep.start()
-    send.start()
-    stores += [keep, send]
+        g_shift = g_shifts[:, 8 * m : 8 * m + 3]
+        for row, lanes in ((mine, sums[m]), (mine + 2, g_shift)):
+            column = jnp.sum(lanes, axis=1, keepdims=True)
+            values = jnp.broadcast_to(column, (dim, HEAD)).T[:8]
+            grad_cond += jnp.where(row_id == row, values, 0.0)
+    pack_extras(0, 0, grad_cond)
+    ship(0, 0, per_block, 4)
     for store in stores:
         store.wait()
 
@@ -561,23 +757,26 @@
         (grad_dec_kv, dim),
         (grad_dec_out, 0),
     )
-    for i, (ref, col) in enumerate(targets):
-        first_chunk = i % 4 * (dim // tall)
-        for c in range(dim // tall):
+    per_block = dim // tall
+
+    @pl.loop(0, per_block)
+    def _(c):
+        tile = pl.ds(pl.multiple_of(c * tall, tall), tall)
+        for i, (ref, col) in enumerate(targets):
             for t in range(heads):
-                ref[c * tall : (c + 1) * tall, col + t * HEAD : col + (t + 1) * HEAD] = grads[
-                    i // 4, first_chunk + c, t * tall : (t + 1) * tall, :
+                ref[tile, col + t * HEAD : col + (t + 1) * HEAD] = grads[
+                    i // 4, i % 4 * per_block + c, t * tall : (t + 1) * tall, :
                 ].astype(F32)
 
-    def extra(i):
+    def extra(half, i):
         return jnp.concatenate(
-            [grads[0, i * heads + t, HEAD:, :].astype(F32) for t in range(heads)], axis=1
+            [grads[half, i * heads + t, HEAD:, :].astype(F32) for t in range(heads)], axis=1
         )
 
     for i in range(-(-channels // 8)):
         count = min(8, channels - i * 8)
-        grad_head[i * 8 : i * 8 + count] = extra(i)[:count]
-    cond = extra(4 * (-(-channels // 32)))
+        grad_head[i * 8 : i * 8 + count] = extra(1, i)[:count]
+    cond = extra(0, 0)
     first = cond[0:1]
     second = cond[1:2]
     grad_scale[...] = noise[0, :, :1] * jnp.where(member == 0, first, second) + noise[
@@ -654,10 +853,10 @@
         compiler_params=pltpu.CompilerParams(vmem_limit_bytes=ALL_VMEM),
         name="pack",
     )(mesh_latent, mesh_nbrs, mesh_bias, member_noise)
+    twin = permute(packet, lambda m, k: (m, k ^ 1))
     beside = permute(packet, lambda m, k: (m, k + 1 if k % 2 else k - 1))
     below = permute(upward, lambda m, k: (1 - m, k + 2))
     above = permute(downward, lambda m, k: (m, k - 2))
-    twin = permute(packet, lambda m, k: (m, k ^ 1))
 
     square = (dim, slots)
     embed_t, norm_t, query_t, grid_logits = pl.pallas_call(
@@ -674,6 +873,7 @@
             pltpu.VMEM((slots, dim), BF16),
             pltpu.VMEM((entries, slots), jnp.int32),
             pltpu.VMEM((entries, slots), F32),
+            pltpu.VMEM((dim, dim), BF16),
             pltpu.VMEM((dim, dim), BF16),
             pltpu.SemaphoreType.DMA((4,)),
         ],
@@ -731,27 +931,49 @@
             pltpu.VMEM((2, channels, slots), F32),
             pltpu.VMEM((2, *half_shape), BF16),
             pltpu.VMEM((outer, dim), BF16),
-            pltpu.VMEM((dim, outer), BF16),
-            pltpu.VMEM((dim, window), BF16),
+            pltpu.VMEM((window, dim), BF16),
+            pltpu.VMEM((outer, dim), BF16),
+            pltpu.VMEM((2 * outer, dim), BF16),
+            pltpu.VMEM((2 * window, dim), BF16),
+            pltpu.VMEM((8, dim), F32),
+            pltpu.VMEM((4, dim, HEAD), F32),
+            pltpu.VMEM((2, dim, HEAD), F32),
+            pltpu.VMEM((16, 3 * dim), F32),
+            pltpu.VMEM((2 * heads, window, slots), F32),
+            pltpu.VMEM((dim + 16, outer), BF16),
+            pltpu.VMEM((dim + 16, window), BF16),
+            pltpu.VMEM((mesh_nbrs.shape[0], window), jnp.int32),
+            pltpu.VMEM((mesh_nbrs.shape[0], window), F32),
             pltpu.VMEM((window, window), F32),
-            pltpu.VMEM((2, dim, window), BF16),
-            pltpu.VMEM((2, outer, 2 * dim), BF16),
-            pltpu.VMEM((2, heads, window, window), BF16),
-            pltpu.VMEM((2, dim, window), BF16),
-            pltpu.VMEM((2, window, dim), BF16),
-            pltpu.VMEM((2, window, dim), BF16),
-            pltpu.VMEM((2, window, 2 * dim), BF16),
-            pltpu.VMEM((2, heads, window, slots), BF16),
-            pltpu.VMEM((2, dim, slots), BF16),
-            pltpu.VMEM((2, dim, slots), BF16),
-            pltpu.VMEM((2, dim, slots), BF16),
-            pltpu.VMEM((2, channel_pad, slots), F32),
-            pltpu.VMEM((2, channel_pad, slots), BF16),
+            pltpu.VMEM((dim, 2 * window), BF16),
+            pltpu.VMEM((2 * outer, 2 * dim), BF16),
+            pltpu.VMEM((2 * heads, outer, window), BF16),
+            pltpu.VMEM((2 * heads, outer, window), BF16),
+            pltpu.VMEM((dim, 2 * window), BF16),
+            pltpu.VMEM((dim, 2 * window), BF16),
+            pltpu.VMEM((2 * window, dim), BF16),
+            pltpu.VMEM((2 * window, dim), BF16),
+            pltpu.VMEM((2 * window, dim), BF16),
+            pltpu.VMEM((dim, 2 * window), BF16),
+            pltpu.VMEM((2 * window, 2 * dim), BF16),
+            pltpu.VMEM((2 * heads, window, slots), BF16),
+            pltpu.VMEM((2 * heads * window, slots), BF16),
+            pltpu.VMEM((dim, 2 * slots), BF16),
+            pltpu.VMEM((dim, 2 * slots), BF16),
+            pltpu.VMEM((dim, 2 * slots), BF16),
+            pltpu.VMEM((dim, 2 * slots), BF16),
+            pltpu.VMEM((dim, 2 * slots), BF16),
+            pltpu.VMEM((channel_pad, 2 * slots), F32),
+            pltpu.VMEM((channel_pad, 2 * slots), BF16),
             pltpu.VMEM((channel_pad, dim), BF16),
-            pltpu.VMEM((2, window, 2 * dim), BF16),
-            pltpu.VMEM((outer, 2 * dim), F32),
+            pltpu.VMEM((dim, channel_pad), BF16),
+            pltpu.VMEM((dim, dim), BF16),
+            pltpu.VMEM((dim, slots), BF16),
+            pltpu.VMEM((2 * window, 2 * dim), BF16),
+            pltpu.VMEM((2 * window, dim), BF16),
+            pltpu.VMEM((2 * outer, 2 * dim), BF16),
             pltpu.SemaphoreType.DMA((14,)),
-            pltpu.SemaphoreType.DMA((4,)),
+            pltpu.SemaphoreType.DMA((5,)),
         ],
         out_shape=[
             jax.ShapeDtypeStruct((channels, slots), F32),

time: 148 us -> 145 us (0.980)
  Pallas kernels: 40.9 us -> 38.7 us
    pallas_call x1, Pallas kernels: 31.5 us -> 28.5 us  [per_device(): pl.pallas_call(lambda *refs: step_kernel(*refs, scale_den=scale_den), in_...]
where the time goes in v4:
time: 145 us
  blocking collectives  74.2 us (51%)
  Pallas kernels  38.7 us (27%)
  starting transfers between devices  19.6 us (14%)
  waiting for transfers between devices  6.76 us (5%)
  other arithmetic  2.2 us (2%)
  local copies, waits for them, and re-layouts  1.79 us (1%)
  between operations  1.59 us (1%)
    all_to_all x2, blocking collectives, over_chips(): return lax.all_to_all(value, axes, 0, 0, axis_index_groups=groups)  74.2 us
    pallas_call x1, Pallas kernels, per_device(): pl.pallas_call(lambda *refs: step_kernel(*refs, scale_den=scale_den), in_...  28.5 us
    ppermute x7, starting transfers between devices, permute(): return lax.ppermute(value, axes, pairs)  19.6 us
    ppermute x7, waiting for transfers between devices, permute(): return lax.ppermute(value, axes, pairs)  6.76 us
    pallas_call x1, Pallas kernels, per_device(): pl.pallas_call(unpack_kernel, in_specs=[pl.BlockSpec(memory_space=pl.ANY)...  4.68 us
    pallas_call x1, Pallas kernels, per_device(): pl.pallas_call(lambda *refs: prepare_kernel(*refs, rows=rows, halo=halo,...  3.34 us
  transfers between devices with their start and end apart: 7, of which 3 were waited for; matrix products, arithmetic and copies ran while one was open for 2% of the time, Pallas kernels for 2%

profile of v4, /device:TPU:1, one launch (start us, length us, event | category | flops | bytes accessed | tf_op | source)
XLA Modules:
  0.0 144.8 jit_solution(14428890867642786960)
XLA Ops:
  0.6 1.7 %pack.1 = (bf16[144,512]{1,0:T(8,128)(2,1)}, bf16[80,512]{1,0:T(8,128)(2,1)}, bf16[64,512]{1,0:T(8,128)(2,1)}) custom-call(bf16[128,512]{1,0:T(8,128)(2,1)} %refs_0_.3, s32[16,128]{1,0:T(8,128)} %refs_1_.2, f32[16,128]{1,0:T(8,128)} %refs_2_.2, f32[1,32]{1,0:T(1,128)} %refs_6_.1), custom_call_target="tpu_custom_call" | custom-call | tf_op jit(solution)/shard_map/pack/pallas_call | solution.py:845
  2.3 2.6 %collective-permute-start.1 = (bf16[144,512]{1,0:T(8,128)(2,1)}, bf16[144,512]{1,0:T(8,128)(2,1)S(1)}, u32[]{:S(2)}, u32[]{:S(2)}) collective-permute-start(bf16[144,512]{1,0:T(8,128)(2,1)} %get-tuple-element.35.refs_1_), channel_id=1, source_target_pairs={{0,63},{1,2},{2,1},{3,4},{4,3},{5,6},{6,5},{7,8},{8,7},{9,10},{10,... | collective-permute-start | bytes 442376 | tf_op jit(solution)/shard_map/ppermute | solution.py:840
  4.9 5.8 %collective-permute-start = (bf16[144,512]{1,0:T(8,128)(2,1)}, bf16[144,512]{1,0:T(8,128)(2,1)S(1)}, u32[]{:S(2)}, u32[]{:S(2)}) collective-permute-start(bf16[144,512]{1,0:T(8,128)(2,1)} %get-tuple-element.35.refs_1_), channel_id=1, source_target_pairs={{0,1},{1,0},{2,3},{3,2},{4,5},{5,4},{6,7},{7,6},{8,9},{9,8},{10,11... | collective-permute-start | bytes 442376 | tf_op jit(solution)/shard_map/ppermute | solution.py:840
  10.7 0.0 collective-permute-start.2
  10.7 6.3 %collective-permute-start.3 = (bf16[64,512]{1,0:T(8,128)(2,1)}, bf16[64,512]{1,0:T(8,128)(2,1)S(1)}, u32[]{:S(2)}, u32[]{:S(2)}) collective-permute-start(bf16[64,512]{1,0:T(8,128)(2,1)} %get-tuple-element.37), channel_id=1, source_target_pairs={{0,62},{1,63},{2,0},{3,1},{4,2},{5,3},{6,4},{7,5},{8,6},{9,7},{10,... | collective-permute-start | bytes 196616 | tf_op jit(solution)/shard_map/ppermute | solution.py:840
  17.7 3.3 %prepare.1 = (bf16[512,512]{1,0:T(8,128)(2,1)}, bf16[512,512]{1,0:T(8,128)(2,1)}, bf16[512,512]{1,0:T(8,128)(2,1)}, f32[256,512]{1,0:T(8,128)}) custom-call(bf16[1024,512]{1,0:T(8,128)(2,1)} %refs_0_.4, s32[3,1024]{1,0:T(4,128)} %refs_1_.3, f32[3,1024]{1,0:T(4,128)} %refs_2_.3, bf16[512,512]{1,0:T(8,128)(2,1)} %refs_3_.3), custom_call_target="tpu_custom_call" | custom-call | flops 268435456 | bytes 3145728 | tf_op jit(solution)/shard_map/prepare/pallas_call | solution.py:862
  21.0 0.0 collective-permute-done.3.refs_5_
  21.0 0.0 copy-start.5
  21.0 0.0 collective-permute-done.2.refs_4_
  21.0 0.0 copy-start.4
  21.0 0.0 collective-permute-done.1.refs_3_
  21.1 0.0 copy-start.2
  21.1 0.0 collective-permute-done.refs_2_
  21.1 0.0 copy-start.3
  21.1 0.6 copy-done.5
  21.6 0.0 copy-done.4
  21.7 0.0 copy-done.2
  21.7 0.1 copy-done.3
  21.8 28.5 %step.1 = (f32[84,512]{1,0:T(8,128)}, f32[84,512]{1,0:T(8,128)}, bf16[64,136,128]{2,1,0:T(8,128)(2,1)}, bf16[64,136,128]{2,1,0:T(8,128)(2,1)}, f32[2,32,128]{2,1,0:T(8,128)}) custom-call(s32[1]{0:T(128)S(6)} %copy.30.refs_0_, bf16[144,512]{1,0:T(8,128)(2,1)} %get-tuple-element.35.refs_1_, bf16[144,512]{1,0:T(8,128)(2,1)} %copy-done.3, ...), custom_call_target="tpu_custom_call" | custom-call | flops 10000000000 | bytes 12582912 | tf_op jit(solution)/shard_map/step/pallas_call | solution.py:912
  50.3 0.6 collective-permute-start.4
  51.0 1.7 %collective-permute-start.5 = (f32[84,512]{1,0:T(8,128)}, f32[84,512]{1,0:T(8,128)S(1)}, u32[]{:S(2)}, u32[]{:S(2)}) collective-permute-start(f32[84,512]{1,0:T(8,128)} %get-tuple-element.44), channel_id=1, source_target_pairs={{0,64},{1,65},{2,66},{3,67},{4,68},{5,69},{6,70},{7,71},{8,72},{9,... | collective-permute-start | bytes 516104 | tf_op jit(solution)/shard_map/ppermute | solution.py:840
  52.7 2.4 %collective-permute-done.4 = bf16[64,136,128]{2,1,0:T(8,128)(2,1)S(1)} collective-permute-done((bf16[64,136,128]{2,1,0:T(8,128)(2,1)}, bf16[64,136,128]{2,1,0:T(8,128)(2,1)S(1)}, u32[]{:S(2)}, u32[]{:S(2)}) %collective-permute-start.4) | collective-permute-done | bytes 2228256 | tf_op jit(solution)/shard_map/ppermute | solution.py:840
  55.1 2.2 %add_convert_fusion = bf16[64,136,128]{2,1,0:T(8,128)(2,1)S(1)} fusion(bf16[64,136,128]{2,1,0:T(8,128)(2,1)S(1)} %collective-permute-done.4, bf16[64,136,128]{2,1,0:T(8,128)(2,1)} %get-tuple-element.42), kind=kLoop, calls=%fused_computation | loop fusion | flops 4456448 | bytes 6684672 | tf_op jit(solution)/shard_map/convert_element_type | solution.py:1003
  57.4 0.0 copy-start
  57.4 1.4 collective-permute-done.5.pred_arrived_hbm
  58.8 37.1 %all_to_all.10.parts = bf16[64,136,128]{2,1,0:T(8,128)(2,1)S(1)} all-to-all(bf16[64,136,128]{2,1,0:T(8,128)(2,1)S(1)} %add_convert_fusion), channel_id=1, replica_groups={{0,2,4,6,8,10,12,14,16,18,20,22,24,26,28,30,32,34,36,38,40,42,44,46,48,..., dimensions={0} | all-to-all | bytes 4456448 | tf_op jit(solution)/shard_map/all_to_all | solution.py:1000
  95.9 0.0 copy-done
  95.9 0.5 sum.1
  96.4 0.0 copy-start.1
  96.4 37.1 %all_to_all.11.mine_hbm = bf16[64,136,128]{2,1,0:T(8,128)(2,1)S(1)} all-to-all(bf16[64,136,128]{2,1,0:T(8,128)(2,1)S(1)} %get-tuple-element.49), channel_id=1, replica_groups={{0,2,4,6,8,10,12,14,16,18,20,22,24,26,28,30,32,34,36,38,40,42,44,46,48,..., dimensions={0} | all-to-all | bytes 4456448 | tf_op jit(solution)/shard_map/all_to_all | solution.py:1000
  133.5 2.5 %collective-permute-start.6 = (bf16[64,136,128]{2,1,0:T(8,128)(2,1)S(1)}, bf16[64,136,128]{2,1,0:T(8,128)(2,1)S(1)}, u32[]{:S(2)}, u32[]{:S(2)}) collective-permute-start(bf16[64,136,128]{2,1,0:T(8,128)(2,1)S(1)} %all_to_all.11.mine_hbm), channel_id=1, source_target_pairs={{0,1},{1,0},{2,3},{3,2},{4,5},{5,4},{6,7},{7,6},{8,9},{9,8},{10,11... | collective-permute-start | bytes 6684680 | tf_op jit(solution)/shard_map/ppermute | solution.py:840
  136.0 1.1 copy.29
  137.1 2.9 %collective-permute-done.6.theirs_hbm = bf16[64,136,128]{2,1,0:T(8,128)(2,1)S(1)} collective-permute-done((bf16[64,136,128]{2,1,0:T(8,128)(2,1)S(1)}, bf16[64,136,128]{2,1,0:T(8,128)(2,1)S(1)}, u32[]{:S(2)}, u32[]{:S(2)}) %collective-permute-start.6) | collective-permute-done | bytes 2228256 | tf_op jit(solution)/shard_map/ppermute | solution.py:840
  140.0 0.0 copy-done.1
  140.0 4.7 %unpack.1 = (f32[32,512]{1,0:T(8,128)}, f32[32,512]{1,0:T(8,128)}, f32[512,1536]{1,0:T(8,128)}, f32[512,512]{1,0:T(8,128)}, f32[512,512]{1,0:T(8,128)}, /*index=...) custom-call(bf16[64,136,128]{2,1,0:T(8,128)(2,1)S(1)} %all_to_all.11.mine_hbm, ...), custom_call_target="tpu_custom_call" | custom-call | tf_op jit(solution)/shard_map/unpack/pallas_call | solution.py:1034
Async XLA Ops:
  2.3 18.8 %collective-permute-start.1 = (bf16[144,512]{1,0:T(8,128)(2,1)}, bf16[144,512]{1,0:T(8,128)(2,1)S(1)}, u32[]{:S(2)}, u32[]{:S(2)}) collective-permute-start(bf16[144,512]{1,0:T(8,128)(2,1)} %get-tuple-element.35.refs_1_), channel_id=1, source_target_pairs={{0,63},{1,2},{2,1},{3,4},{4,3},{5,6},{6,5},{7,8},{8,7},{9,10},{10,... | collective-permute-start | bytes 442376 | tf_op jit(solution)/shard_map/ppermute | solution.py:840
  4.9 16.2 %collective-permute-start = (bf16[144,512]{1,0:T(8,128)(2,1)}, bf16[144,512]{1,0:T(8,128)(2,1)S(1)}, u32[]{:S(2)}, u32[]{:S(2)}) collective-permute-start(bf16[144,512]{1,0:T(8,128)(2,1)} %get-tuple-element.35.refs_1_), channel_id=1, source_target_pairs={{0,1},{1,0},{2,3},{3,2},{4,5},{5,4},{6,7},{7,6},{8,9},{9,8},{10,11... | collective-permute-start | bytes 442376 | tf_op jit(solution)/shard_map/ppermute | solution.py:840
  10.7 10.4 %collective-permute-start.2 = (bf16[80,512]{1,0:T(8,128)(2,1)}, bf16[80,512]{1,0:T(8,128)(2,1)S(1)}, u32[]{:S(2)}, u32[]{:S(2)}) collective-permute-start(bf16[80,512]{1,0:T(8,128)(2,1)} %get-tuple-element.36), channel_id=1, source_target_pairs={{0,66},{1,67},{2,68},{3,69},{4,70},{5,71},{6,72},{7,73},{8,74},{9,... | collective-permute-start | bytes 245768 | tf_op jit(solution)/shard_map/ppermute | solution.py:840
  10.7 10.3 %collective-permute-start.3 = (bf16[64,512]{1,0:T(8,128)(2,1)}, bf16[64,512]{1,0:T(8,128)(2,1)S(1)}, u32[]{:S(2)}, u32[]{:S(2)}) collective-permute-start(bf16[64,512]{1,0:T(8,128)(2,1)} %get-tuple-element.37), channel_id=1, source_target_pairs={{0,62},{1,63},{2,0},{3,1},{4,2},{5,3},{6,4},{7,5},{8,6},{9,7},{10,... | collective-permute-start | bytes 196616 | tf_op jit(solution)/shard_map/ppermute | solution.py:840
  21.0 0.6 copy-start.5
  21.0 0.6 copy-start.4
  21.1 0.7 copy-start.2
  21.1 0.7 copy-start.3
  50.3 4.8 %collective-permute-start.4 = (bf16[64,136,128]{2,1,0:T(8,128)(2,1)}, bf16[64,136,128]{2,1,0:T(8,128)(2,1)S(1)}, u32[]{:S(2)}, u32[]{:S(2)}) collective-permute-start(bf16[64,136,128]{2,1,0:T(8,128)(2,1)} %get-tuple-element.43), channel_id=1, source_target_pairs={{0,1},{1,0},{2,3},{3,2},{4,5},{5,4},{6,7},{7,6},{8,9},{9,8},{10,11... | collective-permute-start | bytes 6684680 | tf_op jit(solution)/shard_map/ppermute | solution.py:840
  51.0 7.8 %collective-permute-start.5 = (f32[84,512]{1,0:T(8,128)}, f32[84,512]{1,0:T(8,128)S(1)}, u32[]{:S(2)}, u32[]{:S(2)}) collective-permute-start(f32[84,512]{1,0:T(8,128)} %get-tuple-element.44), channel_id=1, source_target_pairs={{0,64},{1,65},{2,66},{3,67},{4,68},{5,69},{6,70},{7,71},{8,72},{9,... | collective-permute-start | bytes 516104 | tf_op jit(solution)/shard_map/ppermute | solution.py:840
  57.4 38.5 %copy-start = (f32[84,512]{1,0:T(8,128)S(1)}, f32[84,512]{1,0:T(8,128)}, u32[]{:S(2)}) copy-start(f32[84,512]{1,0:T(8,128)} %get-tuple-element.46.pred_own_hbm) | copy-start | bytes 516100
  96.4 43.6 %copy-start.1 = (f32[2,32,128]{2,1,0:T(8,128)S(1)}, f32[2,32,128]{2,1,0:T(8,128)}, u32[]{:S(2)}) copy-start(f32[2,32,128]{2,1,0:T(8,128)} %get-tuple-element.50.noise) | copy-start | bytes 98308
  133.5 6.5 %collective-permute-start.6 = (bf16[64,136,128]{2,1,0:T(8,128)(2,1)S(1)}, bf16[64,136,128]{2,1,0:T(8,128)(2,1)S(1)}, u32[]{:S(2)}, u32[]{:S(2)}) collective-permute-start(bf16[64,136,128]{2,1,0:T(8,128)(2,1)S(1)} %all_to_all.11.mine_hbm), channel_id=1, source_target_pairs={{0,1},{1,0},{2,3},{3,2},{4,5},{5,4},{6,7},{7,6},{8,9},{9,8},{10,11... | collective-permute-start | bytes 6684680 | tf_op jit(solution)/shard_map/ppermute | solution.py:840

commit v5 on v4

--- a/solution.py
+++ b/solution.py
@@ -717,77 +717,82 @@
         copy.wait()
 
 
-def unpack_kernel(
-    mine_hbm,
-    theirs_hbm,
-    noise,
-    grad_scale,
-    grad_shift,
-    grad_qkv,
-    grad_attn_out,
-    grad_dec_query,
-    grad_dec_kv,
-    grad_dec_out,
-    grad_head,
-    loss,
-    grads,
-    sems,
-):
+def unpack_kernel(*refs, own_half):
+    data, noise = refs[:2]
+    outputs, scratch = (refs[2:11], refs[11:]) if own_half else (refs[11:20], refs[20:])
+    grad_scale, grad_shift, grad_qkv, grad_attn_out = outputs[:4]
+    grad_dec_query, grad_dec_kv, grad_dec_out, grad_head, loss = outputs[4:]
+    blocks, cond, head, tail, sems = scratch
     member = lax.axis_index("member")
     core = lax.rem(lax.axis_index("space"), 2)
-    channels = grad_head.shape[0]
-    dim = grad_attn_out.shape[0]
+    half = core if own_half else 1 - core
+    channels, dim = grad_head.shape
     heads = dim // HEAD
-    copies = [
-        pltpu.make_async_copy(mine_hbm, grads.at[core], sems.at[0]),
-        pltpu.make_async_copy(theirs_hbm, grads.at[1 - core], sems.at[1]),
-    ]
-    for copy in copies:
+    tall = HEAD * HEAD // dim
+    per_block = dim // tall
+    targets = (
+        (
+            grad_qkv.at[:, :dim],
+            grad_qkv.at[:, dim : 2 * dim],
+            grad_qkv.at[:, 2 * dim :],
+            grad_attn_out,
+        ),
+        (grad_dec_query, grad_dec_kv.at[:, :dim], grad_dec_kv.at[:, dim:], grad_dec_out),
+    )
+
+    def block_copy(which, i):
+        return pltpu.make_async_copy(blocks.at[i], targets[which][i], sems.at[i])
+
+    for i in range(4):
+
+        @pl.loop(0, per_block, unroll=2)
+        def _(c):
+            tile = pl.ds(pl.multiple_of(c * tall, tall), tall)
+            for t in range(heads):
+                blocks[i, tile, t * HEAD : (t + 1) * HEAD] = data[
+                    i * per_block + c, t * tall : (t + 1) * tall, :
+                ].astype(F32)
+
+        for which in range(2):
+            pl.when(half == which)(block_copy(which, i).start)
+
+    def extra(i):
+        return jnp.concatenate(
+            [data[i * heads + t, HEAD:, :].astype(F32) for t in range(heads)], axis=1
+        )
+
+    @pl.when(half == 0)
+    def _():
+        sums = extra(0)
+        for k in range(2):
+            first = sums[2 * k : 2 * k + 1]
+            second = sums[2 * k + 1 : 2 * k + 2]
+            mine = jnp.where(member == 0, first, second)
+            other = jnp.where(member == 0, second, first)
+            cond[k] = noise[0, :, :1] * mine + noise[1, :, :1] * other
+        tail[...] = sums[4:5, :HEAD]
+        copies = [
+            pltpu.make_async_copy(cond.at[0], grad_scale, sems.at[4]),
+            pltpu.make_async_copy(cond.at[1], grad_shift, sems.at[5]),
+            pltpu.make_async_copy(tail, loss, sems.at[6]),
+        ]
+        for copy in copies:
+            copy.start()
+        for copy in copies:
+            copy.wait()
+
+    @pl.when(half == 1)
+    def _():
+        for i in range(-(-channels // 8)):
+            count = min(8, channels - i * 8)
+            head[i * 8 : i * 8 + count] = extra(i)[:count]
+        copy = pltpu.make_async_copy(head, grad_head, sems.at[4])
         copy.start()
-    for copy in copies:
         copy.wait()
-    tall = HEAD * HEAD // dim
-    targets = (
-        (grad_qkv, 0),
-        (grad_qkv, dim),
-        (grad_qkv, 2 * dim),
-        (grad_attn_out, 0),
-        (grad_dec_query, 0),
-        (grad_dec_kv, 0),
-        (grad_dec_kv, dim),
-        (grad_dec_out, 0),
-    )
-    per_block = dim // tall
-
-    @pl.loop(0, per_block)
-    def _(c):
-        tile = pl.ds(pl.multiple_of(c * tall, tall), tall)
-        for i, (ref, col) in enumerate(targets):
-            for t in range(heads):
-                ref[tile, col + t * HEAD : col + (t + 1) * HEAD] = grads[
-                    i // 4, i % 4 * per_block + c, t * tall : (t + 1) * tall, :
-                ].astype(F32)
-
-    def extra(half, i):
-        return jnp.concatenate(
-            [grads[half, i * heads + t, HEAD:, :].astype(F32) for t in range(heads)], axis=1
-        )
-
-    for i in range(-(-channels // 8)):
-        count = min(8, channels - i * 8)
-        grad_head[i * 8 : i * 8 + count] = extra(1, i)[:count]
-    cond = extra(0, 0)
-    first = cond[0:1]
-    second = cond[1:2]
-    grad_scale[...] = noise[0, :, :1] * jnp.where(member == 0, first, second) + noise[
-        1, :, :1
-    ] * jnp.where(member == 0, second, first)
-    first = cond[2:3]
-    second = cond[3:4]
-    grad_shift[...] = noise[0, :, :1] * jnp.where(member == 0, first, second) + noise[
-        1, :, :1
-    ] * jnp.where(member == 0, second, first)
-    loss[...] = cond[4:5, :HEAD]
+
+    for i in range(4):
+        for which in range(2):
+            pl.when(half == which)(block_copy(which, i).wait)
 
 
 def whole(shape):
@@ -1031,15 +1036,31 @@
             (1, HEAD),
         )
     ]
-    outputs = pl.pallas_call(
-        unpack_kernel,
-        in_specs=[pl.BlockSpec(memory_space=pl.ANY)] * 2 + [vmem],
-        out_specs=[vmem] * 9,
-        out_shape=grad_shapes,
-        scratch_shapes=[pltpu.VMEM((2, *half_shape), BF16), pltpu.SemaphoreType.DMA((2,))],
-        compiler_params=pltpu.CompilerParams(vmem_limit_bytes=40 * 2**20),
-        name="unpack",
-    )(mine, theirs, noise)
+    anywhere = pl.BlockSpec(memory_space=pl.ANY)
+
+    def unpack(own_half, data, outputs):
+        return pl.pallas_call(
+            lambda *refs: unpack_kernel(*refs, own_half=own_half),
+            in_specs=[vmem, vmem] + [anywhere] * len(outputs),
+            out_specs=[anywhere] * 9,
+            out_shape=grad_shapes,
+            scratch_shapes=[
+                pltpu.VMEM((4, dim, dim), F32),
+                pltpu.VMEM((2, *cond_scale.shape), F32),
+                pltpu.VMEM(head_out.shape, F32),
+                pltpu.VMEM((1, HEAD), F32),
+                pltpu.SemaphoreType.DMA((7,)),
+            ],
+            input_output_aliases={2 + i: i for i in range(len(outputs))},
+            compiler_params=pltpu.CompilerParams(vmem_limit_bytes=32 * 2**20),
+            cost_estimate=pl.CostEstimate(
+                flops=0, bytes_accessed=7 * 2**20, transcendentals=0
+            ),
+            name="unpack_mine" if own_half else "unpack_theirs",
+        )(data, noise, *outputs)
+
+    outputs = unpack(True, mine, ())
+    outputs = unpack(False, theirs, tuple(outputs))
     return (prediction, *outputs[:8], outputs[8][0, 0])
 
 

time: 145 us -> 143 us (0.986)
  waiting for transfers between devices: 6.76 us -> 4.54 us
    ppermute x7, waiting for transfers between devices: 6.76 us -> 4.54 us  [permute(): return lax.ppermute(value, axes, pairs)]
    pallas_call x1 -> x2, Pallas kernels: 4.68 us -> 4.42 us  [unpack(): pl.pallas_call(lambda *refs: unpack_kernel(*refs, own_half=own_half), in_...]
  transfers between devices with their start and end apart: 7 -> 7, of which waited for: 3 -> 3; matrix products, arithmetic and copies ran while one was open for 2% -> 2% of each run, Pallas kernels for 2% -> 4%
where the time goes in v5:
time: 143 us; the launch traced here: 142 us
  blocking collectives  74.2 us (52%)
  Pallas kernels  38.4 us (27%)
  starting transfers between devices  19.6 us (14%)
  waiting for transfers between devices  4.54 us (3%)
  other arithmetic  2.2 us (2%)
  local copies, waits for them, and re-layouts  1.79 us (1%)
  between operations  1.6 us (1%)
    all_to_all x2, blocking collectives, over_chips(): return lax.all_to_all(value, axes, 0, 0, axis_index_groups=groups)  74.2 us
    pallas_call x1, Pallas kernels, per_device(): pl.pallas_call(lambda *refs: step_kernel(*refs, scale_den=scale_den), in_...  28.5 us
    ppermute x7, starting transfers between devices, permute(): return lax.ppermute(value, axes, pairs)  19.6 us
    ppermute x7, waiting for transfers between devices, permute(): return lax.ppermute(value, axes, pairs)  4.54 us
    pallas_call x2, Pallas kernels, unpack(): pl.pallas_call(lambda *refs: unpack_kernel(*refs, own_half=own_half), in_...  4.42 us
    pallas_call x1, Pallas kernels, per_device(): pl.pallas_call(lambda *refs: prepare_kernel(*refs, rows=rows, halo=halo,...  3.34 us
  transfers between devices with their start and end apart: 7, of which 3 were waited for; matrix products, arithmetic and copies ran while one was open for 2% of the time, Pallas kernels for 4%

profile of v5, /device:TPU:1, one launch (start us, length us, event | category | flops | bytes accessed | tf_op | source)
XLA Modules:
  0.0 142.4 jit_solution(2512898665366099804)
XLA Ops:
  0.6 1.7 %pack.1 = (bf16[144,512]{1,0:T(8,128)(2,1)}, bf16[80,512]{1,0:T(8,128)(2,1)}, bf16[64,512]{1,0:T(8,128)(2,1)}) custom-call(bf16[128,512]{1,0:T(8,128)(2,1)} %refs_0_.3, s32[16,128]{1,0:T(8,128)} %refs_1_.2, f32[16,128]{1,0:T(8,128)} %refs_2_.2, f32[1,32]{1,0:T(1,128)} %refs_6_.1), custom_call_target="tpu_custom_call" | custom-call | tf_op jit(solution)/shard_map/pack/pallas_call | solution.py:850
  2.3 2.6 %collective-permute-start.1 = (bf16[144,512]{1,0:T(8,128)(2,1)}, bf16[144,512]{1,0:T(8,128)(2,1)S(1)}, u32[]{:S(2)}, u32[]{:S(2)}) collective-permute-start(bf16[144,512]{1,0:T(8,128)(2,1)} %get-tuple-element.44.refs_1_), channel_id=1, source_target_pairs={{0,63},{1,2},{2,1},{3,4},{4,3},{5,6},{6,5},{7,8},{8,7},{9,10},{10,... | collective-permute-start | bytes 442376 | tf_op jit(solution)/shard_map/ppermute | solution.py:845
  4.9 5.8 %collective-permute-start = (bf16[144,512]{1,0:T(8,128)(2,1)}, bf16[144,512]{1,0:T(8,128)(2,1)S(1)}, u32[]{:S(2)}, u32[]{:S(2)}) collective-permute-start(bf16[144,512]{1,0:T(8,128)(2,1)} %get-tuple-element.44.refs_1_), channel_id=1, source_target_pairs={{0,1},{1,0},{2,3},{3,2},{4,5},{5,4},{6,7},{7,6},{8,9},{9,8},{10,11... | collective-permute-start | bytes 442376 | tf_op jit(solution)/shard_map/ppermute | solution.py:845
  10.7 0.0 collective-permute-start.2
  10.7 6.3 %collective-permute-start.3 = (bf16[64,512]{1,0:T(8,128)(2,1)}, bf16[64,512]{1,0:T(8,128)(2,1)S(1)}, u32[]{:S(2)}, u32[]{:S(2)}) collective-permute-start(bf16[64,512]{1,0:T(8,128)(2,1)} %get-tuple-element.46), channel_id=1, source_target_pairs={{0,62},{1,63},{2,0},{3,1},{4,2},{5,3},{6,4},{7,5},{8,6},{9,7},{10,... | collective-permute-start | bytes 196616 | tf_op jit(solution)/shard_map/ppermute | solution.py:845
  17.7 3.3 %prepare.1 = (bf16[512,512]{1,0:T(8,128)(2,1)}, bf16[512,512]{1,0:T(8,128)(2,1)}, bf16[512,512]{1,0:T(8,128)(2,1)}, f32[256,512]{1,0:T(8,128)}) custom-call(bf16[1024,512]{1,0:T(8,128)(2,1)} %refs_0_.4, s32[3,1024]{1,0:T(4,128)} %refs_1_.3, f32[3,1024]{1,0:T(4,128)} %refs_2_.3, bf16[512,512]{1,0:T(8,128)(2,1)} %refs_3_.3), custom_call_target="tpu_custom_call" | custom-call | flops 268435456 | bytes 3145728 | tf_op jit(solution)/shard_map/prepare/pallas_call | solution.py:867
  21.0 0.0 collective-permute-done.3.refs_5_
  21.0 0.0 copy-start.5
  21.0 0.0 collective-permute-done.2.refs_4_
  21.0 0.0 copy-start.4
  21.0 0.0 collective-permute-done.1.refs_3_
  21.1 0.0 copy-start.2
  21.1 0.0 collective-permute-done.refs_2_
  21.1 0.0 copy-start.3
  21.1 0.6 copy-done.5
  21.6 0.0 copy-done.4
  21.7 0.1 copy-done.2
  21.7 0.1 copy-done.3
  21.8 28.5 %step.1 = (f32[84,512]{1,0:T(8,128)}, f32[84,512]{1,0:T(8,128)}, bf16[64,136,128]{2,1,0:T(8,128)(2,1)}, bf16[64,136,128]{2,1,0:T(8,128)(2,1)}, f32[2,32,128]{2,1,0:T(8,128)}) custom-call(s32[1]{0:T(128)S(6)} %copy.48.refs_0_, bf16[144,512]{1,0:T(8,128)(2,1)} %get-tuple-element.44.refs_1_, bf16[144,512]{1,0:T(8,128)(2,1)} %copy-done.3, ...), custom_call_target="tpu_custom_call" | custom-call | flops 10000000000 | bytes 12582912 | tf_op jit(solution)/shard_map/step/pallas_call | solution.py:917
  50.3 0.6 collective-permute-start.4
  51.0 1.7 %collective-permute-start.5 = (f32[84,512]{1,0:T(8,128)}, f32[84,512]{1,0:T(8,128)S(1)}, u32[]{:S(2)}, u32[]{:S(2)}) collective-permute-start(f32[84,512]{1,0:T(8,128)} %get-tuple-element.53), channel_id=1, source_target_pairs={{0,64},{1,65},{2,66},{3,67},{4,68},{5,69},{6,70},{7,71},{8,72},{9,... | collective-permute-start | bytes 516104 | tf_op jit(solution)/shard_map/ppermute | solution.py:845
  52.7 2.4 %collective-permute-done.4 = bf16[64,136,128]{2,1,0:T(8,128)(2,1)S(1)} collective-permute-done((bf16[64,136,128]{2,1,0:T(8,128)(2,1)}, bf16[64,136,128]{2,1,0:T(8,128)(2,1)S(1)}, u32[]{:S(2)}, u32[]{:S(2)}) %collective-permute-start.4) | collective-permute-done | bytes 2228256 | tf_op jit(solution)/shard_map/ppermute | solution.py:845
  55.1 2.2 %add_convert_fusion = bf16[64,136,128]{2,1,0:T(8,128)(2,1)S(1)} fusion(bf16[64,136,128]{2,1,0:T(8,128)(2,1)S(1)} %collective-permute-done.4, bf16[64,136,128]{2,1,0:T(8,128)(2,1)} %get-tuple-element.51), kind=kLoop, calls=%fused_computation | loop fusion | flops 4456448 | bytes 6684672 | tf_op jit(solution)/shard_map/convert_element_type | solution.py:1008
  57.4 0.0 copy-start
  57.4 1.4 collective-permute-done.5.pred_arrived_hbm
  58.8 37.1 %all_to_all.10.parts = bf16[64,136,128]{2,1,0:T(8,128)(2,1)S(1)} all-to-all(bf16[64,136,128]{2,1,0:T(8,128)(2,1)S(1)} %add_convert_fusion), channel_id=1, replica_groups={{0,2,4,6,8,10,12,14,16,18,20,22,24,26,28,30,32,34,36,38,40,42,44,46,48,..., dimensions={0} | all-to-all | bytes 4456448 | tf_op jit(solution)/shard_map/all_to_all | solution.py:1005
  95.9 0.0 copy-done
  95.9 0.5 sum.1
  96.4 0.0 copy-start.1
  96.4 37.1 %all_to_all.11.refs_0_ = bf16[64,136,128]{2,1,0:T(8,128)(2,1)S(1)} all-to-all(bf16[64,136,128]{2,1,0:T(8,128)(2,1)S(1)} %get-tuple-element.58), channel_id=1, replica_groups={{0,2,4,6,8,10,12,14,16,18,20,22,24,26,28,30,32,34,36,38,40,42,44,46,48,..., dimensions={0} | all-to-all | bytes 4456448 | tf_op jit(solution)/shard_map/all_to_all | solution.py:1005
  133.5 2.5 %collective-permute-start.6 = (bf16[64,136,128]{2,1,0:T(8,128)(2,1)S(1)}, bf16[64,136,128]{2,1,0:T(8,128)(2,1)S(1)}, u32[]{:S(2)}, u32[]{:S(2)}) collective-permute-start(bf16[64,136,128]{2,1,0:T(8,128)(2,1)S(1)} %all_to_all.11.refs_0_), channel_id=1, source_target_pairs={{0,1},{1,0},{2,3},{3,2},{4,5},{5,4},{6,7},{7,6},{8,9},{9,8},{10,11... | collective-permute-start | bytes 6684680 | tf_op jit(solution)/shard_map/ppermute | solution.py:845
  136.0 1.1 copy.38
  137.1 0.0 copy-done.1
  137.1 2.2 %unpack_mine.1 = (f32[32,512]{1,0:T(8,128)}, f32[32,512]{1,0:T(8,128)}, f32[512,1536]{1,0:T(8,128)}, f32[512,512]{1,0:T(8,128)}, f32[512,512]{1,0:T(8,128)}, /*i...) custom-call(bf16[64,136,128]{2,1,0:T(8,128)(2,1)S(1)} %all_to_all.11.refs_0_, ...), custom_call_target="tpu_custom_call" | custom-call | bytes 7340032 | tf_op jit(solution)/shard_map/unpack_mine/pallas_call | solution.py:1042
  139.3 0.7 collective-permute-done.6.refs_0_
  140.0 2.2 %unpack_theirs.1 = (f32[32,512]{1,0:T(8,128)}, f32[32,512]{1,0:T(8,128)}, f32[512,1536]{1,0:T(8,128)}, f32[512,512]{1,0:T(8,128)}, f32[512,512]{1,0:T(8,128)}, /...) custom-call(bf16[64,136,128]{2,1,0:T(8,128)(2,1)S(1)} %collective-pe, ...), custom_call_target="tpu_custom_call", output_to_operand_aliasing={{0}: (2, {}), {1}: (3, {}), {2}: (4, {}), {3}: (5, {}), {4}... | custom-call | bytes 7340032 | tf_op jit(solution)/shard_map/unpack_theirs/pallas_call | solution.py:1042
Async XLA Ops:
  2.3 18.8 %collective-permute-start.1 = (bf16[144,512]{1,0:T(8,128)(2,1)}, bf16[144,512]{1,0:T(8,128)(2,1)S(1)}, u32[]{:S(2)}, u32[]{:S(2)}) collective-permute-start(bf16[144,512]{1,0:T(8,128)(2,1)} %get-tuple-element.44.refs_1_), channel_id=1, source_target_pairs={{0,63},{1,2},{2,1},{3,4},{4,3},{5,6},{6,5},{7,8},{8,7},{9,10},{10,... | collective-permute-start | bytes 442376 | tf_op jit(solution)/shard_map/ppermute | solution.py:845
  4.9 16.2 %collective-permute-start = (bf16[144,512]{1,0:T(8,128)(2,1)}, bf16[144,512]{1,0:T(8,128)(2,1)S(1)}, u32[]{:S(2)}, u32[]{:S(2)}) collective-permute-start(bf16[144,512]{1,0:T(8,128)(2,1)} %get-tuple-element.44.refs_1_), channel_id=1, source_target_pairs={{0,1},{1,0},{2,3},{3,2},{4,5},{5,4},{6,7},{7,6},{8,9},{9,8},{10,11... | collective-permute-start | bytes 442376 | tf_op jit(solution)/shard_map/ppermute | solution.py:845
  10.7 10.4 %collective-permute-start.2 = (bf16[80,512]{1,0:T(8,128)(2,1)}, bf16[80,512]{1,0:T(8,128)(2,1)S(1)}, u32[]{:S(2)}, u32[]{:S(2)}) collective-permute-start(bf16[80,512]{1,0:T(8,128)(2,1)} %get-tuple-element.45), channel_id=1, source_target_pairs={{0,66},{1,67},{2,68},{3,69},{4,70},{5,71},{6,72},{7,73},{8,74},{9,... | collective-permute-start | bytes 245768 | tf_op jit(solution)/shard_map/ppermute | solution.py:845
  10.7 10.3 %collective-permute-start.3 = (bf16[64,512]{1,0:T(8,128)(2,1)}, bf16[64,512]{1,0:T(8,128)(2,1)S(1)}, u32[]{:S(2)}, u32[]{:S(2)}) collective-permute-start(bf16[64,512]{1,0:T(8,128)(2,1)} %get-tuple-element.46), channel_id=1, source_target_pairs={{0,62},{1,63},{2,0},{3,1},{4,2},{5,3},{6,4},{7,5},{8,6},{9,7},{10,... | collective-permute-start | bytes 196616 | tf_op jit(solution)/shard_map/ppermute | solution.py:845
  21.0 0.6 copy-start.5
  21.0 0.6 copy-start.4
  21.1 0.7 copy-start.2
  21.1 0.7 copy-start.3
  50.3 4.8 %collective-permute-start.4 = (bf16[64,136,128]{2,1,0:T(8,128)(2,1)}, bf16[64,136,128]{2,1,0:T(8,128)(2,1)S(1)}, u32[]{:S(2)}, u32[]{:S(2)}) collective-permute-start(bf16[64,136,128]{2,1,0:T(8,128)(2,1)} %get-tuple-element.52), channel_id=1, source_target_pairs={{0,1},{1,0},{2,3},{3,2},{4,5},{5,4},{6,7},{7,6},{8,9},{9,8},{10,11... | collective-permute-start | bytes 6684680 | tf_op jit(solution)/shard_map/ppermute | solution.py:845
  51.0 7.8 %collective-permute-start.5 = (f32[84,512]{1,0:T(8,128)}, f32[84,512]{1,0:T(8,128)S(1)}, u32[]{:S(2)}, u32[]{:S(2)}) collective-permute-start(f32[84,512]{1,0:T(8,128)} %get-tuple-element.53), channel_id=1, source_target_pairs={{0,64},{1,65},{2,66},{3,67},{4,68},{5,69},{6,70},{7,71},{8,72},{9,... | collective-permute-start | bytes 516104 | tf_op jit(solution)/shard_map/ppermute | solution.py:845
  57.4 38.5 %copy-start = (f32[84,512]{1,0:T(8,128)S(1)}, f32[84,512]{1,0:T(8,128)}, u32[]{:S(2)}) copy-start(f32[84,512]{1,0:T(8,128)} %get-tuple-element.55.pred_own_hbm) | copy-start | bytes 516100
  96.4 40.7 %copy-start.1 = (f32[2,32,128]{2,1,0:T(8,128)S(1)}, f32[2,32,128]{2,1,0:T(8,128)}, u32[]{:S(2)}) copy-start(f32[2,32,128]{2,1,0:T(8,128)} %get-tuple-element.59.refs_1_) | copy-start | bytes 98308
  133.5 6.5 %collective-permute-start.6 = (bf16[64,136,128]{2,1,0:T(8,128)(2,1)S(1)}, bf16[64,136,128]{2,1,0:T(8,128)(2,1)S(1)}, u32[]{:S(2)}, u32[]{:S(2)}) collective-permute-start(bf16[64,136,128]{2,1,0:T(8,128)(2,1)S(1)} %all_to_all.11.refs_0_), channel_id=1, source_target_pairs={{0,1},{1,0},{2,3},{3,2},{4,5},{5,4},{6,7},{7,6},{8,9},{9,8},{10,11... | collective-permute-start | bytes 6684680 | tf_op jit(solution)/shard_map/ppermute | solution.py:845

commit v6 on v5

--- a/solution.py
+++ b/solution.py
@@ -58,15 +58,6 @@
     return logits
 
 
-def add_entry(slots, bias, entry, logits):
-    place = slots[pl.ds(entry, 1), :]
-    same = slots[...] == place
-    top = jnp.max(jnp.where(same, bias[...], FAR), axis=0, keepdims=True)
-    terms = jnp.sum(jnp.where(same, jnp.exp(bias[...] - top), 0.0), axis=0, keepdims=True)
-    row_ids = lax.broadcasted_iota(jnp.int32, logits.shape, 0)
-    logits[...] = jnp.where(row_ids == place, (top + jnp.log(terms)) * LOG2E, logits[...])
-
-
 def softmax_rows(scores):
     terms = jnp.exp2(scores - jnp.max(scores, axis=0, keepdims=True))
     return terms * (1.0 / jnp.sum(terms, axis=0, keepdims=True))
@@ -94,19 +85,27 @@
     return lax.axis_index("space") * rows - rows // 2
 
 
-def pack_kernel(latent, nbrs, bias, noise, packet, upward, downward, *, total):
+def pack_kernel(latent, nbrs, bias, packet, *, total):
     rows = latent.shape[0]
-    halo = rows // 2
     packet[:rows] = latent[...]
-    downward[...] = latent[:halo]
     slots = ((nbrs[...] - window_start(rows)) & (total - 1)).astype(F32).astype(BF16)
     packet[rows:] = jnp.concatenate([slots, *split_terms(bias[...])], axis=1)
-    upward[:halo] = latent[halo:]
+
+
+def is_odd():
+    return lax.rem(lax.axis_index("space"), 2) == 1
+
+
+def outward_kernel(packet, twin, noise, outward, *, rows):
+    halo = rows // 2
+    size = packet.shape[0]
+    outward[:size] = packet[...]
+    outward[size : size + halo] = jnp.where(is_odd(), twin[halo:rows], twin[:halo])
     spare = jnp.zeros((1, rows - noise.shape[1]), F32)
     padded = jnp.concatenate([noise[...], spare], axis=1)
-    padded = jnp.broadcast_to(padded, (upward.shape[0] - halo, rows))
+    padded = jnp.broadcast_to(padded, (outward.shape[0] - size - halo, rows))
     terms = split_terms(padded)
-    upward[halo:] = jnp.concatenate([*terms, jnp.zeros_like(terms[0])], axis=1)
+    outward[size + halo :] = jnp.concatenate([*terms, jnp.zeros_like(terms[0])], axis=1)
 
 
 def prepare_kernel(
@@ -114,6 +113,7 @@
     nbrs_hbm,
     bias_hbm,
     weight_hbm,
+    _,
     embed_t,
     norm_t,
     query_t,
@@ -145,7 +145,9 @@
     places = jnp.where(
         local < halo, local + rows, jnp.where(local < halo + rows, local - halo, local)
     )
-    logits[...] = spread_bias(places, bias[...], rows + 2 * halo)
+    for part in range(slots // HEAD):
+        lanes = slice(part * HEAD, (part + 1) * HEAD)
+        logits[:, lanes] = spread_bias(places[:, lanes], bias[:, lanes], rows + 2 * halo)
     copies[0].wait()
     copies[3].wait()
     weight_t[...] = dec_query[...].T
@@ -185,8 +187,7 @@
     packet,
     twin,
     beside,
-    below,
-    above,
+    relay,
     noise_own,
     embed_hbm,
     norm_hbm,
@@ -268,10 +269,11 @@
     load_sems,
     store_sems,
     *,
+    rows,
     scale_den,
 ):
-    halo, dim = above.shape
-    rows = 2 * halo
+    size, dim = packet.shape
+    halo = rows // 2
     window = rows + 2 * halo
     outer = 2 * window
     own = packet[:rows]
@@ -310,16 +312,19 @@
     load("norm", norm_hbm, norm_t)
     start("qkv", "scale", "shift")
 
-    odd = core == 1
-    latent[0:halo] = below[:halo]
+    odd = is_odd()
+    far = slice(size, size + halo)
+    latent[0:halo] = jnp.where(odd, relay[halo:rows], beside[far])
     latent[halo : halo + rows] = jnp.where(odd, twin[:rows], beside[:rows])
     latent[halo + rows : halo + 2 * rows] = own
     latent[halo + 2 * rows : halo + 3 * rows] = jnp.where(odd, beside[:rows], twin[:rows])
-    latent[halo + 3 * rows :] = above[...]
+    latent[halo + 3 * rows :] = jnp.where(odd, beside[far], relay[:halo])
     lane = lax.broadcasted_iota(jnp.int32, (edges.shape[0], rows), 1)
     late = (lane >= halo) == odd
     ends = jnp.where(
-        jnp.concatenate([late] * 4, axis=1), twin[rows:].astype(F32), beside[rows:].astype(F32)
+        jnp.concatenate([late] * 4, axis=1),
+        twin[rows:size].astype(F32),
+        beside[rows:size].astype(F32),
     )
     lists = edges.astype(F32)
 
@@ -331,13 +336,14 @@
 
     list_slots[...] = jnp.concatenate(listed(0), axis=1).astype(jnp.int32)
     list_bias[...] = joined_terms(*(jnp.concatenate(listed(part), axis=1) for part in (1, 2, 3)))
-    mesh_logits[...] = jnp.full(mesh_logits.shape, FAR, F32)
-
-    @pl.loop(0, list_slots.shape[0])
-    def _(entry):
-        add_entry(list_slots, list_bias, entry, mesh_logits)
-
-    noise_row = joined_terms(*(below[halo:, part * rows : (part + 1) * rows] for part in (0, 1, 2)))
+    for part in range(2):
+        lanes = slice(part * rows, (part + 1) * rows)
+        mesh_logits[:, lanes] = spread_bias(list_slots[:, lanes], list_bias[:, lanes], window)
+
+    noise_rows = jnp.where(odd, relay[size + halo :], beside[size + halo :])
+    noise_row = joined_terms(
+        *(noise_rows[:, part * rows : (part + 1) * rows] for part in (0, 1, 2))
+    )
     spread = cond_scale.shape[0]
     own_row = jnp.concatenate([noise_own[...], jnp.zeros((1, rows - spread), F32)], axis=1)
     noise = []
@@ -847,26 +853,27 @@
     smem = pl.BlockSpec(memory_space=pltpu.SMEM)
     vmem = pl.BlockSpec(memory_space=pltpu.VMEM)
     hbm = pl.BlockSpec(memory_space=pltpu.HBM)
-    packet, upward, downward = pl.pallas_call(
+    packet = pl.pallas_call(
         lambda *refs: pack_kernel(*refs, total=total),
-        in_specs=[vmem] * 4,
-        out_shape=[
-            jax.ShapeDtypeStruct((rows + mesh_nbrs.shape[0], dim), BF16),
-            jax.ShapeDtypeStruct((halo + 16, dim), BF16),
-            jax.ShapeDtypeStruct((halo, dim), BF16),
-        ],
+        in_specs=[vmem] * 3,
+        out_shape=jax.ShapeDtypeStruct((rows + mesh_nbrs.shape[0], dim), BF16),
         compiler_params=pltpu.CompilerParams(vmem_limit_bytes=ALL_VMEM),
         name="pack",
-    )(mesh_latent, mesh_nbrs, mesh_bias, member_noise)
+    )(mesh_latent, mesh_nbrs, mesh_bias)
     twin = permute(packet, lambda m, k: (m, k ^ 1))
-    beside = permute(packet, lambda m, k: (m, k + 1 if k % 2 else k - 1))
-    below = permute(upward, lambda m, k: (1 - m, k + 2))
-    above = permute(downward, lambda m, k: (m, k - 2))
+    outward = pl.pallas_call(
+        lambda *refs: outward_kernel(*refs, rows=rows),
+        in_specs=[vmem] * 3,
+        out_shape=jax.ShapeDtypeStruct((packet.shape[0] + halo + 16, dim), BF16),
+        compiler_params=pltpu.CompilerParams(vmem_limit_bytes=32 * 2**20),
+        name="outward",
+    )(packet, twin, member_noise)
+    beside = permute(outward, lambda m, k: (1 - m, k + 1) if k % 2 else (m, k - 1))
 
     square = (dim, slots)
     embed_t, norm_t, query_t, grid_logits = pl.pallas_call(
         lambda *refs: prepare_kernel(*refs, rows=rows, halo=halo, total=total),
-        in_specs=[hbm] * 4,
+        in_specs=[hbm] * 5,
         out_specs=[vmem] * 4,
         out_shape=[
             jax.ShapeDtypeStruct(square, BF16),
@@ -887,7 +894,9 @@
             flops=2 * dim * dim * slots, bytes_accessed=3 * 2**20, transcendentals=0
         ),
         name="prepare",
-    )(grid_embed, grid_nbrs, grid_bias, dec_query)
+    )(grid_embed, grid_nbrs, grid_bias, dec_query, outward)
+    beside, embed_t = lax.optimization_barrier((beside, embed_t))
+    relay = permute(beside, lambda m, k: (m, k ^ 1))
 
     channel_pad = -(-channels // 32) * 32
     chunks = size
@@ -896,8 +905,7 @@
         packet,
         twin,
         beside,
-        below,
-        above,
+        relay,
         member_noise,
         embed_t,
         norm_t,
@@ -915,8 +923,8 @@
         head_out,
     )
     pred_own, pred_other, keep, send, noise = pl.pallas_call(
-        lambda *refs: step_kernel(*refs, scale_den=scale_den),
-        in_specs=[smem] + [vmem] * 6 + [pl.BlockSpec(memory_space=pl.ANY)] * 4 + [hbm] * 10,
+        lambda *refs: step_kernel(*refs, rows=rows, scale_den=scale_den),
+        in_specs=[smem] + [vmem] * 5 + [pl.BlockSpec(memory_space=pl.ANY)] * 4 + [hbm] * 10,
         out_specs=[hbm] * 4 + [vmem],
         scratch_shapes=[
             pltpu.VMEM(square, BF16),

time: 143 us -> 142 us (level)
  starting transfers between devices: 19.6 us -> 14.8 us
  waiting for transfers between devices: 4.54 us -> 6.85 us
  local copies, waits for them, and re-layouts: 1.79 us -> 3.36 us
    ppermute x7 -> x6, starting transfers between devices: 19.6 us -> 14.8 us  [permute(): return lax.ppermute(value, axes, pairs)]
    ppermute x7 -> x6, waiting for transfers between devices: 4.54 us -> 6.85 us  [permute(): return lax.ppermute(value, axes, pairs)]
    unnamed x13 -> x17, local copies, waits for them, and re-layouts: 1.79 us -> 3.36 us
    pallas_call x1 -> x2, Pallas kernels: 28.5 us -> 28.6 us  [the longest x1 28.6 us: per_device(): pl.pallas_call(lambda *refs: step_kernel(*refs, rows=rows, scale_den=scal...]
  transfers between devices with their start and end apart: 7 -> 6, of which waited for: 3 -> 5; matrix products, arithmetic and copies ran while one was open for 2% -> 2% of each run, Pallas kernels for 4% -> 4%
where the time goes in v6:
time: 142 us
  blocking collectives  74.4 us (52%)
  Pallas kernels  38.5 us (27%)
  starting transfers between devices  14.8 us (10%)
  waiting for transfers between devices  6.85 us (5%)
  local copies, waits for them, and re-layouts  3.36 us (2%)
  other arithmetic  2.2 us (2%)
  between operations  1.56 us (1%)
    all_to_all x2, blocking collectives, over_chips(): return lax.all_to_all(value, axes, 0, 0, axis_index_groups=groups)  74.4 us
    pallas_call x1, Pallas kernels, per_device(): pl.pallas_call(lambda *refs: step_kernel(*refs, rows=rows, scale_den=scal...  28.6 us
    ppermute x6, starting transfers between devices, permute(): return lax.ppermute(value, axes, pairs)  14.8 us
    ppermute x6, waiting for transfers between devices, permute(): return lax.ppermute(value, axes, pairs)  6.85 us
    pallas_call x2, Pallas kernels, unpack(): pl.pallas_call(lambda *refs: unpack_kernel(*refs, own_half=own_half), in_...  4.42 us
    pallas_call x1, Pallas kernels, per_device(): pl.pallas_call(lambda *refs: prepare_kernel(*refs, rows=rows, halo=halo,...  3.39 us
    unnamed x17, local copies, waits for them, and re-layouts  3.36 us
  transfers between devices with their start and end apart: 6, of which 5 were waited for; matrix products, arithmetic and copies ran while one was open for 2% of the time, Pallas kernels for 4%

profile of v6, /device:TPU:1, one launch (start us, length us, event | category | flops | bytes accessed | tf_op | source)
XLA Modules:
  0.0 141.8 jit_solution(6517764791837229158)
XLA Ops:
  0.6 1.6 %pack.1.refs_0_.refs_1_ = bf16[144,512]{1,0:T(8,128)(2,1)} custom-call(bf16[128,512]{1,0:T(8,128)(2,1)} %refs_0_.3, s32[16,128]{1,0:T(8,128)} %refs_1_.2, f32[16,128]{1,0:T(8,128)} %refs_2_.3), custom_call_target="tpu_custom_call" | custom-call | tf_op jit(solution)/shard_map/pack/pallas_call | solution.py:856
  2.2 1.4 %collective-permute-start = (bf16[144,512]{1,0:T(8,128)(2,1)}, bf16[144,512]{1,0:T(8,128)(2,1)S(1)}, u32[]{:S(2)}, u32[]{:S(2)}) collective-permute-start(bf16[144,512]{1,0:T(8,128)(2,1)} %pack.1.refs_0_.refs_1_), channel_id=1, source_target_pairs={{0,1},{1,0},{2,3},{3,2},{4,5},{5,4},{6,7},{7,6},{8,9},{9,8},{10,11... | collective-permute-start | bytes 442376 | tf_op jit(solution)/shard_map/ppermute | solution.py:851
  3.7 1.2 collective-permute-done.refs_1_.refs_2_
  4.9 0.0 copy-start.1
  4.9 0.9 copy-done.1
  5.8 0.0 copy-start.5
  5.8 0.7 copy-done.5
  6.4 0.0 copy-start.3
  6.5 0.0 copy-start
  6.5 2.9 %collective-permute-start.1 = (bf16[224,512]{1,0:T(8,128)(2,1)S(1)}, bf16[224,512]{1,0:T(8,128)(2,1)S(1)}, u32[]{:S(2)}, u32[]{:S(2)}) collective-permute-start(bf16[224,512]{1,0:T(8,128)(2,1)S(1)} %outward.1.refs_4_), channel_id=1, source_target_pairs={{0,63},{1,66},{2,1},{3,68},{4,3},{5,70},{6,5},{7,72},{8,7},{9,74},... | collective-permute-start | bytes 688136 | tf_op jit(solution)/shard_map/ppermute | solution.py:851
  9.4 0.0 copy-done
  9.4 3.4 %prepare.1 = (bf16[512,512]{1,0:T(8,128)(2,1)}, bf16[512,512]{1,0:T(8,128)(2,1)}, bf16[512,512]{1,0:T(8,128)(2,1)}, f32[256,512]{1,0:T(8,128)}) custom-call(bf16[1024,512]{1,0:T(8,128)(2,1)} %refs_0_.4, s32[3,1024]{1,0:T(4,128)} %refs_1_.3, f32[3,1024]{1,0:T(4,128)} %refs_2_.5, bf16[512,512]{1,0:T(8,128)(2,1)} %refs_3_.1, bf16[224,512]{1,0:T(8,128)(2,1)} %copy-done), custom_call_target="tpu_custom_call" | custom-call | flops 268435456 | bytes 3145728 | tf_op jit(solution)/shard_map/prepare/pallas_call | solution.py:874
  12.8 0.0 collective-permute-done.1.refs_3_
  12.8 0.0 copy-start.6
  12.8 6.4 %collective-permute-start.2 = (bf16[224,512]{1,0:T(8,128)(2,1)S(1)}, bf16[224,512]{1,0:T(8,128)(2,1)S(1)}, u32[]{:S(2)}, u32[]{:S(2)}) collective-permute-start(bf16[224,512]{1,0:T(8,128)(2,1)S(1)} %collective-permute-done.1.refs_3_), channel_id=1, source_target_pairs={{0,1},{1,0},{2,3},{3,2},{4,5},{5,4},{6,7},{7,6},{8,9},{9,8},{10,11... | collective-permute-start | bytes 688136 | tf_op jit(solution)/shard_map/ppermute | solution.py:851
  19.8 0.5 collective-permute-done.2.refs_4_
  20.3 0.0 copy-start.7
  20.3 0.0 copy-done.3
  20.3 0.0 copy-done.6
  20.3 0.7 copy-done.7
  20.9 28.6 %step.1 = (f32[84,512]{1,0:T(8,128)}, f32[84,512]{1,0:T(8,128)}, bf16[64,136,128]{2,1,0:T(8,128)(2,1)}, bf16[64,136,128]{2,1,0:T(8,128)(2,1)}, f32[2,32,128]{2,1,0:T(8,128)}) custom-call(s32[1]{0:T(128)S(6)} %copy.48.refs_0_, bf16[144,512]{1,0:T(8,128)(2,1)} %pack.1.refs_0_.refs_1_, bf16[144,512]{1,0:T(8,128)(2,1)} %copy-done.3, bf16[224,512]{1,0:T(8,128)(2,1)} %copy-done.6, ...), custom_call_target="tpu_custom_call" | custom-call | flops 10000000000 | bytes 12582912 | tf_op jit(solution)/shard_map/step/pallas_call | solution.py:925
  49.6 0.5 collective-permute-start.3
  50.0 1.0 collective-permute-start.4
  51.0 3.2 %collective-permute-done.3 = bf16[64,136,128]{2,1,0:T(8,128)(2,1)S(1)} collective-permute-done((bf16[64,136,128]{2,1,0:T(8,128)(2,1)}, bf16[64,136,128]{2,1,0:T(8,128)(2,1)S(1)}, u32[]{:S(2)}, u32[]{:S(2)}) %collective-permute-start.3) | collective-permute-done | bytes 2228256 | tf_op jit(solution)/shard_map/ppermute | solution.py:851
  54.2 2.2 %add_convert_fusion = bf16[64,136,128]{2,1,0:T(8,128)(2,1)S(1)} fusion(bf16[64,136,128]{2,1,0:T(8,128)(2,1)S(1)} %collective-permute-done.3, bf16[64,136,128]{2,1,0:T(8,128)(2,1)} %get-tuple-element.49), kind=kLoop, calls=%fused_computation | loop fusion | flops 4456448 | bytes 6684672 | tf_op jit(solution)/shard_map/convert_element_type | solution.py:1016
  56.4 0.0 copy-start.2
  56.4 1.3 collective-permute-done.4.pred_arrived_hbm
  57.7 37.4 %all_to_all.10.parts = bf16[64,136,128]{2,1,0:T(8,128)(2,1)S(1)} all-to-all(bf16[64,136,128]{2,1,0:T(8,128)(2,1)S(1)} %add_convert_fusion), channel_id=1, replica_groups={{0,2,4,6,8,10,12,14,16,18,20,22,24,26,28,30,32,34,36,38,40,42,44,46,48,..., dimensions={0} | all-to-all | bytes 4456448 | tf_op jit(solution)/shard_map/all_to_all | solution.py:1013
  95.2 0.0 copy-done.2
  95.2 0.5 sum.1
  95.7 0.0 copy-start.4
  95.7 37.0 %all_to_all.11.refs_0_ = bf16[64,136,128]{2,1,0:T(8,128)(2,1)S(1)} all-to-all(bf16[64,136,128]{2,1,0:T(8,128)(2,1)S(1)} %get-tuple-element.56), channel_id=1, replica_groups={{0,2,4,6,8,10,12,14,16,18,20,22,24,26,28,30,32,34,36,38,40,42,44,46,48,..., dimensions={0} | all-to-all | bytes 4456448 | tf_op jit(solution)/shard_map/all_to_all | solution.py:1013
  132.7 2.7 %collective-permute-start.5 = (bf16[64,136,128]{2,1,0:T(8,128)(2,1)S(1)}, bf16[64,136,128]{2,1,0:T(8,128)(2,1)S(1)}, u32[]{:S(2)}, u32[]{:S(2)}) collective-permute-start(bf16[64,136,128]{2,1,0:T(8,128)(2,1)S(1)} %all_to_all.11.refs_0_), channel_id=1, source_target_pairs={{0,1},{1,0},{2,3},{3,2},{4,5},{5,4},{6,7},{7,6},{8,9},{9,8},{10,11... | collective-permute-start | bytes 6684680 | tf_op jit(solution)/shard_map/ppermute | solution.py:851
  135.4 1.1 copy.38
  136.5 0.0 copy-done.4
  136.5 2.2 %unpack_mine.1 = (f32[32,512]{1,0:T(8,128)}, f32[32,512]{1,0:T(8,128)}, f32[512,1536]{1,0:T(8,128)}, f32[512,512]{1,0:T(8,128)}, f32[512,512]{1,0:T(8,128)}, /*i...) custom-call(bf16[64,136,128]{2,1,0:T(8,128)(2,1)S(1)} %all_to_all.11.refs_0_, ...), custom_call_target="tpu_custom_call" | custom-call | bytes 7340032 | tf_op jit(solution)/shard_map/unpack_mine/pallas_call | solution.py:1050
  138.7 0.7 collective-permute-done.5.refs_0_
  139.4 2.2 %unpack_theirs.1 = (f32[32,512]{1,0:T(8,128)}, f32[32,512]{1,0:T(8,128)}, f32[512,1536]{1,0:T(8,128)}, f32[512,512]{1,0:T(8,128)}, f32[512,512]{1,0:T(8,128)}, /...) custom-call(bf16[64,136,128]{2,1,0:T(8,128)(2,1)S(1)} %collective-pe, ...), custom_call_target="tpu_custom_call", output_to_operand_aliasing={{0}: (2, {}), {1}: (3, {}), {2}: (4, {}), {3}: (5, {}), {4}... | custom-call | bytes 7340032 | tf_op jit(solution)/shard_map/unpack_theirs/pallas_call | solution.py:1050
  (1 shorter events, 0.0 us)
Async XLA Ops:
  2.2 2.6 %collective-permute-start = (bf16[144,512]{1,0:T(8,128)(2,1)}, bf16[144,512]{1,0:T(8,128)(2,1)S(1)}, u32[]{:S(2)}, u32[]{:S(2)}) collective-permute-start(bf16[144,512]{1,0:T(8,128)(2,1)} %pack.1.refs_0_.refs_1_), channel_id=1, source_target_pairs={{0,1},{1,0},{2,3},{3,2},{4,5},{5,4},{6,7},{7,6},{8,9},{9,8},{10,11... | collective-permute-start | bytes 442376 | tf_op jit(solution)/shard_map/ppermute | solution.py:851
  4.9 0.9 copy-start.1
  5.8 0.7 copy-start.5
  6.4 13.8 %copy-start.3 = (bf16[144,512]{1,0:T(8,128)(2,1)}, bf16[144,512]{1,0:T(8,128)(2,1)S(1)}, u32[]{:S(2)}) copy-start(bf16[144,512]{1,0:T(8,128)(2,1)S(1)} %collective-permute-done.refs_1_.refs_2_) | copy-start | bytes 442372
  6.5 2.9 %copy-start = (bf16[224,512]{1,0:T(8,128)(2,1)}, bf16[224,512]{1,0:T(8,128)(2,1)S(1)}, u32[]{:S(2)}) copy-start(bf16[224,512]{1,0:T(8,128)(2,1)S(1)} %outward.1.refs_4_) | copy-start | bytes 688132
  6.5 6.3 %collective-permute-start.1 = (bf16[224,512]{1,0:T(8,128)(2,1)S(1)}, bf16[224,512]{1,0:T(8,128)(2,1)S(1)}, u32[]{:S(2)}, u32[]{:S(2)}) collective-permute-start(bf16[224,512]{1,0:T(8,128)(2,1)S(1)} %outward.1.refs_4_), channel_id=1, source_target_pairs={{0,63},{1,66},{2,1},{3,68},{4,3},{5,70},{6,5},{7,72},{8,7},{9,74},... | collective-permute-start | bytes 688136 | tf_op jit(solution)/shard_map/ppermute | solution.py:851
  12.8 7.5 %copy-start.6 = (bf16[224,512]{1,0:T(8,128)(2,1)}, bf16[224,512]{1,0:T(8,128)(2,1)S(1)}, u32[]{:S(2)}) copy-start(bf16[224,512]{1,0:T(8,128)(2,1)S(1)} %collective-permute-done.1.refs_3_) | copy-start | bytes 688132
  12.8 7.5 %collective-permute-start.2 = (bf16[224,512]{1,0:T(8,128)(2,1)S(1)}, bf16[224,512]{1,0:T(8,128)(2,1)S(1)}, u32[]{:S(2)}, u32[]{:S(2)}) collective-permute-start(bf16[224,512]{1,0:T(8,128)(2,1)S(1)} %collective-permute-done.1.refs_3_), channel_id=1, source_target_pairs={{0,1},{1,0},{2,3},{3,2},{4,5},{5,4},{6,7},{7,6},{8,9},{9,8},{10,11... | collective-permute-start | bytes 688136 | tf_op jit(solution)/shard_map/ppermute | solution.py:851
  20.3 0.7 copy-start.7
  49.6 4.6 %collective-permute-start.3 = (bf16[64,136,128]{2,1,0:T(8,128)(2,1)}, bf16[64,136,128]{2,1,0:T(8,128)(2,1)S(1)}, u32[]{:S(2)}, u32[]{:S(2)}) collective-permute-start(bf16[64,136,128]{2,1,0:T(8,128)(2,1)} %get-tuple-element.50), channel_id=1, source_target_pairs={{0,1},{1,0},{2,3},{3,2},{4,5},{5,4},{6,7},{7,6},{8,9},{9,8},{10,11... | collective-permute-start | bytes 6684680 | tf_op jit(solution)/shard_map/ppermute | solution.py:851
  50.0 7.7 %collective-permute-start.4 = (f32[84,512]{1,0:T(8,128)}, f32[84,512]{1,0:T(8,128)S(1)}, u32[]{:S(2)}, u32[]{:S(2)}) collective-permute-start(f32[84,512]{1,0:T(8,128)} %get-tuple-element.51), channel_id=1, source_target_pairs={{0,64},{1,65},{2,66},{3,67},{4,68},{5,69},{6,70},{7,71},{8,72},{9,... | collective-permute-start | bytes 516104 | tf_op jit(solution)/shard_map/ppermute | solution.py:851
  56.4 38.8 %copy-start.2 = (f32[84,512]{1,0:T(8,128)S(1)}, f32[84,512]{1,0:T(8,128)}, u32[]{:S(2)}) copy-start(f32[84,512]{1,0:T(8,128)} %get-tuple-element.53.pred_own_hbm) | copy-start | bytes 516100
  95.7 40.8 %copy-start.4 = (f32[2,32,128]{2,1,0:T(8,128)S(1)}, f32[2,32,128]{2,1,0:T(8,128)}, u32[]{:S(2)}) copy-start(f32[2,32,128]{2,1,0:T(8,128)} %get-tuple-element.57.refs_1_) | copy-start | bytes 98308
  132.7 6.7 %collective-permute-start.5 = (bf16[64,136,128]{2,1,0:T(8,128)(2,1)S(1)}, bf16[64,136,128]{2,1,0:T(8,128)(2,1)S(1)}, u32[]{:S(2)}, u32[]{:S(2)}) collective-permute-start(bf16[64,136,128]{2,1,0:T(8,128)(2,1)S(1)} %all_to_all.11.refs_0_), channel_id=1, source_target_pairs={{0,1},{1,0},{2,3},{3,2},{4,5},{5,4},{6,7},{7,6},{8,9},{9,8},{10,11... | collective-permute-start | bytes 6684680 | tf_op jit(solution)/shard_map/ppermute | solution.py:851
